TPU v7x, 32 devices: a whole 2x2x4 slice. The times are simulated.
32 devices in a mesh: tm: 16 (over z, y, x), src: 2 (over core).
Axes of the slice: x: 2, y: 2, z: 4, core: 2. Of those that a mesh axis runs over, the one named last changes fastest.
Arguments:
- feats: bfloat16 [4, 16384, 128], P(None, ('tm', 'src')), may hold values from -6 to 6
- encoded: bfloat16 [4, 16384, 512], P(None, ('tm', 'src')), may hold values from 0.19921875 to 3
- seg_lengths: int32 [4, 8], replicated, may hold values from 256 to 7168, as said below
- owners: int32 [340, 1], replicated, may hold values from 0 to 31; in each aligned block of 340 rows (0 to 339, 340 to 679, ...) at most 11 rows name the same one
- master: float32 [352, 1024], P(('tm', 'src')), may hold values from -0.375 to 0.375
- moment_one: float32 [352, 1024], P(('tm', 'src')), may hold values from -80 to 80
- moment_two: float32 [352, 1024], P(('tm', 'src')), may hold values from 8.192 to 131.072
- out_cot: bfloat16 [4, 16384, 128], P(None, ('tm', 'src')), may hold values from -6 to 6
- wave_cot: bfloat16 [4, 2, 16384, 16], P(None, 'src', 'tm'), may hold values from -6 to 6
Outputs:
- block_out: bfloat16 [4, 16384, 128], P(None, ('tm', 'src'))
- feats_grad: bfloat16 [4, 16384, 128], P(None, ('tm', 'src'))
- waves: bfloat16 [4, 2, 16384, 16], P(None, 'src', 'tm')
- new_master: float32 [352, 1024], P(('tm', 'src'))
- new_one: float32 [352, 1024], P(('tm', 'src'))
- new_two: float32 [352, 1024], P(('tm', 'src'))
Inputs may be any that keep to these rules, and one draw needn't show every extreme that they name: `seg_lengths`: each row sums to 16384. With u = 256, each row holds the lengths u, u, 2u, 3u, 5u, 8u, 16u and 16384 - 36u, in an order drawn from the seed. `owners`: every device owns one or more groups and none more than 11; some device owns exactly 11.
All inputs are finite; a program needn't handle non-finite values.
Results may differ from a plain program's by a relative error of at most 0.0065.
The roundings to bfloat16 on the way count: a program that leaves them out, or rounds other values in their place, can miss the bound.
Values may be sent and summed in bfloat16 or wider, within the bound.
No kernel may reach another device: no remote copies, remote signals or barrier semaphores. Data moves between devices by JAX's collectives and lax.ppermute only.
A program may use at most 128 MiB of HBM per device.

v0:
```python
import jax
import jax.numpy as jnp
from jax import lax
from jax.sharding import PartitionSpec as P

N = 512
L = 16
B = 128
SC = 128
HIDDEN_WIDTH = 512
C = 2
CONV_DILATION = 128
ROW = 1024
SEGS = 8
MICRO = 4
STEP = 10
NCH = 340


norm_eps = 1e-05
adam_eps = 1e-08
beta_one = 0.9
beta_two = 0.999
learn_rate = 0.2
weight_decay = 0.01


def with_halo(value, sides, width):
    for axis, dim in sides:
        size, length = (lax.axis_size(axis), value.shape[dim])
        up = [(i, (i + 1) % size) for i in range(size - 1)]
        down = [(j, i) for i, j in up]
        last = lax.slice_in_dim(value, length - width, length, axis=dim)
        leading = lax.slice_in_dim(value, 0, width, axis=dim)
        before = lax.ppermute(last, axis, up)
        after = lax.ppermute(leading, axis, down)
        value = jnp.concatenate([before, value, after], axis=dim)
    return value


def product(left_side, right_side):
    return jnp.dot(left_side, right_side, preferred_element_type=jnp.float32)


def contract_rows(left_side, right_side):
    return lax.dot_general(
        left_side, right_side, (((0,), (0,)), ((), ())), preferred_element_type=jnp.float32
    )


def contract_cols(left_side, right_side):
    return lax.dot_general(
        left_side, right_side, (((1,), (1,)), ((), ())), preferred_element_type=jnp.float32
    )


def unpack(flat_params):
    shapes = [
        (B, HIDDEN_WIDTH),
        (HIDDEN_WIDTH, B),
        (HIDDEN_WIDTH, SC),
        (C, SC, N),
        (C, N, L),
        (4, HIDDEN_WIDTH),
        (4, HIDDEN_WIDTH),
    ]
    offset = 0
    pieces = []
    for piece_shape in shapes:
        piece_size = 1
        for extent in piece_shape:
            piece_size = piece_size * extent
        pieces.append(flat_params[offset : offset + piece_size].reshape(piece_shape))
        offset = offset + piece_size
    return pieces


def fetch_weights(master, slot_place):
    gathered = lax.all_gather(master.astype(jnp.bfloat16), ("tm", "src"), axis=0, tiled=True)
    return unpack(gathered[slot_place].reshape(-1))


def send_grads(flat_grads, slot_place, slot_total):
    spread = jnp.zeros((slot_total, ROW), jnp.float32).at[slot_place].set(flat_grads)
    return lax.psum_scatter(spread, ("tm", "src"), scatter_dimension=0, tiled=True)


def per_frame(member, per_segment):
    return jnp.sum(member * per_segment[None, :], axis=1)


def norm_forward(values, member, counts):
    first_sum = jnp.sum(member * jnp.sum(values, axis=1)[:, None], axis=0)
    second = jnp.sum(member * jnp.sum(values * values, axis=1)[:, None], axis=0)
    first_sum, second = lax.psum((first_sum, second), ("tm", "src"))
    center = first_sum / counts
    factor = lax.rsqrt(second / counts - center * center + norm_eps)
    factor_rows = per_frame(member, factor)
    return ((values - per_frame(member, center)[:, None]) * factor_rows[:, None], factor_rows)


def norm_backward(grad_hat, normalized_rows, factor_rows, member, counts):
    first_sum = jnp.sum(member * jnp.sum(grad_hat, axis=1)[:, None], axis=0)
    second = jnp.sum(member * jnp.sum(grad_hat * normalized_rows, axis=1)[:, None], axis=0)
    first_sum, second = lax.psum((first_sum, second), ("tm", "src"))
    mean_one = per_frame(member, first_sum / counts)
    mean_two = per_frame(member, second / counts)
    return factor_rows[:, None] * (
        grad_hat - mean_one[:, None] - normalized_rows * mean_two[:, None]
    )


def silu_slope(pre_act, sig_act):
    return sig_act * (1.0 + pre_act * (1.0 - sig_act))


def head_pass(gated_act, encoded, wave_cot, w_mask, w_dec):
    gated_all, encoded_all = (
        lax.all_gather(gated_act, "src", axis=0, tiled=True),
        lax.all_gather(encoded, "src", axis=0, tiled=True),
    )
    source = lax.axis_index("src")
    mask_w = lax.dynamic_index_in_dim(w_mask, source, 0, keepdims=False)
    dec_w = lax.dynamic_index_in_dim(w_dec, source, 0, keepdims=False)
    sig_mask = jax.nn.sigmoid(product(gated_all, mask_w))
    encoded_f = encoded_all.astype(jnp.float32)
    masked = (sig_mask * encoded_f).astype(jnp.bfloat16)
    wave_vals = product(masked, dec_w).astype(jnp.bfloat16)[None]
    wave_grad = wave_cot[0]
    grad_masked = contract_cols(wave_grad, dec_w)
    grad_logits = (grad_masked * encoded_f * sig_mask * (1.0 - sig_mask)).astype(jnp.bfloat16)
    pick = (jnp.arange(C) == source).astype(jnp.float32)[:, None, None]
    grad_dec = pick * contract_rows(masked, wave_grad)[None]
    grad_mask = pick * contract_rows(gated_all, grad_logits)[None]
    grad_gated = lax.psum_scatter(
        contract_cols(grad_logits, mask_w).astype(jnp.bfloat16),
        "src",
        scatter_dimension=0,
        tiled=True,
    ).astype(jnp.float32)
    return (wave_vals, grad_mask, grad_dec, grad_gated)


def micro_pass(weights, feats, encoded, lengths, out_cot, wave_cot):
    w_in, w_res, w_skip, w_mask, w_dec, norm_rows, depth_rows = weights
    norm_f = norm_rows.astype(jnp.float32)
    filter_tap_rows = depth_rows.astype(jnp.float32)
    frame_rows = feats.shape[0]
    leading_frame = lax.axis_index(("tm", "src")) * frame_rows
    bounds = jnp.cumsum(lengths)
    position_list = (
        leading_frame - CONV_DILATION + jnp.arange(frame_rows + 2 * CONV_DILATION, dtype=jnp.int32)
    )
    segment_index_widened = jnp.sum(
        (position_list[:, None] >= bounds[None, :]).astype(jnp.int32), axis=1
    )
    segment_index_here = segment_index_widened[CONV_DILATION : CONV_DILATION + frame_rows]
    member = (segment_index_here[:, None] == jnp.arange(SEGS)[None, :]).astype(jnp.float32)
    counts = lengths.astype(jnp.float32) * HIDDEN_WIDTH
    before_valid = (segment_index_widened[:frame_rows] == segment_index_here).astype(jnp.float32)[
        :, None
    ]
    after_valid = (segment_index_widened[2 * CONV_DILATION :] == segment_index_here).astype(
        jnp.float32
    )[:, None]
    pre_in = product(feats, w_in)
    sig_in = jax.nn.sigmoid(pre_in)
    hat_one, factor_one = norm_forward(pre_in * sig_in, member, counts)
    normalized_single = (hat_one * (1.0 + norm_f[0]) + norm_f[1]).astype(jnp.bfloat16)
    widened_single = with_halo(normalized_single, ((("tm", "src"), 0),), CONV_DILATION).astype(
        jnp.float32
    )
    left_in = widened_single[:frame_rows] * before_valid
    right_input = widened_single[2 * CONV_DILATION :] * after_valid
    middle = normalized_single.astype(jnp.float32)
    pre_depth = (
        filter_tap_rows[0] * left_in
        + filter_tap_rows[1] * middle
        + filter_tap_rows[2] * right_input
        + filter_tap_rows[3]
    )
    sig_depth = jax.nn.sigmoid(pre_depth)
    hat_two, factor_two = norm_forward(pre_depth * sig_depth, member, counts)
    normed_two = (hat_two * (1.0 + norm_f[2]) + norm_f[3]).astype(jnp.bfloat16)
    block_out = (feats.astype(jnp.float32) + product(normed_two, w_res)).astype(jnp.bfloat16)
    skip_pre = product(normed_two, w_skip)
    sig_skip = jax.nn.sigmoid(skip_pre)
    gated_act = (skip_pre * sig_skip).astype(jnp.bfloat16)
    wave_vals, grad_mask, grad_dec, grad_gated = head_pass(
        gated_act, encoded, wave_cot, w_mask, w_dec
    )
    grad_skip = (grad_gated * silu_slope(skip_pre, sig_skip)).astype(jnp.bfloat16)
    grad_res = contract_rows(normed_two, out_cot)
    grad_skipw = contract_rows(normed_two, grad_skip)
    grad_two = contract_cols(out_cot, w_res) + contract_cols(grad_skip, w_skip)
    gain_two = jnp.sum(grad_two * hat_two, axis=0)
    shift_two = jnp.sum(grad_two, axis=0)
    grad_act = norm_backward(grad_two * (1.0 + norm_f[2]), hat_two, factor_two, member, counts)
    depthwise_gradient = (grad_act * silu_slope(pre_depth, sig_depth)).astype(jnp.bfloat16)
    widened_gradient = with_halo(depthwise_gradient, ((("tm", "src"), 0),), CONV_DILATION).astype(
        jnp.float32
    )
    depth_f = depthwise_gradient.astype(jnp.float32)
    tap_grads = jnp.stack(
        [
            jnp.sum(depth_f * left_in, axis=0),
            jnp.sum(depth_f * middle, axis=0),
            jnp.sum(depth_f * right_input, axis=0),
            jnp.sum(depth_f, axis=0),
        ]
    )
    grad_one = (
        filter_tap_rows[1] * depth_f
        + filter_tap_rows[0] * widened_gradient[2 * CONV_DILATION :] * after_valid
        + filter_tap_rows[2] * widened_gradient[:frame_rows] * before_valid
    )
    gain_one = jnp.sum(grad_one * hat_one, axis=0)
    shift_one = jnp.sum(grad_one, axis=0)
    grad_hidden = norm_backward(grad_one * (1.0 + norm_f[0]), hat_one, factor_one, member, counts)
    grad_pre = (grad_hidden * silu_slope(pre_in, sig_in)).astype(jnp.bfloat16)
    grad_win = contract_rows(feats, grad_pre)
    feats_grad = (out_cot.astype(jnp.float32) + contract_cols(grad_pre, w_in)).astype(jnp.bfloat16)
    norm_grads = jnp.stack([gain_one, shift_one, gain_two, shift_two])
    flat_grads = jnp.concatenate(
        [
            grad_win.reshape(-1),
            grad_res.reshape(-1),
            grad_skipw.reshape(-1),
            grad_mask.reshape(-1),
            grad_dec.reshape(-1),
            norm_grads.reshape(-1),
            tap_grads.reshape(-1),
        ]
    ).reshape(NCH, ROW)
    return (block_out, feats_grad, wave_vals, flat_grads)


def local(feats, encoded, seg_lengths, owners, master, moment_one, moment_two, out_cot, wave_cot):
    owner_ids = owners[:, 0]
    slots_here = master.shape[0]
    slot_total = lax.axis_size(("tm", "src")) * slots_here
    group_order = jnp.arange(NCH, dtype=jnp.int32)
    earlier = (owner_ids[:, None] == owner_ids[None, :]) & (
        group_order[None, :] < group_order[:, None]
    )
    slot_rank = jnp.sum(earlier.astype(jnp.int32), axis=1)
    slot_place = owner_ids * slots_here + slot_rank
    block_list = []
    grad_list = []
    wave_list = []
    owned_grads = jnp.zeros((slots_here, ROW), jnp.float32)
    for micro_step in range(MICRO):
        weights = fetch_weights(master, slot_place)
        results = micro_pass(
            weights,
            feats[micro_step],
            encoded[micro_step],
            seg_lengths[micro_step],
            out_cot[micro_step],
            wave_cot[micro_step],
        )
        block_list.append(results[0])
        grad_list.append(results[1])
        wave_list.append(results[2])
        owned_grads = owned_grads + send_grads(results[3], slot_place, slot_total)
    device_here = lax.axis_index(("tm", "src"))
    owned_count = jnp.sum((owner_ids == device_here).astype(jnp.int32))
    used_rows = (jnp.arange(slots_here) < owned_count).astype(jnp.float32)[:, None]
    new_one = beta_one * moment_one + (1.0 - beta_one) * owned_grads
    new_two = beta_two * moment_two + (1.0 - beta_two) * owned_grads * owned_grads
    unbias_one = new_one / (1.0 - beta_one**STEP)
    unbias_two = new_two / (1.0 - beta_two**STEP)
    new_master = master - learn_rate * (
        unbias_one / (jnp.sqrt(unbias_two) + adam_eps) + weight_decay * master
    )
    return (
        jnp.stack(block_list),
        jnp.stack(grad_list),
        jnp.stack(wave_list),
        new_master * used_rows,
        new_one * used_rows,
        new_two * used_rows,
    )


def solution(mesh):
    return jax.shard_map(
        local,
        mesh=mesh,
        in_specs=(
            P(None, ("tm", "src"), None),
            P(None, ("tm", "src"), None),
            P(),
            P(),
            P(("tm", "src"), None),
            P(("tm", "src"), None),
            P(("tm", "src"), None),
            P(None, ("tm", "src"), None),
            P(None, "src", "tm", None),
        ),
        out_specs=(
            P(None, ("tm", "src"), None),
            P(None, ("tm", "src"), None),
            P(None, "src", "tm", None),
            P(("tm", "src"), None),
            P(("tm", "src"), None),
            P(("tm", "src"), None),
        ),
        check_vma=False,
    )
```

profile of v0, /device:TPU:1, one launch (start us, length us, event | category | flops | bytes accessed | tf_op | source)
XLA Modules:
  0.0 628.0 jit_solution(7443521453315402233)
XLA Ops:
  14.0 46.1 %all-gather.4 = bf16[32,11,1024]{2,1,0:T(8,128)(2,1)S(1)} all-gather(bf16[1,11,1024]{2,1,0:T(8,128)(2,1)S(1)} %convert_bitcast_fusion), channel_id=1, replica_groups=mesh['tm'=16,'src'=2] {'tm','src'}, dimensions={0}, use_global_device_ids=true | all-gather | bytes 743424 | tf_op jit(solution)/shard_map/all_gather | solution.py:79
  70.0 35.6 %all-reduce.5 = (f32[8]{0:T(128)S(1)}, f32[8]{0:T(128)S(1)}, f32[8]{0:T(128)S(1)}, f32[8]{0:T(128)S(1)}, f32[8]{0:T(128)S(1)}, /*index=5*/f32[8]{0:T(128)S(1)}, f32[8]{0:T(128)S(1)}, f32[8]{0:T(128)S(1)}) all-reduce(f32[8]{0:T(128)S(1)} %get-tuple-element.137, ...), channel_id=1, replica_groups=mesh['tm'=16,'src'=2] {'tm','src'}, use_global_device_ids=true, to_apply=%region_59.60 | all-reduce | flops 64 | bytes 512 | tf_op jit(solution)/shard_map/psum | solution.py:95
  106.0 3.1 add_convert_fusion.7
  110.0 5.4 collective-permute-start
  117.4 3.6 collective-permute-start.2
  123.7 3.6 collective-permute-start.4
  142.9 3.6 collective-permute-start.6
  161.1 46.7 %all-reduce.4 = (f32[8]{0:T(128)}, f32[8]{0:T(128)}, f32[8]{0:T(128)}, f32[8]{0:T(128)}, f32[8]{0:T(128)}, /*index=5*/f32[8]{0:T(128)}, f32[8]{0:T(128)}, f32[8]{0:T(128)}) all-reduce(f32[8]{0:T(128)} %get-tuple-element.133, f32[8]{0:T(128)} %get-tuple-element.132, ...), channel_id=1, replica_groups=mesh['tm'=16,'src'=2] {'tm','src'}, use_global_device_ids=true, to_apply=%region_67.68 | all-reduce | flops 64 | bytes 512 | tf_op jit(solution)/shard_map/psum | solution.py:95
  211.1 2.7 add_convert_fusion.6
  219.6 3.0 all_gather.32
  250.1 3.4 fusion.15
  253.5 3.5 fusion.11
  299.9 2.8 convolution_add_fusion.2
  302.8 6.2 multiply_reduce_fusion.6
  309.7 38.5 %all-reduce.3 = (f32[8]{0:T(128)S(1)}, f32[8]{0:T(128)S(1)}, f32[8]{0:T(128)S(1)}, f32[8]{0:T(128)S(1)}, f32[8]{0:T(128)S(1)}, /*index=5*/f32[8]{0:T(128)S(1)}, f32[8]{0:T(128)S(1)}, f32[8]{0:T(128)S(1)}) all-reduce(f32[8]{0:T(128)S(1)} %get-tuple-element.104, ...), channel_id=1, replica_groups=mesh['tm'=16,'src'=2] {'tm','src'}, use_global_device_ids=true, to_apply=%region_127.128 | all-reduce | flops 64 | bytes 512 | tf_op jit(solution)/shard_map/psum | solution.py:105
  348.4 3.3 fusion.59
  359.5 5.3 collective-permute-start.10
  366.8 3.6 collective-permute-start.14
  375.0 3.9 collective-permute-start.12
  397.1 41.3 %all-reduce.2 = (f32[8]{0:T(128)S(1)}, f32[8]{0:T(128)S(1)}, f32[8]{0:T(128)S(1)}, f32[8]{0:T(128)S(1)}, f32[8]{0:T(128)S(1)}, /*index=5*/f32[8]{0:T(128)S(1)}, f32[8]{0:T(128)S(1)}, f32[8]{0:T(128)S(1)}) all-reduce(f32[8]{0:T(128)S(1)} %get-tuple-element.100, ...), channel_id=1, replica_groups=mesh['tm'=16,'src'=2] {'tm','src'}, use_global_device_ids=true, to_apply=%region_135.136 | all-reduce | flops 64 | bytes 512 | tf_op jit(solution)/shard_map/psum | solution.py:105
  438.8 4.0 multiply_convert_fusion.6
  464.7 2.8 scatter_custom_fusion.1
  467.5 2.9 scatter_custom_fusion.2
  481.6 3.9 scatter_custom_fusion.3
  496.6 3.6 scatter_custom_fusion
  500.3 3.5 add_add_fusion
  503.8 79.2 %fusion = f32[16,1024]{1,0:T(8,128)S(1)} fusion(f32[352,1024]{1,0:T(8,128)} %add_add_fusion), kind=kCustom, calls=%all-reduce-scatter | all-reduce-scatter fusion | flops 524289 | bytes 1507328
  587.1 7.5 %collective-permute-start.21 = (f32[16,1024]{1,0:T(8,128)S(1)}, f32[16,1024]{1,0:T(8,128)S(1)}, u32[]{:S(2)}, u32[]{:S(2)}) collective-permute-start(f32[16,1024]{1,0:T(8,128)S(1)} %fusion), channel_id=1, source_target_pairs={{0,6},{1,7},{2,8},{3,9},{4,10},{5,11},{6,12},{7,13},{8,14},{9,15},... | collective-permute-start | bytes 196616
  597.3 5.2 collective-permute-start.20
  602.5 4.5 collective-permute-start.19
  608.3 3.1 collective-permute-start.17
  611.5 5.8 collective-permute-start.16
  (676 shorter events, 219.0 us)
Async XLA Ops:
  7.2 230.7 %all-gather.16.cloned.1.call-start = ((), (), s32[]{:S(2)}) async-start(), calls=%async_computation.11 | async-start | bytes 1572864 | tf_op jit(solution)/shard_map/all_gather | solution.py:120
  10.8 234.2 %all-gather.14.cloned.1.call-start = ((), (), s32[]{:S(2)}) async-start(), calls=%async_computation.10 | async-start | bytes 1572864 | tf_op jit(solution)/shard_map/all_gather | solution.py:120
  11.9 238.1 %all-gather.12.cloned.1.call-start = ((), (), s32[]{:S(2)}) async-start(), calls=%async_computation.9 | async-start | bytes 1572864 | tf_op jit(solution)/shard_map/all_gather | solution.py:120
  13.0 240.5 %all-gather.10.cloned.1.call-start = ((), (), s32[]{:S(2)}) async-start(), calls=%async_computation.8 | async-start | bytes 1572864 | tf_op jit(solution)/shard_map/all_gather | solution.py:120
  110.0 37.8 %collective-permute-start = (bf16[128,512]{1,0:T(8,128)(2,1)}, bf16[128,512]{1,0:T(8,128)(2,1)}, u32[]{:S(2)}, u32[]{:S(2)}) collective-permute-start(bf16[128,512]{1,0:T(8,128)(2,1)} %get-tuple-element.218), channel_id=1, source_target_pairs={{0,1},{1,2},{2,3},{3,4},{4,5},{5,6},{6,7},{7,8},{8,9},{9,10},{10,1... | collective-permute-start | bytes 393224 | tf_op jit(solution)/shard_map/ppermute | solution.py:35
  115.4 34.5 %collective-permute-start.1 = (bf16[128,512]{1,0:T(8,128)(2,1)}, bf16[128,512]{1,0:T(8,128)(2,1)}, u32[]{:S(2)}, u32[]{:S(2)}) collective-permute-start(bf16[128,512]{1,0:T(8,128)(2,1)} %get-tuple-element.219), channel_id=1, source_target_pairs={{1,0},{2,1},{3,2},{4,3},{5,4},{6,5},{7,6},{8,7},{9,8},{10,9},{11,1... | collective-permute-start | bytes 393224 | tf_op jit(solution)/shard_map/ppermute | solution.py:36
  117.4 22.9 %collective-permute-start.2 = (bf16[128,512]{1,0:T(8,128)(2,1)S(1)}, bf16[128,512]{1,0:T(8,128)(2,1)S(1)}, u32[]{:S(2)}, u32[]{:S(2)}) collective-permute-start(bf16[128,512]{1,0:T(8,128)(2,1)S(1)} %get-tuple-element.220), channel_id=1, source_target_pairs={{0,1},{1,2},{2,3},{3,4},{4,5},{5,6},{6,7},{7,8},{8,9},{9,10},{10,1... | collective-permute-start | bytes 393224 | tf_op jit(solution)/shard_map/ppermute | solution.py:35
  121.0 21.2 %collective-permute-start.3 = (bf16[128,512]{1,0:T(8,128)(2,1)S(1)}, bf16[128,512]{1,0:T(8,128)(2,1)S(1)}, u32[]{:S(2)}, u32[]{:S(2)}) collective-permute-start(bf16[128,512]{1,0:T(8,128)(2,1)S(1)} %get-tuple-element.221), channel_id=1, source_target_pairs={{1,0},{2,1},{3,2},{4,3},{5,4},{6,5},{7,6},{8,7},{9,8},{10,9},{11,1... | collective-permute-start | bytes 393224 | tf_op jit(solution)/shard_map/ppermute | solution.py:36
  123.7 32.3 %collective-permute-start.4 = (bf16[128,512]{1,0:T(8,128)(2,1)}, bf16[128,512]{1,0:T(8,128)(2,1)}, u32[]{:S(2)}, u32[]{:S(2)}) collective-permute-start(bf16[128,512]{1,0:T(8,128)(2,1)} %get-tuple-element.222), channel_id=1, source_target_pairs={{0,1},{1,2},{2,3},{3,4},{4,5},{5,6},{6,7},{7,8},{8,9},{9,10},{10,1... | collective-permute-start | bytes 393224 | tf_op jit(solution)/shard_map/ppermute | solution.py:35
  128.4 166.2 %reduce-scatter.13.cloned.1.call-start = ((), (), s32[]{:S(2)}) async-start(), calls=%async_computation.7 | async-start | bytes 393216 | tf_op jit(solution)/shard_map/reduce_scatter | solution.py:135
  140.3 15.7 %collective-permute-start.5 = (bf16[128,512]{1,0:T(8,128)(2,1)}, bf16[128,512]{1,0:T(8,128)(2,1)S(1)}, u32[]{:S(2)}, u32[]{:S(2)}) collective-permute-start(bf16[128,512]{1,0:T(8,128)(2,1)} %get-tuple-element.223), channel_id=1, source_target_pairs={{1,0},{2,1},{3,2},{4,3},{5,4},{6,5},{7,6},{8,7},{9,8},{10,9},{11,1... | collective-permute-start | bytes 393224 | tf_op jit(solution)/shard_map/ppermute | solution.py:36
  142.9 10.9 %collective-permute-start.6 = (bf16[128,512]{1,0:T(8,128)(2,1)}, bf16[128,512]{1,0:T(8,128)(2,1)S(1)}, u32[]{:S(2)}, u32[]{:S(2)}) collective-permute-start(bf16[128,512]{1,0:T(8,128)(2,1)} %get-tuple-element.224), channel_id=1, source_target_pairs={{0,1},{1,2},{2,3},{3,4},{4,5},{5,6},{6,7},{7,8},{8,9},{9,10},{10,1... | collective-permute-start | bytes 393224 | tf_op jit(solution)/shard_map/ppermute | solution.py:35
  147.8 6.6 %collective-permute-start.7 = (bf16[128,512]{1,0:T(8,128)(2,1)S(1)}, bf16[128,512]{1,0:T(8,128)(2,1)S(1)}, u32[]{:S(2)}, u32[]{:S(2)}) collective-permute-start(bf16[128,512]{1,0:T(8,128)(2,1)S(1)} %copy-done.101), channel_id=1, source_target_pairs={{1,0},{2,1},{3,2},{4,3},{5,4},{6,5},{7,6},{8,7},{9,8},{10,9},{11,1... | collective-permute-start | bytes 393224 | tf_op jit(solution)/shard_map/ppermute | solution.py:36
  249.6 47.6 %reduce-scatter.11.cloned.1.call-start = ((), (), s32[]{:S(2)}) async-start(), calls=%async_computation.6 | async-start | bytes 393216 | tf_op jit(solution)/shard_map/reduce_scatter | solution.py:135
  262.0 37.9 %reduce-scatter.9.cloned.1.call-start = ((), (), s32[]{:S(2)}) async-start(), calls=%async_computation.5 | async-start | bytes 393216 | tf_op jit(solution)/shard_map/reduce_scatter | solution.py:135
  268.5 34.1 %reduce-scatter.7.cloned.1.call-start = ((), (), s32[]{:S(2)}) async-start(), calls=%async_computation.4 | async-start | bytes 393216 | tf_op jit(solution)/shard_map/reduce_scatter | solution.py:135
  359.5 33.8 %collective-permute-start.10 = (bf16[128,512]{1,0:T(8,128)(2,1)S(1)}, bf16[128,512]{1,0:T(8,128)(2,1)S(1)}, u32[]{:S(2)}, u32[]{:S(2)}) collective-permute-start(bf16[128,512]{1,0:T(8,128)(2,1)S(1)} %get-tuple-element.212), channel_id=1, source_target_pairs={{0,1},{1,2},{2,3},{3,4},{4,5},{5,6},{6,7},{7,8},{8,9},{9,10},{10,1... | collective-permute-start | bytes 393224 | tf_op jit(solution)/shard_map/ppermute | solution.py:35
  364.8 28.5 %collective-permute-start.11 = (bf16[128,512]{1,0:T(8,128)(2,1)S(1)}, bf16[128,512]{1,0:T(8,128)(2,1)S(1)}, u32[]{:S(2)}, u32[]{:S(2)}) collective-permute-start(bf16[128,512]{1,0:T(8,128)(2,1)S(1)} %get-tuple-element.213), channel_id=1, source_target_pairs={{1,0},{2,1},{3,2},{4,3},{5,4},{6,5},{7,6},{8,7},{9,8},{10,9},{11,1... | collective-permute-start | bytes 393224 | tf_op jit(solution)/shard_map/ppermute | solution.py:36
  366.8 22.2 %collective-permute-start.14 = (bf16[128,512]{1,0:T(8,128)(2,1)S(1)}, bf16[128,512]{1,0:T(8,128)(2,1)S(1)}, u32[]{:S(2)}, u32[]{:S(2)}) collective-permute-start(bf16[128,512]{1,0:T(8,128)(2,1)S(1)} %get-tuple-element.216), channel_id=1, source_target_pairs={{0,1},{1,2},{2,3},{3,4},{4,5},{5,6},{6,7},{7,8},{8,9},{9,10},{10,1... | collective-permute-start | bytes 393224 | tf_op jit(solution)/shard_map/ppermute | solution.py:35
  372.6 7.0 %collective-permute-start.9 = (bf16[128,512]{1,0:T(8,128)(2,1)S(1)}, bf16[128,512]{1,0:T(8,128)(2,1)S(1)}, u32[]{:S(2)}, u32[]{:S(2)}) collective-permute-start(bf16[128,512]{1,0:T(8,128)(2,1)S(1)} %get-tuple-element.211), channel_id=1, source_target_pairs={{1,0},{2,1},{3,2},{4,3},{5,4},{6,5},{7,6},{8,7},{9,8},{10,9},{11,1... | collective-permute-start | bytes 393224 | tf_op jit(solution)/shard_map/ppermute | solution.py:36
  375.0 9.2 %collective-permute-start.12 = (bf16[128,512]{1,0:T(8,128)(2,1)S(1)}, bf16[128,512]{1,0:T(8,128)(2,1)S(1)}, u32[]{:S(2)}, u32[]{:S(2)}) collective-permute-start(bf16[128,512]{1,0:T(8,128)(2,1)S(1)} %get-tuple-element.214), channel_id=1, source_target_pairs={{0,1},{1,2},{2,3},{3,4},{4,5},{5,6},{6,7},{7,8},{8,9},{9,10},{10,1... | collective-permute-start | bytes 393224 | tf_op jit(solution)/shard_map/ppermute | solution.py:35
  379.6 6.7 %collective-permute-start.13 = (bf16[128,512]{1,0:T(8,128)(2,1)S(1)}, bf16[128,512]{1,0:T(8,128)(2,1)S(1)}, u32[]{:S(2)}, u32[]{:S(2)}) collective-permute-start(bf16[128,512]{1,0:T(8,128)(2,1)S(1)} %get-tuple-element.215), channel_id=1, source_target_pairs={{1,0},{2,1},{3,2},{4,3},{5,4},{6,5},{7,6},{8,7},{9,8},{10,9},{11,1... | collective-permute-start | bytes 393224 | tf_op jit(solution)/shard_map/ppermute | solution.py:36
  384.2 6.4 %collective-permute-start.15 = (bf16[128,512]{1,0:T(8,128)(2,1)S(1)}, bf16[128,512]{1,0:T(8,128)(2,1)S(1)}, u32[]{:S(2)}, u32[]{:S(2)}) collective-permute-start(bf16[128,512]{1,0:T(8,128)(2,1)S(1)} %get-tuple-element.217), channel_id=1, source_target_pairs={{1,0},{2,1},{3,2},{4,3},{5,4},{6,5},{7,6},{8,7},{9,8},{10,9},{11,1... | collective-permute-start | bytes 393224 | tf_op jit(solution)/shard_map/ppermute | solution.py:36
  583.1 19.4 %collective-permute-start.24 = (f32[16,1024]{1,0:T(8,128)S(1)}, f32[16,1024]{1,0:T(8,128)S(1)}, u32[]{:S(2)}, u32[]{:S(2)}) collective-permute-start(f32[16,1024]{1,0:T(8,128)S(1)} %fusion), channel_id=1, source_target_pairs={{0,9},{1,10},{2,11},{3,12},{4,13},{5,14},{6,15},{7,16},{8,17},{9,1... | collective-permute-start | bytes 196616
  584.5 22.5 %collective-permute-start.23 = (f32[16,1024]{1,0:T(8,128)S(1)}, f32[16,1024]{1,0:T(8,128)S(1)}, u32[]{:S(2)}, u32[]{:S(2)}) collective-permute-start(f32[16,1024]{1,0:T(8,128)S(1)} %fusion), channel_id=1, source_target_pairs={{0,8},{1,9},{2,10},{3,11},{4,12},{5,13},{6,14},{7,15},{8,16},{9,17... | collective-permute-start | bytes 196616
  585.8 22.5 %collective-permute-start.22 = (f32[16,1024]{1,0:T(8,128)S(1)}, f32[16,1024]{1,0:T(8,128)S(1)}, u32[]{:S(2)}, u32[]{:S(2)}) collective-permute-start(f32[16,1024]{1,0:T(8,128)S(1)} %fusion), channel_id=1, source_target_pairs={{0,7},{1,8},{2,9},{3,10},{4,11},{5,12},{6,13},{7,14},{8,15},{9,16}... | collective-permute-start | bytes 196616
  587.1 24.3 %collective-permute-start.21 = (f32[16,1024]{1,0:T(8,128)S(1)}, f32[16,1024]{1,0:T(8,128)S(1)}, u32[]{:S(2)}, u32[]{:S(2)}) collective-permute-start(f32[16,1024]{1,0:T(8,128)S(1)} %fusion), channel_id=1, source_target_pairs={{0,6},{1,7},{2,8},{3,9},{4,10},{5,11},{6,12},{7,13},{8,14},{9,15},... | collective-permute-start | bytes 196616
  597.3 20.9 %collective-permute-start.20 = (f32[16,1024]{1,0:T(8,128)S(1)}, f32[16,1024]{1,0:T(8,128)S(1)}, u32[]{:S(2)}, u32[]{:S(2)}) collective-permute-start(f32[16,1024]{1,0:T(8,128)S(1)} %fusion), channel_id=1, source_target_pairs={{0,5},{1,6},{2,7},{3,8},{4,9},{5,10},{6,11},{7,12},{8,13},{9,14},{... | collective-permute-start | bytes 196616
  602.5 15.7 %collective-permute-start.19 = (f32[16,1024]{1,0:T(8,128)S(1)}, f32[16,1024]{1,0:T(8,128)S(1)}, u32[]{:S(2)}, u32[]{:S(2)}) collective-permute-start(f32[16,1024]{1,0:T(8,128)S(1)} %fusion), channel_id=1, source_target_pairs={{0,4},{1,5},{2,6},{3,7},{4,8},{5,9},{6,10},{7,11},{8,12},{9,13},{1... | collective-permute-start | bytes 196616
  607.0 11.1 %collective-permute-start.18 = (f32[16,1024]{1,0:T(8,128)S(1)}, f32[16,1024]{1,0:T(8,128)S(1)}, u32[]{:S(2)}, u32[]{:S(2)}) collective-permute-start(f32[16,1024]{1,0:T(8,128)S(1)} %fusion), channel_id=1, source_target_pairs={{0,3},{1,4},{2,5},{3,6},{4,7},{5,8},{6,9},{7,10},{8,11},{9,12},{10... | collective-permute-start | bytes 196616
  608.3 9.8 %collective-permute-start.17 = (f32[16,1024]{1,0:T(8,128)S(1)}, f32[16,1024]{1,0:T(8,128)S(1)}, u32[]{:S(2)}, u32[]{:S(2)}) collective-permute-start(f32[16,1024]{1,0:T(8,128)S(1)} %fusion), channel_id=1, source_target_pairs={{0,2},{1,3},{2,4},{3,5},{4,6},{5,7},{6,8},{7,9},{8,10},{9,11},{10,... | collective-permute-start | bytes 196616
  611.5 7.1 %collective-permute-start.16 = (f32[16,1024]{1,0:T(8,128)S(1)}, f32[16,1024]{1,0:T(8,128)S(1)}, u32[]{:S(2)}, u32[]{:S(2)}) collective-permute-start(f32[16,1024]{1,0:T(8,128)S(1)} %fusion), channel_id=1, source_target_pairs={{0,1},{1,2},{2,3},{3,4},{4,5},{5,6},{6,7},{7,8},{8,9},{9,10},{10,1... | collective-permute-start | bytes 196616
  (197 other events, 1959.0 us)
Sparse Core Ops, SparseCore 0:
  10.9 11.5 all-gather.15
  24.0 10.0 all-gather.13
  35.7 10.2 all-gather.11
  128.5 11.2 all-gather.9
  249.7 6.8 reduce-scatter.12
  262.1 6.7 reduce-scatter.10
  271.2 8.8 reduce-scatter.8
  287.1 6.8 reduce-scatter.6
where the time goes:
time: 637 us; the launch traced here: 628 us
  blocking collectives  296 us (46%)
  matrix products  87.9 us (14%)
  starting transfers between devices  80.8 us (13%)
  local copies, waits for them, and re-layouts  80 us (13%)
  other arithmetic  60.8 us (10%)
  between operations  17.6 us (3%)
    psum x2, blocking collectives, norm_forward(): first_sum, second = lax.psum((first_sum, second), ('tm', 'src'))  82.3 us
    psum x2, blocking collectives, norm_backward(): first_sum, second = lax.psum((first_sum, second), ('tm', 'src'))  79.8 us
    unnamed x1, blocking collectives  79.2 us
    all_gather x1, blocking collectives, fetch_weights(): lax.all_gather(master.astype(jnp.bfloat16), ('tm', 'src'), axis=0, tiled=...  46.1 us
    dot_general x20, matrix products, contract_cols(): lax.dot_general(left_side, right_side, (((1,), (1,)), ((), ())), preferre...  40.4 us
    unnamed x425, local copies, waits for them, and re-layouts  38.1 us
    unnamed x10, starting transfers between devices  32.7 us
    ppermute x8, starting transfers between devices, with_halo(): before = lax.ppermute(last, axis, up)  31.2 us
  transfers between devices with their start and end apart: 34, of which 5 were waited for; matrix products, arithmetic and copies ran while one was open for 20% of the time, Pallas kernels for 0%

commit v1 on v0

v1 whole, which is shorter than its diff:
```python
import functools

import jax
import jax.numpy as jnp
from jax import lax
from jax.experimental import pallas as pl
from jax.experimental.pallas import tpu as pltpu
from jax.sharding import PartitionSpec as P

N = 512
L = 16
B = 128
SC = 128
HW = 512
C = 2
DIL = 128
ROW = 1024
SEGS = 8
MICRO = 4
STEP = 10
NCH = 340
BLK = 256
KINDS = 8

norm_eps = 1e-05
adam_eps = 1e-08
beta_one = 0.9
beta_two = 0.999
learn_rate = 0.2
weight_decay = 0.01

AXES = ("tm", "src")
f32 = jnp.float32
bf16 = jnp.bfloat16
VMEM_LIMIT = 56 * 1024 * 1024

R_IN, R_RES, R_SKIP, R_MASK, R_DEC, R_VEC = 0, 512, 1024, 1536, 2560, 2688
ROWS_ALL = 2720


def mm(a, b):
    return lax.dot_general(a, b, (((1,), (0,)), ((), ())), preferred_element_type=f32)


def mm_t(a, b):
    return lax.dot_general(a, b, (((1,), (1,)), ((), ())), preferred_element_type=f32)


def mm_rows(a, b):
    return lax.dot_general(a, b, (((0,), (0,)), ((), ())), preferred_element_type=f32)


def sigmoid(v):
    return 0.5 * jnp.tanh(0.5 * v) + 0.5


def vmem():
    return pl.BlockSpec(memory_space=pltpu.VMEM)


def smem():
    return pl.BlockSpec(memory_space=pltpu.SMEM)


def stages(n_dev):
    bits = n_dev.bit_length() - 1
    groups = []
    hi = bits - 1
    while hi >= 1:
        lo = max(1, hi - 1)
        groups.append(tuple(range(lo, hi + 1)))
        hi = lo - 1
    groups.append((0,))
    return groups


def spread(bits, k):
    return sum(((k >> j) & 1) << b for j, b in enumerate(bits))


def swap(value, mask, n_dev):
    return lax.ppermute(value, AXES, [(i, i ^ mask) for i in range(n_dev)])


def gather_tiles(tiles, n_dev):
    z = tiles
    groups = stages(n_dev)
    for bits in groups[:-1]:
        parts = [z] + [swap(z, spread(bits, k), n_dev) for k in range(1, 1 << len(bits))]
        z = jnp.concatenate(parts, axis=0)
    return z, swap(z, 1, n_dev)


def relative_block(owner, me, n_dev):
    q = owner ^ me
    index = jnp.zeros_like(q)
    size = 1
    for bits in stages(n_dev):
        digit = sum(((q >> b) & 1) << j for j, b in enumerate(bits))
        index = index + digit * size
        size = size << len(bits)
    return index


def share_sums(rows, n_dev):
    return lax.all_to_all(rows, AXES, 0, 0, tiled=True)


def tile_kernel(m_ref, out_ref, buf):
    slots = m_ref.shape[0]
    for j in range(8):
        buf[pl.ds(j, slots, stride=8), :] = m_ref[:, 128 * j : 128 * j + 128]
    out_ref[...] = buf[...].astype(bf16)


def to_tiles(master):
    slots = master.shape[0]
    return pl.pallas_call(
        tile_kernel,
        out_shape=jax.ShapeDtypeStruct((slots * 8, 128), bf16),
        in_specs=[vmem()],
        out_specs=vmem(),
        scratch_shapes=[pltpu.VMEM((slots * 8, 128), f32)],
        name="to_tiles",
    )(master)


def stat_rows(values, shape):
    lane = lax.broadcasted_iota(jnp.int32, shape, 1)
    row = jnp.zeros(shape, f32)
    for where, v in values.items():
        row = jnp.where(lane == where, v, row)
    return row


def unpack_kernel(
    pos_ref, own_ref, got_ref, x_ref, w_in, w_rs, w_mask, w_dec, w_dect, vec, stats, g, t, wd
):
    half = own_ref.shape[0]
    g[0:half, :] = own_ref[...].astype(f32)
    g[half : 2 * half, :] = got_ref[...].astype(f32)
    for i in range(NCH):
        start = pl.multiple_of(pos_ref[i] * 8, 8)
        t[8 * i : 8 * i + 8, :] = g[pl.ds(start, 8), :]
    for k in range(4):
        cols = slice(128 * k, 128 * k + 128)
        w_in[:, cols] = t[pl.ds(R_IN + k, 128, stride=4), :].astype(bf16)
        for c in range(C):
            w_mask[:, 512 * c + 128 * k : 512 * c + 128 * k + 128] = t[
                pl.ds(R_MASK + 512 * c + k, 128, stride=4), :
            ].astype(bf16)
        vec[:, cols] = t[pl.ds(R_VEC + k, 8, stride=4), :]
    w_rs[:, 0:128] = t[R_RES : R_RES + 512, :].astype(bf16)
    w_rs[:, 128:256] = t[R_SKIP : R_SKIP + 512, :].astype(bf16)
    part = lax.broadcasted_iota(jnp.int32, (64, 128), 1) // L
    for s in range(8):
        for c in range(C):
            rows = t[R_DEC + 64 * c : R_DEC + 64 * c + 64, :]
            rows = pltpu.roll(rows, (L * (c - s)) % 128, 1)
            wd[pl.ds(512 * c + s, 64, stride=8), :] = jnp.where(part == c, rows, 0.0)
    dec = wd[...]
    w_dec[...] = dec.astype(bf16)
    w_dect[...] = dec.T.astype(bf16)
    micro, frames, _ = x_ref.shape
    nb = frames // BLK
    sums = {}
    for m in range(micro):
        for b in range(nb):
            a = mm(x_ref[m, b * BLK : (b + 1) * BLK, :], w_in[...])
            u = a * sigmoid(a)
            first = jnp.sum(jnp.sum(u, axis=0, keepdims=True), axis=1, keepdims=True)
            second = jnp.sum(jnp.sum(u * u, axis=0, keepdims=True), axis=1, keepdims=True)
            sums[(m * nb + b) * KINDS] = first
            sums[(m * nb + b) * KINDS + 1] = second
    row = stat_rows(sums, (1, 128))
    stats[...] = jnp.broadcast_to(row[None], stats.shape)


def unpack(pos, own, got, feats, n_dev):
    outs = (
        jax.ShapeDtypeStruct((B, HW), bf16),
        jax.ShapeDtypeStruct((HW, B + SC), bf16),
        jax.ShapeDtypeStruct((SC, C * N), bf16),
        jax.ShapeDtypeStruct((C * N, 128), bf16),
        jax.ShapeDtypeStruct((128, C * N), bf16),
        jax.ShapeDtypeStruct((8, HW), f32),
        jax.ShapeDtypeStruct((n_dev, 1, 128), f32),
    )
    return pl.pallas_call(
        unpack_kernel,
        out_shape=outs,
        in_specs=[smem(), vmem(), vmem(), vmem()],
        out_specs=tuple(vmem() for _ in outs),
        scratch_shapes=[
            pltpu.VMEM((2 * own.shape[0], 128), f32),
            pltpu.VMEM((ROWS_ALL, 128), f32),
            pltpu.VMEM((C * N, 128), f32),
        ],
        compiler_params=pltpu.CompilerParams(vmem_limit_bytes=VMEM_LIMIT),
        name="unpack",
    )(pos, own, got, feats)


def norm_scale(stats, sel):
    means, factors = [], []
    lane = lax.broadcasted_iota(jnp.int32, (1, 128), 1) % KINDS
    for o in range(sel.shape[0]):
        t = jnp.sum(stats * sel[o], axis=0, keepdims=True)
        mean = jnp.sum(jnp.where(lane == 0, t, 0.0), axis=1, keepdims=True)
        second = jnp.sum(jnp.where(lane == 1, t, 0.0), axis=1, keepdims=True)
        means.append(mean)
        factors.append(lax.rsqrt(second - mean * mean + norm_eps))
    return means, factors


def taps(vec, same_ref, m, nb):
    k0, k2 = vec[4:5, :], vec[6:7, :]
    out = []
    for h in range(2 * nb):
        lo = k0 * same_ref[m, h // 2] if h % 2 == 0 else k0
        hi = k2 if h % 2 == 0 else k2 * same_ref[m, h // 2 + 1]
        out.append((lo, hi))
    return out


def depth_kernel(
    same_ref, stats_ref, sel_ref, x_ref, xb_ref, xa_ref, w_in, vec, d_ref, out_stats, acc
):
    m = pl.program_id(0)
    frames = x_ref.shape[1]
    nb = frames // BLK
    means, factors = norm_scale(stats_ref[:, 0, :], sel_ref[0])
    g1, b1 = 1.0 + vec[0:1, :], vec[1:2, :]

    def normed(x, o):
        a = mm(x, w_in[...])
        u = a * sigmoid(a)
        scale = factors[o] * g1
        return (u * scale + (b1 - means[o] * scale)).astype(bf16).astype(f32)

    n1 = [normed(xb_ref[0], 0)]
    for h in range(2 * nb):
        n1.append(normed(x_ref[0, h * DIL : (h + 1) * DIL, :], 1 + h // 2))
    n1.append(normed(xa_ref[0], nb + 1))
    tap = taps(vec, same_ref, m, nb)
    k1, kb = vec[5:6, :], vec[7:8, :]
    lane = lax.broadcasted_iota(jnp.int32, (1, 128), 1)
    row = jnp.where(m == 0, jnp.zeros((1, 128), f32), acc[...])
    for b in range(nb):
        first, second = 0.0, 0.0
        for h in (2 * b, 2 * b + 1):
            d = tap[h][0] * n1[h] + k1 * n1[h + 1] + tap[h][1] * n1[h + 2] + kb
            d_ref[0, h * DIL : (h + 1) * DIL, :] = d
            v = d * sigmoid(d)
            first = first + jnp.sum(v, axis=0, keepdims=True)
            second = second + jnp.sum(v * v, axis=0, keepdims=True)
        at = (m * nb + b) * KINDS
        row = jnp.where(lane == at, jnp.sum(first, axis=1, keepdims=True), row)
        row = jnp.where(lane == at + 1, jnp.sum(second, axis=1, keepdims=True), row)
    acc[...] = row
    out_stats[...] = jnp.broadcast_to(row[None], out_stats.shape)


def per_micro(shape):
    rest = tuple(shape[1:])
    zeros = (0,) * len(rest)
    return pl.BlockSpec((1,) + rest, lambda m: (m,) + zeros)


def whole(shape):
    zeros = (0,) * len(shape)
    return pl.BlockSpec(tuple(shape), lambda m: zeros)


def depth(same, stats, sel, feats, before, after, w_in, vec):
    micro, frames, _ = feats.shape
    return pl.pallas_call(
        depth_kernel,
        grid=(micro,),
        out_shape=(
            jax.ShapeDtypeStruct((micro, frames, HW), f32),
            jax.ShapeDtypeStruct(stats.shape, f32),
        ),
        in_specs=[
            smem(),
            whole(stats.shape),
            per_micro(sel.shape),
            per_micro(feats.shape),
            per_micro(before.shape),
            per_micro(after.shape),
            whole(w_in.shape),
            whole(vec.shape),
        ],
        out_specs=(per_micro((micro, frames, HW)), whole(stats.shape)),
        scratch_shapes=[pltpu.VMEM((1, 128), f32)],
        compiler_params=pltpu.CompilerParams(vmem_limit_bytes=VMEM_LIMIT),
        name="depth",
    )(same, stats, sel, feats, before, after, w_in, vec)


def head_kernel(
    same_ref,
    stats_ref,
    sel_ref,
    d_ref,
    x_ref,
    enc_ref,
    dy_ref,
    dw_ref,
    w_rs,
    w_mask,
    w_dec,
    w_dect,
    vec,
    block_ref,
    waves_ref,
    dn2_ref,
    out_stats,
    g_rs,
    g_mask,
    g_dec,
    g_vec,
    acc,
):
    m = pl.program_id(0)
    frames = d_ref.shape[1]
    nb = frames // BLK

    @pl.when(m == 0)
    def _():
        g_rs[...] = jnp.zeros_like(g_rs)
        g_mask[...] = jnp.zeros_like(g_mask)
        g_dec[...] = jnp.zeros_like(g_dec)
        g_vec[...] = jnp.zeros_like(g_vec)
        acc[...] = jnp.zeros_like(acc)

    means, factors = norm_scale(stats_ref[:, 0, :], sel_ref[0])
    g1, g2, b1, b2 = 1.0 + vec[0:1, :], 1.0 + vec[2:3, :], vec[1:2, :], vec[3:4, :]
    k1, kb = vec[5:6, :], vec[7:8, :]
    tap = taps(vec, same_ref, m, nb)
    lane = lax.broadcasted_iota(jnp.int32, (1, 128), 1)
    row = acc[...]
    for b in range(nb):
        rows = slice(b * BLK, (b + 1) * BLK)
        mean, factor = means[1 + b], factors[1 + b]
        scale = factor * g2
        shift = b2 - mean * scale
        d = d_ref[0, rows, :]
        v = d * sigmoid(d)
        n2 = (v * scale + shift).astype(bf16)
        ys = mm(n2, w_rs[...])
        block_ref[0, rows, :] = (x_ref[0, rows, :].astype(f32) + ys[:, 0:B]).astype(bf16)
        s = ys[:, B : B + SC]
        sg = sigmoid(s)
        z = (s * sg).astype(bf16)
        slope = sg * (1.0 + s * (1.0 - sg))
        dw = dw_ref[0, rows, :]
        enc = enc_ref[0, rows, :].astype(f32)
        dz = jnp.zeros((BLK, SC), f32)
        wave = jnp.zeros((BLK, 128), f32)
        for c in range(C):
            cols = slice(c * N, (c + 1) * N)
            p = sigmoid(mm(z, w_mask[:, cols]))
            pe = p * enc
            e = pe.astype(bf16)
            wave = wave + mm(e, w_dec[cols, :])
            dq = (mm(dw, w_dect[0 : C * L, cols]) * (pe - pe * p)).astype(bf16)
            dz = dz + mm_t(dq, w_mask[:, cols])
            g_dec[:, cols] += mm_rows(dw, e)
            g_mask[:, cols] += mm_rows(z, dq)
        waves_ref[0, rows, :] = wave[:, 0 : C * L].astype(bf16)
        ds = (dz * slope).astype(bf16)
        dys = jnp.concatenate([dy_ref[0, rows, :], ds], axis=1)
        dn2 = mm_t(dys, w_rs[...])
        g_rs[...] += mm_rows(dys, n2)
        dn2_ref[0, rows, :] = dn2
        sum_d = jnp.sum(dn2, axis=0, keepdims=True)
        sum_dv = jnp.sum(dn2 * v, axis=0, keepdims=True)
        gain = (sum_dv - mean * sum_d) * factor
        g_vec[2:3, :] += gain
        g_vec[3:4, :] += sum_d
        vals = [sum_d * g2, gain * g2]
        six = [jnp.zeros((1, HW), f32)] * 6
        for h in (0, 1):
            hr = slice(b * BLK + h * DIL, b * BLK + (h + 1) * DIL)
            dh = d_ref[0, hr, :]
            sig = sigmoid(dh)
            vh = dh * sig
            sd = sig + vh * (1.0 - sig)
            a = dn2_ref[0, hr, :] * sd
            cv = vh * sd
            a0 = jnp.sum(a, axis=0, keepdims=True)
            a1 = jnp.sum(a * dh, axis=0, keepdims=True)
            s0 = jnp.sum(sd, axis=0, keepdims=True)
            s1 = jnp.sum(sd * dh, axis=0, keepdims=True)
            c0 = jnp.sum(cv, axis=0, keepdims=True)
            c1 = jnp.sum(cv * dh, axis=0, keepdims=True)
            lo, hi = tap[2 * b + h]
            kappa = k1 + lo + hi
            vw = g1 * kappa
            delta = kb + b1 * kappa
            a0, a1 = a0 * scale, a1 * scale
            s0, s1 = s0 * factor, s1 * factor
            c0, c1 = c0 * factor * factor - mean * factor * s0, c1 * factor * factor - mean * factor * s1
            new = [vw * a0, vw * s0, vw * c0, a1 - delta * a0, s1 - delta * s0, c1 - delta * c0]
            six = [p0 + p1 for p0, p1 in zip(six, new)]
        for k, val in enumerate(vals + six):
            at = (m * nb + b) * KINDS + k
            row = jnp.where(lane == at, jnp.sum(val, axis=1, keepdims=True), row)
    acc[...] = row
    out_stats[...] = jnp.broadcast_to(row[None], out_stats.shape)


def head(same, stats, sel, d, feats, enc, dy, dw, w_rs, w_mask, w_dec, w_dect, vec):
    micro, frames, _ = feats.shape
    outs = (
        (feats.shape, bf16, True),
        ((micro, frames, C * L), bf16, True),
        (d.shape, f32, True),
        (stats.shape, f32, False),
        ((B + SC, HW), f32, False),
        ((SC, C * N), f32, False),
        ((C * L, C * N), f32, False),
        ((8, HW), f32, False),
    )
    return pl.pallas_call(
        head_kernel,
        grid=(micro,),
        out_shape=tuple(jax.ShapeDtypeStruct(s, t) for s, t, _ in outs),
        in_specs=[
            smem(),
            whole(stats.shape),
            per_micro(sel.shape),
            per_micro(d.shape),
            per_micro(feats.shape),
            per_micro(enc.shape),
            per_micro(dy.shape),
            per_micro(dw.shape),
            whole(w_rs.shape),
            whole(w_mask.shape),
            whole(w_dec.shape),
            whole(w_dect.shape),
            whole(vec.shape),
        ],
        out_specs=tuple(per_micro(s) if each else whole(s) for s, _, each in outs),
        scratch_shapes=[pltpu.VMEM((1, 128), f32)],
        compiler_params=pltpu.CompilerParams(vmem_limit_bytes=VMEM_LIMIT),
        name="head",
    )(same, stats, sel, d, feats, enc, dy, dw, w_rs, w_mask, w_dec, w_dect, vec)


def back_means(stats, sel):
    lane = lax.broadcasted_iota(jnp.int32, (1, 128), 1) % KINDS
    t = jnp.sum(stats * sel, axis=0, keepdims=True)
    v = [jnp.sum(jnp.where(lane == k, t, 0.0), axis=1, keepdims=True) for k in range(KINDS)]
    p2, q2 = v[0], v[1]
    return p2, q2, v[2] - p2 * v[3] - q2 * v[4], v[5] - p2 * v[6] - q2 * v[7]


def depth_grad(d, dn2, mean, factor, g2, p2, q2):
    sig = sigmoid(d)
    v = d * sig
    sd = sig + v * (1.0 - sig)
    scale = factor * g2
    slope = factor * factor * q2
    shift = factor * p2 - slope * mean
    return (sd * (dn2 * scale - v * slope - shift)).astype(bf16)


def edge_kernel(stats2_ref, stats3_ref, sel_ref, d_ref, dn2_ref, vec, lo_ref, hi_ref):
    frames = d_ref.shape[1]
    nb = frames // BLK
    means, factors = norm_scale(stats2_ref[:, 0, :], sel_ref[0])
    g2 = 1.0 + vec[2:3, :]
    for ref, b, start in ((lo_ref, 0, 0), (hi_ref, nb - 1, frames - DIL)):
        p2, q2, _, _ = back_means(stats3_ref[:, 0, :], sel_ref[0, 1 + b])
        rows = slice(start, start + DIL)
        ref[0] = depth_grad(
            d_ref[0, rows, :], dn2_ref[0, rows, :], means[1 + b], factors[1 + b], g2, p2, q2
        )


def edges(stats2, stats3, sel, d, dn2, vec):
    micro, frames, _ = d.shape
    return pl.pallas_call(
        edge_kernel,
        grid=(micro,),
        out_shape=(jax.ShapeDtypeStruct((micro, DIL, HW), bf16),) * 2,
        in_specs=[
            whole(stats2.shape),
            whole(stats3.shape),
            per_micro(sel.shape),
            per_micro(d.shape),
            per_micro(dn2.shape),
            whole(vec.shape),
        ],
        out_specs=(per_micro((micro, DIL, HW)),) * 2,
        compiler_params=pltpu.CompilerParams(vmem_limit_bytes=VMEM_LIMIT),
        name="edges",
    )(stats2, stats3, sel, d, dn2, vec)


def input_kernel(
    same_ref,
    stats1_ref,
    stats2_ref,
    stats3_ref,
    sel_ref,
    d_ref,
    dn2_ref,
    lo_ref,
    hi_ref,
    x_ref,
    dy_ref,
    w_in,
    vec,
    feats_ref,
    g_in,
    g_vec,
):
    m = pl.program_id(0)
    frames = d_ref.shape[1]
    nb = frames // BLK

    @pl.when(m == 0)
    def _():
        g_in[...] = jnp.zeros_like(g_in)
        g_vec[...] = jnp.zeros_like(g_vec)

    sel = sel_ref[0]
    mean1, factor1 = norm_scale(stats1_ref[:, 0, :], sel)
    mean2, factor2 = norm_scale(stats2_ref[:, 0, :], sel)
    g1, g2, b1 = 1.0 + vec[0:1, :], 1.0 + vec[2:3, :], vec[1:2, :]
    k0, k1, k2 = vec[4:5, :], vec[5:6, :], vec[6:7, :]
    back = [back_means(stats3_ref[:, 0, :], sel[1 + b]) for b in range(nb)]
    dd = [lo_ref[0].astype(f32)]
    for h in range(2 * nb):
        rows = slice(h * DIL, (h + 1) * DIL)
        b = h // 2
        dd.append(
            depth_grad(
                d_ref[0, rows, :], dn2_ref[0, rows, :], mean2[1 + b], factor2[1 + b], g2, back[b][0], back[b][1]
            ).astype(f32)
        )
    dd.append(hi_ref[0].astype(f32))
    zero = jnp.zeros((1, HW), f32)
    t0, t1, t2, tb, gg, gb = zero, zero, zero, zero, zero, zero
    for h in range(2 * nb):
        b = h // 2
        rows = slice(h * DIL, (h + 1) * DIL)
        x = x_ref[0, rows, :]
        a = mm(x, w_in[...])
        sig = sigmoid(a)
        u = a * sig
        mean, factor = mean1[1 + b], factor1[1 + b]
        scale = factor * g1
        n1 = (u * scale + (b1 - mean * scale)).astype(bf16).astype(f32)
        lo = same_ref[m, b] if h % 2 == 0 else 1.0
        hi = 1.0 if h % 2 == 0 else same_ref[m, b + 1]
        here, prev, nxt = dd[h + 1], dd[h], dd[h + 2]
        t0 = t0 + jnp.sum(nxt * n1, axis=0, keepdims=True) * hi
        t1 = t1 + jnp.sum(here * n1, axis=0, keepdims=True)
        t2 = t2 + jnp.sum(prev * n1, axis=0, keepdims=True) * lo
        tb = tb + jnp.sum(here, axis=0, keepdims=True)
        dn1 = k1 * here + (k0 * hi) * nxt + (k2 * lo) * prev
        h1 = (u - mean) * factor
        gg = gg + jnp.sum(dn1 * h1, axis=0, keepdims=True)
        gb = gb + jnp.sum(dn1, axis=0, keepdims=True)
        du = factor * (dn1 * g1 - back[b][2] - h1 * back[b][3])
        da = (du * (sig + u * (1.0 - sig))).astype(bf16)
        g_in[...] += mm_rows(x, da)
        feats_ref[0, rows, :] = (dy_ref[0, rows, :].astype(f32) + mm_t(da, w_in[...])).astype(bf16)
    for r, val in ((0, gg), (1, gb), (4, t0), (5, t1), (6, t2), (7, tb)):
        g_vec[r : r + 1, :] += val


def input_grad(same, stats1, stats2, stats3, sel, d, dn2, lo, hi, feats, dy, w_in, vec):
    micro, frames, _ = d.shape
    return pl.pallas_call(
        input_kernel,
        grid=(micro,),
        out_shape=(
            jax.ShapeDtypeStruct(feats.shape, bf16),
            jax.ShapeDtypeStruct((B, HW), f32),
            jax.ShapeDtypeStruct((8, HW), f32),
        ),
        in_specs=[
            smem(),
            whole(stats1.shape),
            whole(stats2.shape),
            whole(stats3.shape),
            per_micro(sel.shape),
            per_micro(d.shape),
            per_micro(dn2.shape),
            per_micro(lo.shape),
            per_micro(hi.shape),
            per_micro(feats.shape),
            per_micro(dy.shape),
            whole(w_in.shape),
            whole(vec.shape),
        ],
        out_specs=(per_micro(feats.shape), whole((B, HW)), whole((8, HW))),
        compiler_params=pltpu.CompilerParams(vmem_limit_bytes=VMEM_LIMIT),
        name="input_grad",
    )(same, stats1, stats2, stats3, sel, d, dn2, lo, hi, feats, dy, w_in, vec)


def pack_kernel(pos_ref, g_in, g_rs, g_mask, g_dec, vec_a, vec_b, keep_ref, send_ref, t, out, wd):
    for k in range(4):
        cols = slice(128 * k, 128 * k + 128)
        t[pl.ds(R_IN + k, 128, stride=4), :] = g_in[:, cols]
        for c in range(C):
            t[pl.ds(R_MASK + 512 * c + k, 128, stride=4), :] = g_mask[
                :, 512 * c + 128 * k : 512 * c + 128 * k + 128
            ]
        t[pl.ds(R_VEC + k, 8, stride=4), :] = vec_a[:, cols] + vec_b[:, cols]
    t[R_RES : R_RES + 512, :] = g_rs[0:128, :].T
    t[R_SKIP : R_SKIP + 512, :] = g_rs[128:256, :].T
    wd[...] = jnp.concatenate([g_dec[...], jnp.zeros((128 - C * L, C * N), f32)], axis=0).T
    part = lax.broadcasted_iota(jnp.int32, (64, 128), 1) // L
    for c in range(C):
        rows = jnp.zeros((64, 128), f32)
        for s in range(8):
            piece = pltpu.roll(wd[pl.ds(512 * c + s, 64, stride=8), :], (L * (s - c)) % 128, 1)
            rows = jnp.where(part == s, piece, rows)
        t[R_DEC + 64 * c : R_DEC + 64 * c + 64, :] = rows
    out[...] = jnp.zeros_like(out)
    for i in range(NCH):
        start = pl.multiple_of(pos_ref[i] * 8, 8)
        out[pl.ds(start, 8), :] = t[8 * i : 8 * i + 8, :]
    half = keep_ref.shape[0]
    keep_ref[...] = out[0:half, :]
    send_ref[...] = out[half : 2 * half, :].astype(bf16)


def pack(pos, g_in, g_rs, g_mask, g_dec, vec_a, vec_b, rows):
    return pl.pallas_call(
        pack_kernel,
        out_shape=(
            jax.ShapeDtypeStruct((rows // 2, 128), f32),
            jax.ShapeDtypeStruct((rows // 2, 128), bf16),
        ),
        in_specs=[smem()] + [vmem()] * 6,
        out_specs=(vmem(), vmem()),
        scratch_shapes=[
            pltpu.VMEM((ROWS_ALL, 128), f32),
            pltpu.VMEM((rows, 128), f32),
            pltpu.VMEM((C * N, 128), f32),
        ],
        compiler_params=pltpu.CompilerParams(vmem_limit_bytes=VMEM_LIMIT),
        name="pack",
    )(pos, g_in, g_rs, g_mask, g_dec, vec_a, vec_b)


def fold_kernel(n_got, n_next, *refs):
    keep_ref, got = refs[0], refs[1 : 1 + n_got]
    outs = refs[1 + n_got :]
    total = keep_ref[...]
    for g in got:
        total = total + g[...].astype(f32)
    size = total.shape[0] // n_next
    outs[0][...] = total[0:size, :]
    for q in range(1, n_next):
        outs[q][...] = total[q * size : (q + 1) * size, :].astype(bf16)


def fold(keep, got, n_next):
    size = keep.shape[0] // n_next
    outs = [jax.ShapeDtypeStruct((size, 128), f32)]
    outs += [jax.ShapeDtypeStruct((size, 128), bf16)] * (n_next - 1)
    return pl.pallas_call(
        functools.partial(fold_kernel, len(got), n_next),
        out_shape=tuple(outs),
        in_specs=[vmem()] * (1 + len(got)),
        out_specs=tuple(vmem() for _ in outs),
        name="fold",
    )(keep, *got)


def adam_kernel(n_got, count_ref, *refs):
    keep_ref, got = refs[0], refs[1 : 1 + n_got]
    master_ref, one_ref, two_ref, new_master, new_one, new_two, buf = refs[1 + n_got :]
    total = keep_ref[...]
    for g in got:
        total = total + g[...].astype(f32)
    buf[...] = total
    slots = master_ref.shape[0]
    used = lax.broadcasted_iota(jnp.int32, (slots, 128), 0) < count_ref[0]
    for j in range(8):
        cols = slice(128 * j, 128 * j + 128)
        grad = buf[pl.ds(j, slots, stride=8), :]
        master = master_ref[:, cols]
        one = beta_one * one_ref[:, cols] + (1.0 - beta_one) * grad
        two = beta_two * two_ref[:, cols] + (1.0 - beta_two) * grad * grad
        unbias_one = one / (1.0 - beta_one**STEP)
        unbias_two = two / (1.0 - beta_two**STEP)
        new = master - learn_rate * (
            unbias_one / (jnp.sqrt(unbias_two) + adam_eps) + weight_decay * master
        )
        new_master[:, cols] = jnp.where(used, new, 0.0)
        new_one[:, cols] = jnp.where(used, one, 0.0)
        new_two[:, cols] = jnp.where(used, two, 0.0)


def adam(count, keep, got, master, one, two):
    out = jax.ShapeDtypeStruct(master.shape, f32)
    return pl.pallas_call(
        functools.partial(adam_kernel, len(got)),
        out_shape=(out, out, out),
        in_specs=[smem()] + [vmem()] * (4 + len(got)),
        out_specs=(vmem(), vmem(), vmem()),
        scratch_shapes=[pltpu.VMEM(keep.shape, f32)],
        name="adam",
    )(count, keep, *got, master, one, two)


def local(n_tm, n_src, feats, encoded, seg_lengths, owners, master, moment_one, moment_two, out_cot, wave_cot):
    n_dev = n_tm * n_src
    me = lax.axis_index(AXES)
    core = lax.axis_index("src")
    micro, frames, _ = feats.shape
    nb = frames // BLK
    slots = master.shape[0]

    tiles = to_tiles(master)
    own, got = gather_tiles(tiles, n_dev)

    up = [(i, i + 1) for i in range(n_dev - 1)]
    down = [(i + 1, i) for i in range(n_dev - 1)]
    before = lax.ppermute(feats[:, frames - DIL :, :], AXES, up)
    after = lax.ppermute(feats[:, :DIL, :], AXES, down)

    pair = [(2 * i + j, 2 * i + 1 - j) for i in range(n_tm) for j in range(2)]
    dw_keep = lax.dynamic_slice_in_dim(wave_cot[:, 0], core * frames, frames, axis=1)
    dw_send = lax.dynamic_slice_in_dim(wave_cot[:, 0], (1 - core) * frames, frames, axis=1)
    dw_got = lax.ppermute(dw_send, AXES, pair)
    first_core = core == 0
    dw = jnp.concatenate(
        [jnp.where(first_core, dw_keep, dw_got), jnp.where(first_core, dw_got, dw_keep)], axis=2
    )

    owner_ids = owners[:, 0]
    order = jnp.arange(NCH, dtype=jnp.int32)
    earlier = (owner_ids[:, None] == owner_ids[None, :]) & (order[None, :] < order[:, None])
    rank = jnp.sum(earlier.astype(jnp.int32), axis=1)
    pos = relative_block(owner_ids, me, n_dev) * slots + rank
    count = jnp.sum((owner_ids == me).astype(jnp.int32)).reshape(1)

    seg_order = jnp.arange(SEGS)
    bounds = jnp.sum(
        jnp.where(seg_order[:, None] >= seg_order[None, :], seg_lengths[:, None, :], 0), axis=2
    )
    def segment(block):
        return jnp.sum((block[..., None] * BLK >= bounds[:, None, None, :]).astype(jnp.int32), axis=-1)
    lane = jnp.arange(128)
    all_blocks = jnp.arange(n_dev)[:, None] * nb + (lane[None, :] // KINDS) % nb
    seg_all = segment(all_blocks[None])
    near = me * nb - 1 + jnp.arange(nb + 2)
    seg_near = segment(near[None, :, None])[:, :, 0]
    seg_near = jnp.where((near >= 0) & (near < n_dev * nb), seg_near, -1)
    lengths = jnp.sum(
        jnp.where(seg_near[:, :, None] == seg_order[None, None, :], seg_lengths[:, None, :], 0), axis=2
    )
    inverse = 1.0 / (jnp.maximum(lengths, 1).astype(f32) * HW)
    lane_micro = lane // (KINDS * nb)
    sel = jnp.where(
        (seg_all[:, None] == seg_near[:, :, None, None])
        & (lane_micro[None, None, None, :] == jnp.arange(micro)[:, None, None, None]),
        inverse[:, :, None, None],
        0.0,
    )
    same = (seg_near[:, 1:] == seg_near[:, :-1]).astype(f32)

    w_in, w_rs, w_mask, w_dec, w_dect, vec, stats = unpack(pos, own, got, feats, n_dev)
    stats1 = share_sums(stats, n_dev)
    d, stats = depth(same, stats1, sel, feats, before, after, w_in, vec)
    stats2 = share_sums(stats, n_dev)
    block_out, waves2, dn2, stats, g_rs, g_mask, g_dec, vec_a = head(
        same, stats2, sel, d, feats, encoded, out_cot, dw, w_rs, w_mask, w_dec, w_dect, vec
    )
    stats3 = share_sums(stats, n_dev)

    mine = jnp.where(first_core, waves2[:, :, :L], waves2[:, :, L:])
    other = jnp.where(first_core, waves2[:, :, L:], waves2[:, :, :L])
    theirs = lax.ppermute(other, AXES, pair)
    waves = jnp.concatenate(
        [jnp.where(first_core, mine, theirs), jnp.where(first_core, theirs, mine)], axis=1
    )[:, None]

    low, high = edges(stats2, stats3, sel, d, dn2, vec)
    prev_dd = lax.ppermute(high, AXES, up)
    next_dd = lax.ppermute(low, AXES, down)
    feats_grad, g_in, vec_b = input_grad(
        same, stats1, stats2, stats3, sel, d, dn2, prev_dd, next_dd, feats, out_cot, w_in, vec
    )

    keep, send = pack(pos, g_in, g_rs, g_mask, g_dec, vec_a, vec_b, n_dev * slots * 8)
    received = [swap(send, 1, n_dev)]
    for bits in reversed(stages(n_dev)[:-1]):
        n_next = 1 << len(bits)
        keep, *sends = fold(keep, received, n_next)
        received = [swap(s, spread(bits, k + 1), n_dev) for k, s in enumerate(sends)]
    new_master, new_one, new_two = adam(count, keep, received, master, moment_one, moment_two)
    return block_out, feats_grad, waves, new_master, new_one, new_two


def solution(mesh):
    n_tm, n_src = mesh.shape["tm"], mesh.shape["src"]
    return jax.shard_map(
        functools.partial(local, n_tm, n_src),
        mesh=mesh,
        in_specs=(
            P(None, AXES, None),
            P(None, AXES, None),
            P(),
            P(),
            P(AXES, None),
            P(AXES, None),
            P(AXES, None),
            P(None, AXES, None),
            P(None, "src", "tm", None),
        ),
        out_specs=(
            P(None, AXES, None),
            P(None, AXES, None),
            P(None, "src", "tm", None),
            P(AXES, None),
            P(AXES, None),
            P(AXES, None),
        ),
        check_vma=False,
    )
```

time: 637 us -> 162 us (0.25)
  the two profiles are of different devices: /device:TPU:1 before, /device:TPU:0 now
where the time goes in v1:
time: 162 us; the launch traced here: 161 us
  Pallas kernels  57.2 us (35%)
  starting transfers between devices  44.2 us (27%)
  waiting for transfers between devices  31.5 us (19%)
  blocking collectives  10.2 us (6%)
  other arithmetic  8.89 us (5%)
  local copies, waits for them, and re-layouts  8.34 us (5%)
    ppermute x14, starting transfers between devices, swap(): return lax.ppermute(value, AXES, [(i, i ^ mask) for i in range(n_dev)])  27.8 us
    pallas_call x1, Pallas kernels, head(): pl.pallas_call(head_kernel, grid=(micro,), out_shape=tuple((jax.ShapeDtyp...  18 us
    ppermute x14, waiting for transfers between devices, swap(): return lax.ppermute(value, AXES, [(i, i ^ mask) for i in range(n_dev)])  16 us
    all_to_all x2, waiting for transfers between devices, share_sums(): return lax.all_to_all(rows, AXES, 0, 0, tiled=True)  12.9 us
    pallas_call x1, Pallas kernels, input_grad(): pl.pallas_call(input_kernel, grid=(micro,), out_shape=(jax.ShapeDtypeStru...  12.3 us
    all_to_all x1, blocking collectives, share_sums(): return lax.all_to_all(rows, AXES, 0, 0, tiled=True)  10.2 us
    all_to_all x2, starting transfers between devices, share_sums(): return lax.all_to_all(rows, AXES, 0, 0, tiled=True)  6.96 us
    pallas_call x1, Pallas kernels, depth(): pl.pallas_call(depth_kernel, grid=(micro,), out_shape=(jax.ShapeDtypeStru...  6.9 us
  transfers between devices with their start and end apart: 22, of which 11 were waited for; matrix products, arithmetic and copies ran while one was open for 8% of the time, Pallas kernels for 4%

profile of v1, /device:TPU:0, one launch (start us, length us, event | category | flops | bytes accessed | tf_op | source)
XLA Modules:
  0.0 161.3 jit_solution(5328931538863691862)
XLA Ops:
  0.6 1.5 to_tiles.1
  2.1 5.0 %collective-permute-start.2 = (bf16[88,128]{1,0:T(8,128)(2,1)}, bf16[88,128]{1,0:T(8,128)(2,1)S(1)}, u32[]{:S(2)}, u32[]{:S(2)}) collective-permute-start(bf16[88,128]{1,0:T(8,128)(2,1)} %to_tiles.1), channel_id=1, source_target_pairs={{0,24},{1,25},{2,26},{3,27},{4,28},{5,29},{6,30},{7,31},{8,16},{9,... | collective-permute-start | bytes 67592 | tf_op jit(solution)/shard_map/ppermute | solution.py:82
  10.0 3.0 %collective-permute-start.7 = (bf16[4,128,128]{2,1,0:T(8,128)(2,1)S(1)}, bf16[4,128,128]{2,1,0:T(8,128)(2,1)S(1)}, u32[]{:S(2)}, u32[]{:S(2)}) collective-permute-start(bf16[4,128,128]{2,1,0:T(8,128)(2,1)S(1)} %get-tuple-element.99), channel_id=1, source_target_pairs={{0,1},{1,2},{2,3},{3,4},{4,5},{5,6},{6,7},{7,8},{8,9},{9,10},{10,1... | collective-permute-start | bytes 393224 | tf_op jit(solution)/shard_map/ppermute | solution.py:730
  19.1 1.4 collective-permute-start.9
  21.2 3.4 %collective-permute-start.5 = (bf16[352,128]{1,0:T(8,128)(2,1)S(1)}, bf16[352,128]{1,0:T(8,128)(2,1)S(1)}, u32[]{:S(2)}, u32[]{:S(2)}) collective-permute-start(bf16[352,128]{1,0:T(8,128)(2,1)S(1)} %pad_maximum_fusion.1), channel_id=1, source_target_pairs={{0,6},{1,7},{2,4},{3,5},{4,2},{5,3},{6,0},{7,1},{8,14},{9,15},{10,... | collective-permute-start | bytes 270344 | tf_op jit(solution)/shard_map/ppermute | solution.py:82
  24.7 4.5 %collective-permute-done.3 = bf16[352,128]{1,0:T(8,128)(2,1)S(1)} collective-permute-done((bf16[352,128]{1,0:T(8,128)(2,1)S(1)}, bf16[352,128]{1,0:T(8,128)(2,1)S(1)}, u32[]{:S(2)}, u32[]{:S(2)}) %collective-permute-start.3) | collective-permute-done | bytes 90144 | tf_op jit(solution)/shard_map/ppermute | solution.py:82
  29.9 3.7 %collective-permute-done.4 = bf16[352,128]{1,0:T(8,128)(2,1)S(1)} collective-permute-done((bf16[352,128]{1,0:T(8,128)(2,1)S(1)}, bf16[352,128]{1,0:T(8,128)(2,1)S(1)}, u32[]{:S(2)}, u32[]{:S(2)}) %collective-permute-start.4) | collective-permute-done | bytes 90144 | tf_op jit(solution)/shard_map/ppermute | solution.py:82
  36.7 4.0 %unpack.1 = (bf16[128,512]{1,0:T(8,128)(2,1)}, bf16[512,256]{1,0:T(8,128)(2,1)}, bf16[128,1024]{1,0:T(8,128)(2,1)}, bf16[1024,128]{1,0:T(8,128)(2,1)}, bf16[128,...) custom-call(s32[340]{0:T(512)} %get-tuple-element.103.pos_ref, bf16[1408,128]{1,0:T(8,128)(2,1)} %copy-done.3, ...), custom_call_target="tpu_custom_call" | custom-call | tf_op jit(solution)/shard_map/unpack/pallas_call | solution.py:189
  40.8 4.4 %all-to-all-start = ((f32[32,1,128]{2,1,0:T(1,128)}), f32[32,1,128]{2,1,0:T(1,128)S(1)}, u32[]{:S(2)}, u32[]{:S(2)}) async-start(f32[32,1,128]{2,1,0:T(1,128)} %get-tuple-element.41), calls=%async_computation | async-start | bytes 32768 | tf_op jit(solution)/shard_map/all_to_all | solution.py:106
  45.3 6.9 %all-to-all-done.stats_ref.stats1_ref = f32[32,1,128]{2,1,0:T(1,128)S(1)} async-done(((f32[32,1,128]{2,1,0:T(1,128)}), f32[32,1,128]{2,1,0:T(1,128)S(1)}, u32[]{:S(2)}, u32[]{:S(2)}) %all-to-all-start) | async-done | bytes 16416 | tf_op jit(solution)/shard_map/all_to_all | solution.py:106
  52.9 6.9 %depth.1 = (f32[4,512,512]{2,1,0:T(8,128)}, f32[32,1,128]{2,1,0:T(1,128)}) custom-call(f32[4,3]{1,0:T(4,128)} %fusion.1.same_ref, f32[32,1,128]{2,1,0:T(1,128)} %copy-done.7, f32[4,4,32,128]{3,2,1,0:T(8,128)} %and_select_fusion.sel_ref, bf16[4,512,128]{2,1,0:T(8,128)(2,1)} %x_ref.7, bf16[4,128,128]{2,1,0:T(8,128)(2,1)} %copy-done.9, ...), custom_call_target="tpu_custom_call" | custom-call | tf_op jit(solution)/shard_map/depth/pallas_call | solution.py:277
  59.8 2.5 %all-to-all-start.1 = ((f32[32,1,128]{2,1,0:T(1,128)}), f32[32,1,128]{2,1,0:T(1,128)S(1)}, u32[]{:S(2)}, u32[]{:S(2)}) async-start(f32[32,1,128]{2,1,0:T(1,128)} %get-tuple-element.44), calls=%async_computation.1 | async-start | bytes 32768 | tf_op jit(solution)/shard_map/all_to_all | solution.py:106
  63.4 6.0 %all-to-all-done.1.stats_ref.stats2_ref = f32[32,1,128]{2,1,0:T(1,128)S(1)} async-done(((f32[32,1,128]{2,1,0:T(1,128)}), f32[32,1,128]{2,1,0:T(1,128)S(1)}, u32[]{:S(2)}, u32[]{:S(2)}) %all-to-all-start.1) | async-done | bytes 16416 | tf_op jit(solution)/shard_map/all_to_all | solution.py:106
  70.0 18.0 %head.1 = (bf16[4,512,128]{2,1,0:T(8,128)(2,1)}, bf16[4,512,32]{2,1,0:T(8,128)(2,1)}, f32[4,512,512]{2,1,0:T(8,128)}, f32[32,1,128]{2,1,0:T(1,128)}, f32[256,512...) custom-call(f32[4,3]{1,0:T(4,128)} %fusion.1.same_ref, f32[32,1,128]{2,1,0:T(1,128)} %copy-done.6, ...), custom_call_target="tpu_custom_call" | custom-call | tf_op jit(solution)/shard_map/head/pallas_call | solution.py:426
  88.0 10.2 %all_to_all.15.stats3_ref = f32[32,1,128]{2,1,0:T(1,128)} all-to-all(f32[32,1,128]{2,1,0:T(1,128)} %get-tuple-element.51), channel_id=1, replica_groups=mesh['tm'=16,'src'=2] {'tm','src'}, dimensions={0} | all-to-all | bytes 32768 | tf_op jit(solution)/shard_map/all_to_all | solution.py:106
  98.2 5.6 %edges.1 = (bf16[4,128,512]{2,1,0:T(8,128)(2,1)}, bf16[4,128,512]{2,1,0:T(8,128)(2,1)}) custom-call(f32[32,1,128]{2,1,0:T(1,128)} %copy-done.6, f32[32,1,128]{2,1,0:T(1,128)} %all_to_all.15.stats3_ref, f32[4,4,32,128]{3,2,1,0:T(8,128)} %and_select_fusion.sel_ref, f32[4,512,512]{2,1,0:T(8,128)} %get-tuple-element.45.d_ref, ...), custom_call_target="tpu_custom_call" | custom-call | tf_op jit(solution)/shard_map/edges/pallas_call | solution.py:485
  103.8 2.0 %collective-permute-start.10 = (bf16[4,128,512]{2,1,0:T(8,128)(2,1)}, bf16[4,128,512]{2,1,0:T(8,128)(2,1)S(1)}, u32[]{:S(2)}, u32[]{:S(2)}) collective-permute-start(bf16[4,128,512]{2,1,0:T(8,128)(2,1)} %get-tuple-element.53), channel_id=1, source_target_pairs={{0,1},{1,2},{2,3},{3,4},{4,5},{5,6},{6,7},{7,8},{8,9},{9,10},{10,1... | collective-permute-start | bytes 1572872 | tf_op jit(solution)/shard_map/ppermute | solution.py:791
  105.8 1.6 collective-permute-start.11
  107.5 2.5 %collective-permute-done.11.hi_ref = bf16[4,128,512]{2,1,0:T(8,128)(2,1)S(1)} collective-permute-done((bf16[4,128,512]{2,1,0:T(8,128)(2,1)}, bf16[4,128,512]{2,1,0:T(8,128)(2,1)S(1)}, u32[]{:S(2)}, u32[]{:S(2)}) %collective-permute-start.11) | collective-permute-done | bytes 524320 | tf_op jit(solution)/shard_map/ppermute | solution.py:792
  110.8 12.3 %input_grad.1 = (bf16[4,512,128]{2,1,0:T(8,128)(2,1)}, f32[128,512]{1,0:T(8,128)}, f32[8,512]{1,0:T(8,128)}) custom-call(f32[4,3]{1,0:T(4,128)} %fusion.1.same_ref, f32[32,1,128]{2,1,0:T(1,128)} %copy-done.7, f32[32,1,128]{2,1,0:T(1,128)} %copy-done.6, f32[32,1,128]{2,1,0:T(1,128)} %all_to_all.15.stats3_ref, f32[4,4,32,128]{3,2,1,0:T(8,128)} %and_select_fusion.sel_ref, ...), custom_call_target="tpu_custom_call" | custom-call | tf_op jit(solution)/shard_map/input_grad/pallas_call | solution.py:579
  123.1 2.9 %pack.1 = (f32[1408,128]{1,0:T(8,128)}, bf16[1408,128]{1,0:T(8,128)(2,1)}) custom-call(s32[340]{0:T(512)} %get-tuple-element.103.pos_ref, f32[128,512]{1,0:T(8,128)} %get-tuple-element.57.g_in, f32[256,512]{1,0:T(8,128)} %get-tuple-element.58.g_rs, f32[128,1024]{1,0:T(8,128)} %get-tuple-element.59.g_mask, f32[32,1024]{1,0:T(8,128)} %get-tuple-element.60.g_dec, ...), custom_call_target="tpu_custom_call" | custom-call | tf_op jit(solution)/shard_map/pack/pallas_call | solution.py:637
  126.0 10.1 %collective-permute-start.13 = (bf16[1408,128]{1,0:T(8,128)(2,1)}, bf16[1408,128]{1,0:T(8,128)(2,1)S(1)}, u32[]{:S(2)}, u32[]{:S(2)}) collective-permute-start(bf16[1408,128]{1,0:T(8,128)(2,1)} %get-tuple-element.64), channel_id=1, source_target_pairs={{0,1},{1,0},{2,3},{3,2},{4,5},{5,4},{6,7},{7,6},{8,9},{9,8},{10,11... | collective-permute-start | bytes 1081352 | tf_op jit(solution)/shard_map/ppermute | solution.py:82
  138.3 2.0 %fold.2 = (f32[352,128]{1,0:T(8,128)}, bf16[352,128]{1,0:T(8,128)(2,1)}, bf16[352,128]{1,0:T(8,128)(2,1)}, bf16[352,128]{1,0:T(8,128)(2,1)}) custom-call(f32[1408,128]{1,0:T(8,128)} %get-tuple-element.63.refs_0_, bf16[1408,128]{1,0:T(8,128)(2,1)} %copy-done.4), custom_call_target="tpu_custom_call" | custom-call | tf_op jit(solution)/shard_map/fold/pallas_call | solution.py:671
  142.2 1.6 collective-permute-start.16
  144.4 1.5 collective-permute-done.14.refs_1_
  145.9 1.9 %collective-permute-done.16.refs_3_ = bf16[352,128]{1,0:T(8,128)(2,1)S(1)} collective-permute-done((bf16[352,128]{1,0:T(8,128)(2,1)}, bf16[352,128]{1,0:T(8,128)(2,1)S(1)}, u32[]{:S(2)}, u32[]{:S(2)}) %collective-permute-start.16) | collective-permute-done | bytes 90144 | tf_op jit(solution)/shard_map/ppermute | solution.py:82
  148.5 1.7 %fold.3 = (f32[88,128]{1,0:T(8,128)}, bf16[88,128]{1,0:T(8,128)(2,1)}, bf16[88,128]{1,0:T(8,128)(2,1)}, bf16[88,128]{1,0:T(8,128)(2,1)}) custom-call(f32[352,128]{1,0:T(8,128)} %get-tuple-element.65.refs_0_, bf16[352,128]{1,0:T(8,128)(2,1)} %copy-done.10, bf16[352,128]{1,0:T(8,128)(2,1)} %copy-done.11, bf16[352,128]{1,0:T(8,128)(2,1)} %copy-done.12), custom_call_target="tpu_custom_call" | custom-call | tf_op jit(solution)/shard_map/fold/pallas_call | solution.py:671
  150.2 1.7 %collective-permute-start.17 = (bf16[88,128]{1,0:T(8,128)(2,1)}, bf16[88,128]{1,0:T(8,128)(2,1)S(1)}, u32[]{:S(2)}, u32[]{:S(2)}) collective-permute-start(bf16[88,128]{1,0:T(8,128)(2,1)} %get-tuple-element.70), channel_id=1, source_target_pairs={{0,8},{1,9},{2,10},{3,11},{4,12},{5,13},{6,14},{7,15},{8,0},{9,1},... | collective-permute-start | bytes 67592 | tf_op jit(solution)/shard_map/ppermute | solution.py:82
  152.5 2.1 %collective-permute-start.19 = (bf16[88,128]{1,0:T(8,128)(2,1)}, bf16[88,128]{1,0:T(8,128)(2,1)S(1)}, u32[]{:S(2)}, u32[]{:S(2)}) collective-permute-start(bf16[88,128]{1,0:T(8,128)(2,1)} %get-tuple-element.72), channel_id=1, source_target_pairs={{0,24},{1,25},{2,26},{3,27},{4,28},{5,29},{6,30},{7,31},{8,16},{9,... | collective-permute-start | bytes 67592 | tf_op jit(solution)/shard_map/ppermute | solution.py:82
  155.3 1.6 collective-permute-done.18.refs_2_
  156.8 1.5 collective-permute-done.19.refs_3_
  158.9 2.3 %adam.1 = (f32[11,1024]{1,0:T(8,128)}, f32[11,1024]{1,0:T(8,128)}, f32[11,1024]{1,0:T(8,128)}) custom-call(s32[1]{0:T(128)} %bitcast.4.count_ref, f32[88,128]{1,0:T(8,128)} %get-tuple-element.69.refs_0_, bf16[88,128]{1,0:T(8,128)(2,1)} %copy-done.13, bf16[88,128]{1,0:T(8,128)(2,1)} %copy-done.14, bf16[88,128]{1,0:T(8,128)(2,1)} %copy-done.15, ...), custom_call_target="tpu_custom_call" | custom-call | tf_op jit(solution)/shard_map/adam/pallas_call | solution.py:707
  (92 shorter events, 23.9 us)
Async XLA Ops:
  2.1 17.0 %collective-permute-start.2 = (bf16[88,128]{1,0:T(8,128)(2,1)}, bf16[88,128]{1,0:T(8,128)(2,1)S(1)}, u32[]{:S(2)}, u32[]{:S(2)}) collective-permute-start(bf16[88,128]{1,0:T(8,128)(2,1)} %to_tiles.1), channel_id=1, source_target_pairs={{0,24},{1,25},{2,26},{3,27},{4,28},{5,29},{6,30},{7,31},{8,16},{9,... | collective-permute-start | bytes 67592 | tf_op jit(solution)/shard_map/ppermute | solution.py:82
  7.1 13.3 %collective-permute-start.1 = (bf16[88,128]{1,0:T(8,128)(2,1)}, bf16[88,128]{1,0:T(8,128)(2,1)S(1)}, u32[]{:S(2)}, u32[]{:S(2)}) collective-permute-start(bf16[88,128]{1,0:T(8,128)(2,1)} %to_tiles.1), channel_id=1, source_target_pairs={{0,16},{1,17},{2,18},{3,19},{4,20},{5,21},{6,22},{7,23},{8,24},{9,... | collective-permute-start | bytes 67592 | tf_op jit(solution)/shard_map/ppermute | solution.py:82
  7.1 13.3 %collective-permute-start = (bf16[88,128]{1,0:T(8,128)(2,1)}, bf16[88,128]{1,0:T(8,128)(2,1)S(1)}, u32[]{:S(2)}, u32[]{:S(2)}) collective-permute-start(bf16[88,128]{1,0:T(8,128)(2,1)} %to_tiles.1), channel_id=1, source_target_pairs={{0,8},{1,9},{2,10},{3,11},{4,12},{5,13},{6,14},{7,15},{8,0},{9,1},... | collective-permute-start | bytes 67592 | tf_op jit(solution)/shard_map/ppermute | solution.py:82
  8.7 36.6 %collective-permute-start.8 = (bf16[4,128,128]{2,1,0:T(8,128)(2,1)S(1)}, bf16[4,128,128]{2,1,0:T(8,128)(2,1)S(1)}, u32[]{:S(2)}, u32[]{:S(2)}) collective-permute-start(bf16[4,128,128]{2,1,0:T(8,128)(2,1)S(1)} %get-tuple-element.98), channel_id=1, source_target_pairs={{1,0},{2,1},{3,2},{4,3},{5,4},{6,5},{7,6},{8,7},{9,8},{10,9},{11,1... | collective-permute-start | bytes 393224 | tf_op jit(solution)/shard_map/ppermute | solution.py:731
  10.0 35.3 %collective-permute-start.7 = (bf16[4,128,128]{2,1,0:T(8,128)(2,1)S(1)}, bf16[4,128,128]{2,1,0:T(8,128)(2,1)S(1)}, u32[]{:S(2)}, u32[]{:S(2)}) collective-permute-start(bf16[4,128,128]{2,1,0:T(8,128)(2,1)S(1)} %get-tuple-element.99), channel_id=1, source_target_pairs={{0,1},{1,2},{2,3},{3,4},{4,5},{5,6},{6,7},{7,8},{8,9},{9,10},{10,1... | collective-permute-start | bytes 393224 | tf_op jit(solution)/shard_map/ppermute | solution.py:730
  19.1 26.1 %collective-permute-start.9 = (bf16[4,512,16]{2,1,0:T(8,128)(2,1)S(1)}, bf16[4,512,16]{2,1,0:T(8,128)(2,1)S(1)}, u32[]{:S(2)}, u32[]{:S(2)}) collective-permute-start(bf16[4,512,16]{2,1,0:T(8,128)(2,1)S(1)} %bitcast.9), channel_id=1, source_target_pairs={{0,1},{1,0},{2,3},{3,2},{4,5},{5,4},{6,7},{7,6},{8,9},{9,8},{10,11... | collective-permute-start | bytes 196616 | tf_op jit(solution)/shard_map/ppermute | solution.py:736
  21.2 12.5 %collective-permute-start.5 = (bf16[352,128]{1,0:T(8,128)(2,1)S(1)}, bf16[352,128]{1,0:T(8,128)(2,1)S(1)}, u32[]{:S(2)}, u32[]{:S(2)}) collective-permute-start(bf16[352,128]{1,0:T(8,128)(2,1)S(1)} %pad_maximum_fusion.1), channel_id=1, source_target_pairs={{0,6},{1,7},{2,4},{3,5},{4,2},{5,3},{6,0},{7,1},{8,14},{9,15},{10,... | collective-permute-start | bytes 270344 | tf_op jit(solution)/shard_map/ppermute | solution.py:82
  24.6 4.5 %collective-permute-start.3 = (bf16[352,128]{1,0:T(8,128)(2,1)S(1)}, bf16[352,128]{1,0:T(8,128)(2,1)S(1)}, u32[]{:S(2)}, u32[]{:S(2)}) collective-permute-start(bf16[352,128]{1,0:T(8,128)(2,1)S(1)} %pad_maximum_fusion.1), channel_id=1, source_target_pairs={{0,2},{1,3},{2,0},{3,1},{4,6},{5,7},{6,4},{7,5},{8,10},{9,11},{10,... | collective-permute-start | bytes 270344 | tf_op jit(solution)/shard_map/ppermute | solution.py:82
  29.2 4.5 %collective-permute-start.4 = (bf16[352,128]{1,0:T(8,128)(2,1)S(1)}, bf16[352,128]{1,0:T(8,128)(2,1)S(1)}, u32[]{:S(2)}, u32[]{:S(2)}) collective-permute-start(bf16[352,128]{1,0:T(8,128)(2,1)S(1)} %pad_maximum_fusion.1), channel_id=1, source_target_pairs={{0,4},{1,5},{2,6},{3,7},{4,0},{5,1},{6,2},{7,3},{8,12},{9,13},{10,... | collective-permute-start | bytes 270344 | tf_op jit(solution)/shard_map/ppermute | solution.py:82
  33.7 2.3 %copy-start.3 = (bf16[1408,128]{1,0:T(8,128)(2,1)}, bf16[1408,128]{1,0:T(8,128)(2,1)S(1)}, u32[]{:S(2)}) copy-start(bf16[1408,128]{1,0:T(8,128)(2,1)S(1)} %constant_dynamic-update-slice_fusion.own_ref) | copy-start | bytes 1081348
  33.7 2.2 %collective-permute-start.6 = (bf16[1408,128]{1,0:T(8,128)(2,1)S(1)}, bf16[1408,128]{1,0:T(8,128)(2,1)S(1)}, u32[]{:S(2)}, u32[]{:S(2)}) collective-permute-start(bf16[1408,128]{1,0:T(8,128)(2,1)S(1)} %constant_dynamic-update-slice_fusion.own_ref), channel_id=1, source_target_pairs={{0,1},{1,0},{2,3},{3,2},{4,5},{5,4},{6,7},{7,6},{8,9},{9,8},{10,11... | collective-permute-start | bytes 1081352 | tf_op jit(solution)/shard_map/ppermute | solution.py:82
  40.8 11.5 %all-to-all-start = ((f32[32,1,128]{2,1,0:T(1,128)}), f32[32,1,128]{2,1,0:T(1,128)S(1)}, u32[]{:S(2)}, u32[]{:S(2)}) async-start(f32[32,1,128]{2,1,0:T(1,128)} %get-tuple-element.41), calls=%async_computation | async-start | bytes 32768 | tf_op jit(solution)/shard_map/all_to_all | solution.py:106
  45.3 7.0 %copy-start.8 = (bf16[4,128,128]{2,1,0:T(8,128)(2,1)}, bf16[4,128,128]{2,1,0:T(8,128)(2,1)S(1)}, u32[]{:S(2)}) copy-start(bf16[4,128,128]{2,1,0:T(8,128)(2,1)S(1)} %collective-permute-done.8.xa_ref) | copy-start | bytes 393220
  45.3 7.0 %copy-start.9 = (bf16[4,128,128]{2,1,0:T(8,128)(2,1)}, bf16[4,128,128]{2,1,0:T(8,128)(2,1)S(1)}, u32[]{:S(2)}) copy-start(bf16[4,128,128]{2,1,0:T(8,128)(2,1)S(1)} %collective-permute-done.7.xb_ref) | copy-start | bytes 393220
  59.8 9.6 %all-to-all-start.1 = ((f32[32,1,128]{2,1,0:T(1,128)}), f32[32,1,128]{2,1,0:T(1,128)S(1)}, u32[]{:S(2)}, u32[]{:S(2)}) async-start(f32[32,1,128]{2,1,0:T(1,128)} %get-tuple-element.44), calls=%async_computation.1 | async-start | bytes 32768 | tf_op jit(solution)/shard_map/all_to_all | solution.py:106
  103.8 3.7 %collective-permute-start.10 = (bf16[4,128,512]{2,1,0:T(8,128)(2,1)}, bf16[4,128,512]{2,1,0:T(8,128)(2,1)S(1)}, u32[]{:S(2)}, u32[]{:S(2)}) collective-permute-start(bf16[4,128,512]{2,1,0:T(8,128)(2,1)} %get-tuple-element.53), channel_id=1, source_target_pairs={{0,1},{1,2},{2,3},{3,4},{4,5},{5,6},{6,7},{7,8},{8,9},{9,10},{10,1... | collective-permute-start | bytes 1572872 | tf_op jit(solution)/shard_map/ppermute | solution.py:791
  105.8 30.3 %copy-start = (bf16[4,512,32]{2,1,0:T(8,128)(2,1)S(1)}, bf16[4,512,32]{2,1,0:T(8,128)(2,1)}, u32[]{:S(2)}) copy-start(bf16[4,512,32]{2,1,0:T(8,128)(2,1)} %get-tuple-element.56) | copy-start | bytes 393220
  105.8 4.2 %collective-permute-start.11 = (bf16[4,128,512]{2,1,0:T(8,128)(2,1)}, bf16[4,128,512]{2,1,0:T(8,128)(2,1)S(1)}, u32[]{:S(2)}, u32[]{:S(2)}) collective-permute-start(bf16[4,128,512]{2,1,0:T(8,128)(2,1)} %get-tuple-element.54), channel_id=1, source_target_pairs={{1,0},{2,1},{3,2},{4,3},{5,4},{6,5},{7,6},{8,7},{9,8},{10,9},{11,1... | collective-permute-start | bytes 1572872 | tf_op jit(solution)/shard_map/ppermute | solution.py:792
  107.5 2.5 %copy-start.1 = (bf16[4,128,512]{2,1,0:T(8,128)(2,1)}, bf16[4,128,512]{2,1,0:T(8,128)(2,1)S(1)}, u32[]{:S(2)}) copy-start(bf16[4,128,512]{2,1,0:T(8,128)(2,1)S(1)} %collective-permute-done.10.lo_ref) | copy-start | bytes 1572868
  110.0 0.8 copy-start.2
  126.0 11.6 %collective-permute-start.13 = (bf16[1408,128]{1,0:T(8,128)(2,1)}, bf16[1408,128]{1,0:T(8,128)(2,1)S(1)}, u32[]{:S(2)}, u32[]{:S(2)}) collective-permute-start(bf16[1408,128]{1,0:T(8,128)(2,1)} %get-tuple-element.64), channel_id=1, source_target_pairs={{0,1},{1,0},{2,3},{3,2},{4,5},{5,4},{6,7},{7,6},{8,9},{9,8},{10,11... | collective-permute-start | bytes 1081352 | tf_op jit(solution)/shard_map/ppermute | solution.py:82
  136.3 7.5 %collective-permute-start.12 = (bf16[4,512,16]{2,1,0:T(8,128)(2,1)S(1)}, bf16[4,512,16]{2,1,0:T(8,128)(2,1)S(1)}, u32[]{:S(2)}, u32[]{:S(2)}) collective-permute-start(bf16[4,512,16]{2,1,0:T(8,128)(2,1)S(1)} %broadcast_select_fusion.2), channel_id=1, source_target_pairs={{0,1},{1,0},{2,3},{3,2},{4,5},{5,4},{6,7},{7,6},{8,9},{9,8},{10,11... | collective-permute-start | bytes 196616 | tf_op jit(solution)/shard_map/ppermute | solution.py:785
  140.3 5.6 %collective-permute-start.14 = (bf16[352,128]{1,0:T(8,128)(2,1)}, bf16[352,128]{1,0:T(8,128)(2,1)S(1)}, u32[]{:S(2)}, u32[]{:S(2)}) collective-permute-start(bf16[352,128]{1,0:T(8,128)(2,1)} %get-tuple-element.66), channel_id=1, source_target_pairs={{0,2},{1,3},{2,0},{3,1},{4,6},{5,7},{6,4},{7,5},{8,10},{9,11},{10,... | collective-permute-start | bytes 270344 | tf_op jit(solution)/shard_map/ppermute | solution.py:82
  140.8 5.1 %collective-permute-start.15 = (bf16[352,128]{1,0:T(8,128)(2,1)}, bf16[352,128]{1,0:T(8,128)(2,1)S(1)}, u32[]{:S(2)}, u32[]{:S(2)}) collective-permute-start(bf16[352,128]{1,0:T(8,128)(2,1)} %get-tuple-element.67), channel_id=1, source_target_pairs={{0,4},{1,5},{2,6},{3,7},{4,0},{5,1},{6,2},{7,3},{8,12},{9,13},{10,... | collective-permute-start | bytes 270344 | tf_op jit(solution)/shard_map/ppermute | solution.py:82
  142.2 5.6 %collective-permute-start.16 = (bf16[352,128]{1,0:T(8,128)(2,1)}, bf16[352,128]{1,0:T(8,128)(2,1)S(1)}, u32[]{:S(2)}, u32[]{:S(2)}) collective-permute-start(bf16[352,128]{1,0:T(8,128)(2,1)} %get-tuple-element.68), channel_id=1, source_target_pairs={{0,6},{1,7},{2,4},{3,5},{4,2},{5,3},{6,0},{7,1},{8,14},{9,15},{10,... | collective-permute-start | bytes 270344 | tf_op jit(solution)/shard_map/ppermute | solution.py:82
  145.9 1.9 %copy-start.10 = (bf16[352,128]{1,0:T(8,128)(2,1)}, bf16[352,128]{1,0:T(8,128)(2,1)S(1)}, u32[]{:S(2)}) copy-start(bf16[352,128]{1,0:T(8,128)(2,1)S(1)} %collective-permute-done.14.refs_1_) | copy-start | bytes 270340
  145.9 1.9 %copy-start.11 = (bf16[352,128]{1,0:T(8,128)(2,1)}, bf16[352,128]{1,0:T(8,128)(2,1)S(1)}, u32[]{:S(2)}) copy-start(bf16[352,128]{1,0:T(8,128)(2,1)S(1)} %collective-permute-done.15.refs_2_) | copy-start | bytes 270340
  150.2 5.1 %collective-permute-start.17 = (bf16[88,128]{1,0:T(8,128)(2,1)}, bf16[88,128]{1,0:T(8,128)(2,1)S(1)}, u32[]{:S(2)}, u32[]{:S(2)}) collective-permute-start(bf16[88,128]{1,0:T(8,128)(2,1)} %get-tuple-element.70), channel_id=1, source_target_pairs={{0,8},{1,9},{2,10},{3,11},{4,12},{5,13},{6,14},{7,15},{8,0},{9,1},... | collective-permute-start | bytes 67592 | tf_op jit(solution)/shard_map/ppermute | solution.py:82
  151.9 4.9 %collective-permute-start.18 = (bf16[88,128]{1,0:T(8,128)(2,1)}, bf16[88,128]{1,0:T(8,128)(2,1)S(1)}, u32[]{:S(2)}, u32[]{:S(2)}) collective-permute-start(bf16[88,128]{1,0:T(8,128)(2,1)} %get-tuple-element.71), channel_id=1, source_target_pairs={{0,16},{1,17},{2,18},{3,19},{4,20},{5,21},{6,22},{7,23},{8,24},{9,... | collective-permute-start | bytes 67592 | tf_op jit(solution)/shard_map/ppermute | solution.py:82
  152.5 5.8 %collective-permute-start.19 = (bf16[88,128]{1,0:T(8,128)(2,1)}, bf16[88,128]{1,0:T(8,128)(2,1)S(1)}, u32[]{:S(2)}, u32[]{:S(2)}) collective-permute-start(bf16[88,128]{1,0:T(8,128)(2,1)} %get-tuple-element.72), channel_id=1, source_target_pairs={{0,24},{1,25},{2,26},{3,27},{4,28},{5,29},{6,30},{7,31},{8,16},{9,... | collective-permute-start | bytes 67592 | tf_op jit(solution)/shard_map/ppermute | solution.py:82
  155.2 3.1 %copy-start.13 = (bf16[88,128]{1,0:T(8,128)(2,1)}, bf16[88,128]{1,0:T(8,128)(2,1)S(1)}, u32[]{:S(2)}) copy-start(bf16[88,128]{1,0:T(8,128)(2,1)S(1)} %collective-permute-done.17.refs_1_) | copy-start | bytes 67588
  156.8 1.5 copy-start.14
  (6 other events, 3.9 us)

commit v2 on v1

v2 whole, which is shorter than its diff:
```python
import functools

import jax
import jax.numpy as jnp
from jax import lax
from jax.experimental import pallas as pl
from jax.experimental.pallas import tpu as pltpu
from jax.sharding import PartitionSpec as P

N = 512
L = 16
B = 128
SC = 128
HW = 512
C = 2
DIL = 128
ROW = 1024
SEGS = 8
MICRO = 4
STEP = 10
NCH = 340
BLK = 256
KINDS = 8
CHUNK = 16

norm_eps = 1e-05
adam_eps = 1e-08
beta_one = 0.9
beta_two = 0.999
learn_rate = 0.2
weight_decay = 0.01

AXES = ("tm", "src")
f32 = jnp.float32
bf16 = jnp.bfloat16
MIB = 1024 * 1024
DEPTH_MIB = HEAD_MIB = INPUT_MIB = 52

R_IN, R_RES, R_SKIP, R_MASK, R_DEC, R_VEC = 0, 512, 1024, 1536, 2560, 2688
ROWS_ALL = 2720


def mm(a, b):
    return lax.dot_general(a, b, (((1,), (0,)), ((), ())), preferred_element_type=f32)


def mm_t(a, b):
    return lax.dot_general(a, b, (((1,), (1,)), ((), ())), preferred_element_type=f32)


def mm_rows(a, b):
    return lax.dot_general(a, b, (((0,), (0,)), ((), ())), preferred_element_type=f32)


def sigmoid(v):
    return 0.5 * jnp.tanh(0.5 * v) + 0.5


def vmem():
    return pl.BlockSpec(memory_space=pltpu.VMEM)


def smem():
    return pl.BlockSpec(memory_space=pltpu.SMEM)


def stages(n_dev):
    bits = n_dev.bit_length() - 1
    groups = []
    hi = bits - 1
    while hi >= 1:
        lo = max(1, hi - 1)
        groups.append(tuple(range(lo, hi + 1)))
        hi = lo - 1
    groups.append((0,))
    return groups


def spread(bits, k):
    return sum(((k >> j) & 1) << b for j, b in enumerate(bits))


def swap(value, mask, n_dev):
    return lax.ppermute(value, AXES, [(i, i ^ mask) for i in range(n_dev)])


def gather_tiles(tiles, n_dev, *late):
    parts = [tiles]
    for bits in stages(n_dev)[:-1]:
        z = parts[0] if len(parts) == 1 else jnp.concatenate(parts, axis=0)
        parts = [z] + [swap(z, spread(bits, k), n_dev) for k in range(1, 1 << len(bits))]
    parts, late = lax.optimization_barrier((parts, late))
    return parts + [swap(z, 1, n_dev) for z in parts], late


def relative_block(owner, me, n_dev):
    q = owner ^ me
    index = jnp.zeros_like(q)
    size = 1
    for bits in stages(n_dev):
        digit = sum(((q >> b) & 1) << j for j, b in enumerate(bits))
        index = index + digit * size
        size = size << len(bits)
    return index


def share_sums(rows, n_dev):
    return lax.all_to_all(rows, AXES, 0, 0, tiled=True)


def tile_kernel(m_ref, out_ref, buf):
    slots = m_ref.shape[0]
    for j in range(8):
        buf[pl.ds(j, slots, stride=8), :] = m_ref[:, 128 * j : 128 * j + 128]
    out_ref[...] = buf[...].astype(bf16)


def to_tiles(master):
    slots = master.shape[0]
    return pl.pallas_call(
        tile_kernel,
        out_shape=jax.ShapeDtypeStruct((slots * 8, 128), bf16),
        in_specs=[vmem()],
        out_specs=vmem(),
        scratch_shapes=[pltpu.VMEM((slots * 8, 128), f32)],
        compiler_params=pltpu.CompilerParams(vmem_limit_bytes=4 * MIB),
        name="to_tiles",
    )(master)


def stat_rows(values, shape):
    lane = lax.broadcasted_iota(jnp.int32, shape, 1)
    row = jnp.zeros(shape, f32)
    for where, v in values.items():
        row = jnp.where(lane == where, v, row)
    return row


def unpack_kernel(n_parts, pos_ref, x_ref, *refs):
    parts, refs = refs[:n_parts], refs[n_parts:]
    w_in, w_rs, w_mask, w_dect, vec, stats, g, t, wd = refs
    size = parts[0].shape[0]
    for k, part in enumerate(parts):
        g[k * size : (k + 1) * size, :] = part[...].astype(f32)
    for i in range(NCH):
        start = pl.multiple_of(pos_ref[i] * 8, 8)
        t[8 * i : 8 * i + 8, :] = g[pl.ds(start, 8), :]
    for k in range(4):
        cols = slice(128 * k, 128 * k + 128)
        w_in[:, cols] = t[pl.ds(R_IN + k, 128, stride=4), :].astype(bf16)
        for c in range(C):
            w_mask[:, 512 * c + 128 * k : 512 * c + 128 * k + 128] = t[
                pl.ds(R_MASK + 512 * c + k, 128, stride=4), :
            ].astype(bf16)
        vec[:, cols] = t[pl.ds(R_VEC + k, 8, stride=4), :]
    w_rs[:, 0:128] = t[R_RES : R_RES + 512, :].astype(bf16)
    w_rs[:, 128:256] = t[R_SKIP : R_SKIP + 512, :].astype(bf16)
    part = lax.broadcasted_iota(jnp.int32, (64, 128), 1) // L
    for s in range(8):
        for c in range(C):
            rows = t[R_DEC + 64 * c : R_DEC + 64 * c + 64, :]
            rows = pltpu.roll(rows, (-L * s) % 128, 1)
            wd[pl.ds(512 * c + s, 64, stride=8), :] = jnp.where(part == 0, rows, 0.0)
    w_dect[...] = wd[...].T[0:L, :].astype(bf16)
    micro, frames, _ = x_ref.shape
    nb = frames // BLK
    sums = {}
    for m in range(micro):
        for b in range(nb):
            a = mm(x_ref[m, b * BLK : (b + 1) * BLK, :], w_in[...])
            u = a * sigmoid(a)
            first = jnp.sum(jnp.sum(u, axis=0, keepdims=True), axis=1, keepdims=True)
            second = jnp.sum(jnp.sum(u * u, axis=0, keepdims=True), axis=1, keepdims=True)
            sums[(m * nb + b) * KINDS] = first
            sums[(m * nb + b) * KINDS + 1] = second
    row = stat_rows(sums, (1, 128))
    stats[...] = jnp.broadcast_to(row[None], stats.shape)


def unpack(pos, parts, feats, n_dev):
    outs = (
        jax.ShapeDtypeStruct((B, HW), bf16),
        jax.ShapeDtypeStruct((HW, B + SC), bf16),
        jax.ShapeDtypeStruct((SC, C * N), bf16),
        jax.ShapeDtypeStruct((L, C * N), bf16),
        jax.ShapeDtypeStruct((8, HW), f32),
        jax.ShapeDtypeStruct((n_dev, 1, 128), f32),
    )
    return pl.pallas_call(
        functools.partial(unpack_kernel, len(parts)),
        out_shape=outs,
        in_specs=[smem()] + [vmem()] * (1 + len(parts)),
        out_specs=tuple(vmem() for _ in outs),
        scratch_shapes=[
            pltpu.VMEM((len(parts) * parts[0].shape[0], 128), f32),
            pltpu.VMEM((ROWS_ALL, 128), f32),
            pltpu.VMEM((C * N, 128), f32),
        ],
        compiler_params=pltpu.CompilerParams(vmem_limit_bytes=16 * MIB),
        name="unpack",
    )(pos, feats, *parts)


class Segments:
    def __init__(self, seg_ref, me_ref, m, nb, n_dev):
        bounds, total = [], 0
        for k in range(SEGS):
            total = total + seg_ref[m, k]
            bounds.append(total)
        shape = (n_dev, 128)
        lane = lax.broadcasted_iota(jnp.int32, shape, 1)
        start = (lax.broadcasted_iota(jnp.int32, shape, 0) * nb + (lane // KINDS) % nb) * BLK
        ids = jnp.where(lane // (KINDS * nb) == m, 0, SEGS + 1)
        for bound in bounds:
            ids = ids + (start >= bound).astype(jnp.int32)
        self.ids = ids
        self.here, self.inverse = [], []
        for o in range(-1, nb + 1):
            at = (me_ref[0] * nb + o) * BLK
            here, length = jnp.where(at < 0, -1, 0), 0
            for bound in bounds:
                here = here + jnp.where(at >= bound, 1, 0)
            for k in range(SEGS):
                length = length + jnp.where(here == k, seg_ref[m, k], 0)
            self.here.append(here)
            count = jnp.full((1, 1), jnp.maximum(length, 1), jnp.int32).astype(f32) * HW
            self.inverse.append(1.0 / count)
        self.same = [
            jnp.where(p == q, 1.0, 0.0).astype(f32) for p, q in zip(self.here[:-1], self.here[1:])
        ]

    def means(self, stats, kinds):
        lane = lax.broadcasted_iota(jnp.int32, (1, 128), 1) % KINDS
        rows = [
            jnp.sum(jnp.where(self.ids == here, stats, 0.0), axis=0, keepdims=True) * inverse
            for here, inverse in zip(self.here, self.inverse)
        ]
        t = jnp.concatenate(rows, axis=0)
        cols = [jnp.sum(jnp.where(lane == k, t, 0.0), axis=1, keepdims=True) for k in range(kinds)]
        return [[c[o : o + 1, :] for o in range(len(rows))] for c in cols]

    def norm(self, stats):
        mean, second = self.means(stats, 2)
        return mean, [lax.rsqrt(q - p * p + norm_eps) for p, q in zip(mean, second)]

    def taps(self, vec, h):
        k0, k2 = vec[4:5, :], vec[6:7, :]
        lo = k0 * self.same[h // 2 - 1] if h % 2 == 0 else k0
        hi = k2 if h % 2 == 0 else k2 * self.same[h // 2]
        return lo, hi


def depth_kernel(
    me_ref, seg_ref, stats_ref, x_ref, near_ref, far_ref, w_in, vec, d_ref, edge_ref, out_stats, acc
):
    m = pl.program_id(0)
    frames = x_ref.shape[1]
    nb = frames // BLK
    seg = Segments(seg_ref, me_ref, m, nb, stats_ref.shape[0])
    means, factors = seg.norm(stats_ref[:, 0, :])
    g1, b1 = 1.0 + vec[0:1, :], vec[1:2, :]

    def normed(x, o):
        a = mm(x, w_in[...])
        u = a * sigmoid(a)
        scale = factors[o] * g1
        return (u * scale + (b1 - means[o] * scale)).astype(bf16).astype(f32)

    even = me_ref[0] % 2 == 0
    n1 = []
    for h in range(2 * nb + 4):
        if h < 2:
            rows = slice(h * DIL, (h + 1) * DIL)
            x = jnp.where(even, far_ref[0, rows, :], near_ref[0, rows, :])
        elif h < 2 * nb + 2:
            x = x_ref[0, (h - 2) * DIL : (h - 1) * DIL, :]
        else:
            rows = slice((h - 2 * nb - 2) * DIL, (h - 2 * nb - 1) * DIL)
            x = jnp.where(even, near_ref[0, rows, :], far_ref[0, rows, :])
        n1.append(normed(x, h // 2))
    k1, kb = vec[5:6, :], vec[7:8, :]

    def conv(h):
        lo, hi = seg.taps(vec, h)
        return lo * n1[h - 1] + k1 * n1[h] + hi * n1[h + 1] + kb

    edge_ref[0, 0:DIL, :] = conv(1)
    edge_ref[0, DIL : 2 * DIL, :] = conv(2 * nb + 2)
    lane = lax.broadcasted_iota(jnp.int32, (1, 128), 1)
    row = jnp.where(m == 0, jnp.zeros((1, 128), f32), acc[...])
    for b in range(nb):
        first, second = 0.0, 0.0
        for h in (2 * b, 2 * b + 1):
            d = conv(h + 2)
            d_ref[0, h * DIL : (h + 1) * DIL, :] = d
            v = d * sigmoid(d)
            first = first + jnp.sum(v, axis=0, keepdims=True)
            second = second + jnp.sum(v * v, axis=0, keepdims=True)
        at = (m * nb + b) * KINDS
        row = jnp.where(lane == at, jnp.sum(first, axis=1, keepdims=True), row)
        row = jnp.where(lane == at + 1, jnp.sum(second, axis=1, keepdims=True), row)
    acc[...] = row
    out_stats[...] = jnp.broadcast_to(row[None], out_stats.shape)


def per_micro(shape):
    rest = tuple(shape[1:])
    zeros = (0,) * len(rest)
    return pl.BlockSpec((1,) + rest, lambda m: (m,) + zeros)


def whole(shape):
    zeros = (0,) * len(shape)
    return pl.BlockSpec(tuple(shape), lambda m: zeros)


def depth(me, lengths, stats, feats, near, far, w_in, vec):
    micro, frames, _ = feats.shape
    return pl.pallas_call(
        depth_kernel,
        grid=(micro,),
        out_shape=(
            jax.ShapeDtypeStruct((micro, frames, HW), f32),
            jax.ShapeDtypeStruct((micro, 2 * DIL, HW), f32),
            jax.ShapeDtypeStruct(stats.shape, f32),
        ),
        in_specs=[
            smem(),
            smem(),
            whole(stats.shape),
            per_micro(feats.shape),
            pl.BlockSpec((1, BLK, B), lambda m: (m, 0, 0)),
            pl.BlockSpec((1, BLK, B), lambda m: (m, 0, 0)),
            whole(w_in.shape),
            whole(vec.shape),
        ],
        out_specs=(
            per_micro((micro, frames, HW)),
            per_micro((micro, 2 * DIL, HW)),
            whole(stats.shape),
        ),
        scratch_shapes=[pltpu.VMEM((1, 128), f32)],
        compiler_params=pltpu.CompilerParams(vmem_limit_bytes=DEPTH_MIB * MIB),
        name="depth",
    )(me, lengths, stats, feats, near, far, w_in, vec)


def fold_rows(v):
    return functools.reduce(lambda p, q: p + q, [v[i : i + 8, :] for i in range(0, v.shape[0], 8)])


def head_kernel(
    me_ref,
    seg_ref,
    stats_ref,
    d_ref,
    x_ref,
    enc_ref,
    dy_ref,
    own_ref,
    other_ref,
    w_rs,
    w_mask,
    w_dect,
    vec,
    block_ref,
    wave_own_ref,
    wave_other_ref,
    ds_ref,
    out_stats,
    g_rs,
    g_mask,
    g_dec,
    g_vec,
    acc,
    n2_s,
    v_s,
    sd_s,
    q_s,
    gm_s,
    e_s,
    dq_s,
    dn2_s,
):
    m = pl.program_id(0)
    frames = d_ref.shape[1]
    nb = frames // BLK

    @pl.when(m == 0)
    def _():
        g_rs[...] = jnp.zeros_like(g_rs)
        g_mask[...] = jnp.zeros_like(g_mask)
        g_dec[...] = jnp.zeros_like(g_dec)
        g_vec[...] = jnp.zeros_like(g_vec)
        acc[...] = jnp.zeros_like(acc)

    core = me_ref[0] % 2
    seg = Segments(seg_ref, me_ref, m, nb, stats_ref.shape[0])
    means, factors = seg.norm(stats_ref[:, 0, :])
    g1, g2, b1, b2 = 1.0 + vec[0:1, :], 1.0 + vec[2:3, :], vec[1:2, :], vec[3:4, :]
    k1, kb = vec[5:6, :], vec[7:8, :]
    lane = lax.broadcasted_iota(jnp.int32, (1, 128), 1)
    scales = [factors[1 + b] * g2 for b in range(nb)]
    zero = jnp.zeros((8, HW), f32)

    sums = []
    for h in range(2 * nb):
        scale = scales[h // 2]
        shift = b2 - means[1 + h // 2] * scale
        s0 = s1 = c0 = c1 = zero
        for r in range(h * DIL, (h + 1) * DIL, CHUNK):
            rows = slice(r, r + CHUNK)
            d = d_ref[0, rows, :]
            sig = sigmoid(d)
            v = d * sig
            sd = sig + v * (1.0 - sig)
            n2_s[rows, :] = (v * scale + shift).astype(bf16)
            v_s[rows, :] = v
            sd_s[rows, :] = sd
            cv = v * sd
            s0 = s0 + fold_rows(sd)
            s1 = s1 + fold_rows(sd * d)
            c0 = c0 + fold_rows(cv)
            c1 = c1 + fold_rows(cv * d)
        sums.append((s0, s1, c0, c1))

    n2 = n2_s[...]
    ys = mm(n2, w_rs[...])
    block_ref[0] = (x_ref[0].astype(f32) + ys[:, 0:B]).astype(bf16)
    s = ys[:, B : B + SC]
    sg = sigmoid(s)
    z = (s * sg).astype(bf16)
    slope = sg * (1.0 + s * (1.0 - sg))
    dz = jnp.zeros((frames, SC), f32)
    for k, (c, dw_ref, wave_ref) in enumerate(
        ((core, own_ref, wave_own_ref), (1 - core, other_ref, wave_other_ref))
    ):
        cols = pl.ds(pl.multiple_of(c * N, N), N)
        dw = dw_ref[0]
        q_s[k] = mm(z, w_mask[:, cols])
        gm_s[k] = mm_rows(dw, w_dect[:, cols])
        for r in range(0, frames, CHUNK):
            rows = slice(r, r + CHUNK)
            p = sigmoid(q_s[k, rows, :])
            pe = p * enc_ref[0, rows, :].astype(f32)
            e_s[k, rows, :] = pe.astype(bf16)
            dq_s[k, rows, :] = (gm_s[k, rows, :] * (pe - pe * p)).astype(bf16)
        e = e_s[k]
        dq = dq_s[k]
        wave_ref[0] = mm_t(w_dect[:, cols], e).astype(bf16)
        dz = dz + mm_t(dq, w_mask[:, cols])
        g_dec[:, cols] += mm(dw, e)
        g_mask[:, cols] += mm_rows(z, dq)
    ds = (dz * slope).astype(bf16)
    ds_ref[0] = ds
    dys = jnp.concatenate([dy_ref[0], ds], axis=1)
    g_rs[...] += mm_rows(dys, n2)
    dn2_s[...] = mm_t(dys, w_rs[...])

    row = acc[...]
    for b in range(nb):
        mean, factor, scale = means[1 + b], factors[1 + b], scales[b]
        sum_d = sum_dv = zero
        six = [jnp.zeros((1, HW), f32)] * 6
        for h in (2 * b, 2 * b + 1):
            a0 = a1 = zero
            for r in range(h * DIL, (h + 1) * DIL, CHUNK):
                rows = slice(r, r + CHUNK)
                dn2 = dn2_s[rows, :]
                a = dn2 * sd_s[rows, :]
                sum_d = sum_d + fold_rows(dn2)
                sum_dv = sum_dv + fold_rows(dn2 * v_s[rows, :])
                a0 = a0 + fold_rows(a)
                a1 = a1 + fold_rows(a * d_ref[0, rows, :])
            a0, a1, s0, s1, c0, c1 = [
                jnp.sum(p, axis=0, keepdims=True) for p in (a0, a1) + sums[h]
            ]
            lo, hi = seg.taps(vec, h + 2)
            kappa = k1 + lo + hi
            vw = g1 * kappa
            delta = kb + b1 * kappa
            a0, a1 = a0 * scale, a1 * scale
            s0, s1 = s0 * factor, s1 * factor
            c0 = c0 * factor * factor - mean * factor * s0
            c1 = c1 * factor * factor - mean * factor * s1
            new = [vw * a0, vw * s0, vw * c0, a1 - delta * a0, s1 - delta * s0, c1 - delta * c0]
            six = [p0 + p1 for p0, p1 in zip(six, new)]
        sum_d = jnp.sum(sum_d, axis=0, keepdims=True)
        gain = (jnp.sum(sum_dv, axis=0, keepdims=True) - mean * sum_d) * factor
        g_vec[2:3, :] += gain
        g_vec[3:4, :] += sum_d
        for k, val in enumerate([sum_d * g2, gain * g2] + six):
            at = (m * nb + b) * KINDS + k
            row = jnp.where(lane == at, jnp.sum(val, axis=1, keepdims=True), row)
    acc[...] = row
    out_stats[...] = jnp.broadcast_to(row[None], out_stats.shape)


def head(me, lengths, stats, d, feats, enc, dy, own, other, w_rs, w_mask, w_dect, vec):
    micro, frames, _ = feats.shape
    outs = (
        (feats.shape, bf16, True),
        ((micro, L, frames), bf16, True),
        ((micro, L, frames), bf16, True),
        ((micro, frames, SC), bf16, True),
        (stats.shape, f32, False),
        ((B + SC, HW), f32, False),
        ((SC, C * N), f32, False),
        ((L, C * N), f32, False),
        ((8, HW), f32, False),
    )

    def each(shape):
        zeros = (0,) * (len(shape) - 1)
        return pl.BlockSpec((1,) + tuple(shape[1:]), lambda m, me_ref: (m,) + zeros)

    def once(shape):
        zeros = (0,) * len(shape)
        return pl.BlockSpec(tuple(shape), lambda m, me_ref: zeros)

    ours = pl.BlockSpec((1, L, frames), lambda m, me_ref: (m, 0, me_ref[0] % 2))
    return pl.pallas_call(
        head_kernel,
        grid_spec=pltpu.PrefetchScalarGridSpec(
            num_scalar_prefetch=1,
            grid=(micro,),
            in_specs=[
                smem(),
                once(stats.shape),
                each(d.shape),
                each(feats.shape),
                each(enc.shape),
                each(dy.shape),
                ours,
                ours,
                once(w_rs.shape),
                once(w_mask.shape),
                once(w_dect.shape),
                once(vec.shape),
            ],
            out_specs=tuple(each(s) if per else once(s) for s, _, per in outs),
            scratch_shapes=[
                pltpu.VMEM((1, 128), f32),
                pltpu.VMEM((frames, HW), bf16),
                pltpu.VMEM((frames, HW), f32),
                pltpu.VMEM((frames, HW), f32),
                pltpu.VMEM((C, frames, N), f32),
                pltpu.VMEM((C, frames, N), f32),
                pltpu.VMEM((C, frames, N), bf16),
                pltpu.VMEM((C, frames, N), bf16),
                pltpu.VMEM((frames, HW), f32),
            ],
        ),
        out_shape=tuple(jax.ShapeDtypeStruct(s, t) for s, t, _ in outs),
        compiler_params=pltpu.CompilerParams(vmem_limit_bytes=HEAD_MIB * MIB),
        name="head",
    )(me, lengths, stats, d, feats, enc, dy, own, other, w_rs, w_mask, w_dect, vec)


def back_means(seg, stats):
    v = seg.means(stats, KINDS)
    p2, q2 = v[0], v[1]
    p1 = [a - p * b - q * c for a, p, b, q, c in zip(v[2], p2, v[3], q2, v[4])]
    q1 = [a - p * b - q * c for a, p, b, q, c in zip(v[5], p2, v[6], q2, v[7])]
    return p2, q2, p1, q1


def depth_grad(d, dn2, mean, factor, g2, p2, q2):
    sig = sigmoid(d)
    v = d * sig
    sd = sig + v * (1.0 - sig)
    scale = factor * g2
    slope = factor * factor * q2
    shift = factor * p2 - slope * mean
    return (sd * (dn2 * scale - v * slope - shift)).astype(bf16)


def input_kernel(
    me_ref,
    seg_ref,
    stats1_ref,
    stats2_ref,
    stats3_ref,
    d_ref,
    edge_ref,
    x_ref,
    dy_ref,
    dy_near,
    dy_far,
    ds_ref,
    ds_near,
    ds_far,
    w_in,
    w_rs,
    vec,
    feats_ref,
    g_in,
    g_vec,
):
    m = pl.program_id(0)
    frames = d_ref.shape[1]
    nb = frames // BLK

    @pl.when(m == 0)
    def _():
        g_in[...] = jnp.zeros_like(g_in)
        g_vec[...] = jnp.zeros_like(g_vec)

    seg = Segments(seg_ref, me_ref, m, nb, stats1_ref.shape[0])
    mean1, factor1 = seg.norm(stats1_ref[:, 0, :])
    mean2, factor2 = seg.norm(stats2_ref[:, 0, :])
    p2, q2, p1, q1 = back_means(seg, stats3_ref[:, 0, :])
    g1, g2, b1 = 1.0 + vec[0:1, :], 1.0 + vec[2:3, :], vec[1:2, :]
    k0, k1, k2 = vec[4:5, :], vec[5:6, :], vec[6:7, :]
    even = me_ref[0] % 2 == 0
    dd = []
    for h in range(1, 2 * nb + 3):
        o = h // 2
        if h == 1:
            d = edge_ref[0, 0:DIL, :]
            dy = jnp.where(even, dy_far[0], dy_near[0])
            ds = jnp.where(even, ds_far[0], ds_near[0])
        elif h == 2 * nb + 2:
            d = edge_ref[0, DIL : 2 * DIL, :]
            dy = jnp.where(even, dy_near[0], dy_far[0])
            ds = jnp.where(even, ds_near[0], ds_far[0])
        else:
            rows = slice((h - 2) * DIL, (h - 1) * DIL)
            d, dy, ds = d_ref[0, rows, :], dy_ref[0, rows, :], ds_ref[0, rows, :]
        dn2 = mm_t(jnp.concatenate([dy, ds], axis=1), w_rs[...])
        dd.append(depth_grad(d, dn2, mean2[o], factor2[o], g2, p2[o], q2[o]).astype(f32))
    zero = jnp.zeros((1, HW), f32)
    t0, t1, t2, tb, gg, gb = zero, zero, zero, zero, zero, zero
    for h in range(2 * nb):
        o = h // 2 + 1
        rows = slice(h * DIL, (h + 1) * DIL)
        x = x_ref[0, rows, :]
        a = mm(x, w_in[...])
        sig = sigmoid(a)
        u = a * sig
        mean, factor = mean1[o], factor1[o]
        scale = factor * g1
        n1 = (u * scale + (b1 - mean * scale)).astype(bf16).astype(f32)
        lo = seg.same[o - 1] if h % 2 == 0 else 1.0
        hi = 1.0 if h % 2 == 0 else seg.same[o]
        here, prev, nxt = dd[h + 1], dd[h], dd[h + 2]
        t0 = t0 + jnp.sum(nxt * n1, axis=0, keepdims=True) * hi
        t1 = t1 + jnp.sum(here * n1, axis=0, keepdims=True)
        t2 = t2 + jnp.sum(prev * n1, axis=0, keepdims=True) * lo
        tb = tb + jnp.sum(here, axis=0, keepdims=True)
        dn1 = k1 * here + (k0 * hi) * nxt + (k2 * lo) * prev
        h1 = (u - mean) * factor
        gg = gg + jnp.sum(dn1 * h1, axis=0, keepdims=True)
        gb = gb + jnp.sum(dn1, axis=0, keepdims=True)
        du = factor * (dn1 * g1 - p1[o] - h1 * q1[o])
        da = (du * (sig + u * (1.0 - sig))).astype(bf16)
        g_in[...] += mm_rows(x, da)
        feats_ref[0, rows, :] = (dy_ref[0, rows, :].astype(f32) + mm_t(da, w_in[...])).astype(bf16)
    for r, val in ((0, gg), (1, gb), (4, t0), (5, t1), (6, t2), (7, tb)):
        g_vec[r : r + 1, :] += val


def input_grad(me, lengths, stats, d, edge, feats, dy, near, far, ds, ds_near, ds_far, w_in, w_rs, vec):
    micro, frames, _ = d.shape
    halo = pl.BlockSpec((1, DIL, B), lambda m: (m, BLK // DIL, 0))
    return pl.pallas_call(
        input_kernel,
        grid=(micro,),
        out_shape=(
            jax.ShapeDtypeStruct(feats.shape, bf16),
            jax.ShapeDtypeStruct((B, HW), f32),
            jax.ShapeDtypeStruct((8, HW), f32),
        ),
        in_specs=[smem(), smem()]
        + [whole(s.shape) for s in stats]
        + [per_micro(v.shape) for v in (d, edge, feats, dy)]
        + [halo, halo]
        + [per_micro(v.shape) for v in (ds, ds_near, ds_far)]
        + [whole(w.shape) for w in (w_in, w_rs, vec)],
        out_specs=(per_micro(feats.shape), whole((B, HW)), whole((8, HW))),
        compiler_params=pltpu.CompilerParams(vmem_limit_bytes=INPUT_MIB * MIB),
        name="input_grad",
    )(me, lengths, *stats, d, edge, feats, dy, near, far, ds, ds_near, ds_far, w_in, w_rs, vec)


def pack_kernel(pos_ref, g_in, g_rs, g_mask, g_dec, vec_a, vec_b, keep_ref, send_ref, t, out, wd):
    for k in range(4):
        cols = slice(128 * k, 128 * k + 128)
        t[pl.ds(R_IN + k, 128, stride=4), :] = g_in[:, cols]
        for c in range(C):
            t[pl.ds(R_MASK + 512 * c + k, 128, stride=4), :] = g_mask[
                :, 512 * c + 128 * k : 512 * c + 128 * k + 128
            ]
        t[pl.ds(R_VEC + k, 8, stride=4), :] = vec_a[:, cols] + vec_b[:, cols]
    t[R_RES : R_RES + 512, :] = g_rs[0:128, :].T
    t[R_SKIP : R_SKIP + 512, :] = g_rs[128:256, :].T
    wd[...] = jnp.concatenate([g_dec[...], jnp.zeros((128 - L, C * N), f32)], axis=0).T
    part = lax.broadcasted_iota(jnp.int32, (64, 128), 1) // L
    for c in range(C):
        rows = jnp.zeros((64, 128), f32)
        for s in range(8):
            piece = pltpu.roll(wd[pl.ds(512 * c + s, 64, stride=8), :], L * s, 1)
            rows = jnp.where(part == s, piece, rows)
        t[R_DEC + 64 * c : R_DEC + 64 * c + 64, :] = rows
    out[...] = jnp.zeros_like(out)
    for i in range(NCH):
        start = pl.multiple_of(pos_ref[i] * 8, 8)
        out[pl.ds(start, 8), :] = t[8 * i : 8 * i + 8, :]
    half = keep_ref.shape[0]
    keep_ref[...] = out[0:half, :]
    send_ref[...] = out[half : 2 * half, :].astype(bf16)


def pack(pos, g_in, g_rs, g_mask, g_dec, vec_a, vec_b, rows):
    return pl.pallas_call(
        pack_kernel,
        out_shape=(
            jax.ShapeDtypeStruct((rows // 2, 128), f32),
            jax.ShapeDtypeStruct((rows // 2, 128), bf16),
        ),
        in_specs=[smem()] + [vmem()] * 6,
        out_specs=(vmem(), vmem()),
        scratch_shapes=[
            pltpu.VMEM((ROWS_ALL, 128), f32),
            pltpu.VMEM((rows, 128), f32),
            pltpu.VMEM((C * N, 128), f32),
        ],
        compiler_params=pltpu.CompilerParams(vmem_limit_bytes=16 * MIB),
        name="pack",
    )(pos, g_in, g_rs, g_mask, g_dec, vec_a, vec_b)


def fold_kernel(n_got, n_next, *refs):
    keep_ref, got = refs[0], refs[1 : 1 + n_got]
    outs = refs[1 + n_got :]
    total = keep_ref[...]
    for g in got:
        total = total + g[...].astype(f32)
    size = total.shape[0] // n_next
    outs[0][...] = total[0:size, :]
    for q in range(1, n_next):
        outs[q][...] = total[q * size : (q + 1) * size, :].astype(bf16)


def fold(keep, got, n_next):
    size = keep.shape[0] // n_next
    outs = [jax.ShapeDtypeStruct((size, 128), f32)]
    outs += [jax.ShapeDtypeStruct((size, 128), bf16)] * (n_next - 1)
    return pl.pallas_call(
        functools.partial(fold_kernel, len(got), n_next),
        out_shape=tuple(outs),
        in_specs=[vmem()] * (1 + len(got)),
        out_specs=tuple(vmem() for _ in outs),
        compiler_params=pltpu.CompilerParams(vmem_limit_bytes=8 * MIB),
        name="fold",
    )(keep, *got)


def adam_kernel(n_got, count_ref, *refs):
    keep_ref, got = refs[0], refs[1 : 1 + n_got]
    master_ref, one_ref, two_ref, new_master, new_one, new_two, buf = refs[1 + n_got :]
    total = keep_ref[...]
    for g in got:
        total = total + g[...].astype(f32)
    buf[...] = total
    slots = master_ref.shape[0]
    used = lax.broadcasted_iota(jnp.int32, (slots, 128), 0) < count_ref[0]
    for j in range(8):
        cols = slice(128 * j, 128 * j + 128)
        grad = buf[pl.ds(j, slots, stride=8), :]
        master = master_ref[:, cols]
        one = beta_one * one_ref[:, cols] + (1.0 - beta_one) * grad
        two = beta_two * two_ref[:, cols] + (1.0 - beta_two) * grad * grad
        unbias_one = one / (1.0 - beta_one**STEP)
        unbias_two = two / (1.0 - beta_two**STEP)
        new = master - learn_rate * (
            unbias_one / (jnp.sqrt(unbias_two) + adam_eps) + weight_decay * master
        )
        new_master[:, cols] = jnp.where(used, new, 0.0)
        new_one[:, cols] = jnp.where(used, one, 0.0)
        new_two[:, cols] = jnp.where(used, two, 0.0)


def adam(count, keep, got, master, one, two):
    out = jax.ShapeDtypeStruct(master.shape, f32)
    return pl.pallas_call(
        functools.partial(adam_kernel, len(got)),
        out_shape=(out, out, out),
        in_specs=[smem()] + [vmem()] * (4 + len(got)),
        out_specs=(vmem(), vmem(), vmem()),
        scratch_shapes=[pltpu.VMEM(keep.shape, f32)],
        compiler_params=pltpu.CompilerParams(vmem_limit_bytes=4 * MIB),
        name="adam",
    )(count, keep, *got, master, one, two)


def local(n_tm, n_src, feats, encoded, seg_lengths, owners, master, moment_one, moment_two, out_cot, wave_cot):
    n_dev = n_tm * n_src
    me = lax.axis_index(AXES)
    core = lax.axis_index("src")
    micro, frames, _ = feats.shape
    nb = frames // BLK
    slots = master.shape[0]


    across = [(i, i + 1) for i in range(1, n_dev - 1, 2)]
    across = across + [(j, i) for i, j in across]

    def ends(at_end, *arrays):
        size = [jnp.where(at_end, v.shape[1] - w, 0) for v, w in arrays]
        rows = [lax.dynamic_slice_in_dim(v, at, w, axis=1) for (v, w), at in zip(arrays, size)]
        return rows[0] if len(rows) == 1 else jnp.concatenate(rows, axis=1)

    cot = jnp.transpose(wave_cot[:, 0], (0, 2, 1))
    halo = (feats, BLK), (out_cot, DIL)
    parts, (near, far, cot_other) = gather_tiles(
        to_tiles(master), n_dev, ends(core == 0, *halo), ends(core == 1, *halo), cot
    )
    near = swap(near, 1, n_dev)
    far = lax.ppermute(far, AXES, across)
    cot_other = swap(cot_other, 1, n_dev)

    owner_ids = owners[:, 0]
    order = jnp.arange(NCH, dtype=jnp.int32)
    earlier = (owner_ids[:, None] == owner_ids[None, :]) & (order[None, :] < order[:, None])
    rank = jnp.sum(earlier.astype(jnp.int32), axis=1)
    pos = relative_block(owner_ids, me, n_dev) * slots + rank
    count = jnp.sum((owner_ids == me).astype(jnp.int32)).reshape(1)
    here = me.astype(jnp.int32).reshape(1)

    w_in, w_rs, w_mask, w_dect, vec, stats = unpack(pos, parts, feats, n_dev)
    stats1 = share_sums(stats, n_dev)
    d, edge, stats = depth(here, seg_lengths, stats1, feats, near, far, w_in, vec)
    stats2 = share_sums(stats, n_dev)
    block_out, wave_own, wave_other, ds, stats, g_rs, g_mask, g_dec, vec_a = head(
        here, seg_lengths, stats2, d, feats, encoded, out_cot, cot, cot_other, w_rs, w_mask, w_dect, vec
    )
    stats3 = share_sums(stats, n_dev)
    ds_near = swap(ends(core == 0, (ds, DIL)), 1, n_dev)
    ds_far = lax.ppermute(ends(core == 1, (ds, DIL)), AXES, across)

    wave_got = swap(wave_other, 1, n_dev)
    waves = jnp.concatenate(
        [jnp.where(core == 0, wave_own, wave_got), jnp.where(core == 0, wave_got, wave_own)], axis=2
    )
    waves = jnp.transpose(waves, (0, 2, 1))[:, None]

    feats_grad, g_in, vec_b = input_grad(
        here, seg_lengths, (stats1, stats2, stats3), d, edge, feats, out_cot, near, far, ds, ds_near, ds_far, w_in, w_rs, vec
    )

    keep, send = pack(pos, g_in, g_rs, g_mask, g_dec, vec_a, vec_b, n_dev * slots * 8)
    received = [swap(send, 1, n_dev)]
    for bits in reversed(stages(n_dev)[:-1]):
        n_next = 1 << len(bits)
        keep, *sends = fold(keep, received, n_next)
        received = [swap(s, spread(bits, k + 1), n_dev) for k, s in enumerate(sends)]
    new_master, new_one, new_two = adam(count, keep, received, master, moment_one, moment_two)
    return block_out, feats_grad, waves, new_master, new_one, new_two


def solution(mesh):
    n_tm, n_src = mesh.shape["tm"], mesh.shape["src"]
    return jax.shard_map(
        functools.partial(local, n_tm, n_src),
        mesh=mesh,
        in_specs=(
            P(None, AXES, None),
            P(None, AXES, None),
            P(),
            P(),
            P(AXES, None),
            P(AXES, None),
            P(AXES, None),
            P(None, AXES, None),
            P(None, "src", "tm", None),
        ),
        out_specs=(
            P(None, AXES, None),
            P(None, AXES, None),
            P(None, "src", "tm", None),
            P(AXES, None),
            P(AXES, None),
            P(AXES, None),
        ),
        check_vma=False,
    )
```

time: 162 us -> 115 us (0.71)
  starting transfers between devices: 44.2 us -> 26.7 us
  Pallas kernels: 57.2 us -> 41.7 us
  waiting for transfers between devices: 31.5 us -> 19.5 us
  blocking collectives: 10.2 us -> 21.3 us
  other arithmetic: 8.89 us -> 1.67 us
  local copies, waits for them, and re-layouts: 8.34 us -> 3.04 us
    all_to_all x1 -> x2, blocking collectives: 10.2 us -> 21.3 us  [share_sums(): return lax.all_to_all(rows, AXES, 0, 0, tiled=True)]
    pallas_call x3 -> x2, Pallas kernels: 27.6 us -> 16.7 us  [the longest x1 14.1 us: head(): pl.pallas_call(head_kernel, grid_spec=pltpu.PrefetchScalarGridSpec(num_sc...]
    ppermute x6 -> x2, starting transfers between devices: 9.37 us -> 1.34 us  [the longest x1 0.67 us: local(): far = lax.ppermute(far, AXES, across)]
    all_to_all x2 -> x1, waiting for transfers between devices: 12.9 us -> 7.06 us  [share_sums(): return lax.all_to_all(rows, AXES, 0, 0, tiled=True)]
    ppermute x14 -> x21, starting transfers between devices: 27.8 us -> 22.9 us  [swap(): return lax.ppermute(value, AXES, [(i, i ^ mask) for i in range(n_dev)])]
    unnamed x38 -> x22, local copies, waits for them, and re-layouts: 5.53 us -> 0.93 us
    all_to_all x2 -> x1, starting transfers between devices: 6.96 us -> 2.54 us  [share_sums(): return lax.all_to_all(rows, AXES, 0, 0, tiled=True)]
    ppermute x14 -> x21, waiting for transfers between devices: 16 us -> 12.4 us  [swap(): return lax.ppermute(value, AXES, [(i, i ^ mask) for i in range(n_dev)])]
  transfers between devices with their start and end apart: 22 -> 24, of which waited for: 11 -> 12; matrix products, arithmetic and copies ran while one was open for 8% -> 3% of each run, Pallas kernels for 4% -> 9%
where the time goes in v2:
time: 115 us
  Pallas kernels  41.7 us (36%)
  starting transfers between devices  26.7 us (23%)
  blocking collectives  21.3 us (19%)
  waiting for transfers between devices  19.5 us (17%)
  local copies, waits for them, and re-layouts  3.04 us (3%)
  other arithmetic  1.67 us (1%)
    ppermute x21, starting transfers between devices, swap(): return lax.ppermute(value, AXES, [(i, i ^ mask) for i in range(n_dev)])  22.9 us
    all_to_all x2, blocking collectives, share_sums(): return lax.all_to_all(rows, AXES, 0, 0, tiled=True)  21.3 us
    pallas_call x1, Pallas kernels, input_grad(): pl.pallas_call(input_kernel, grid=(micro,), out_shape=(jax.ShapeDtypeStru...  14.4 us
    pallas_call x1, Pallas kernels, head(): pl.pallas_call(head_kernel, grid_spec=pltpu.PrefetchScalarGridSpec(num_sc...  14.1 us
    ppermute x21, waiting for transfers between devices, swap(): return lax.ppermute(value, AXES, [(i, i ^ mask) for i in range(n_dev)])  12.4 us
    pallas_call x1, Pallas kernels, depth(): pl.pallas_call(depth_kernel, grid=(micro,), out_shape=(jax.ShapeDtypeStru...  7.79 us
    all_to_all x1, waiting for transfers between devices, share_sums(): return lax.all_to_all(rows, AXES, 0, 0, tiled=True)  7.06 us
    pallas_call x1, Pallas kernels, unpack(): pl.pallas_call(functools.partial(unpack_kernel, len(parts)), out_shape=ou...  2.55 us
  transfers between devices with their start and end apart: 24, of which 12 were waited for; matrix products, arithmetic and copies ran while one was open for 3% of the time, Pallas kernels for 9%

profile of v2, /device:TPU:0, one launch (start us, length us, event | category | flops | bytes accessed | tf_op | source)
XLA Modules:
  0.0 114.8 jit_solution(7042330363321345127)
XLA Ops:
  0.7 0.9 copy-done.4
  1.6 5.1 %collective-permute-start.2 = (bf16[88,128]{1,0:T(8,128)(2,1)S(1)}, bf16[88,128]{1,0:T(8,128)(2,1)S(1)}, u32[]{:S(2)}, u32[]{:S(2)}) collective-permute-start(bf16[88,128]{1,0:T(8,128)(2,1)S(1)} %to_tiles.1), channel_id=1, source_target_pairs={{0,24},{1,25},{2,26},{3,27},{4,28},{5,29},{6,30},{7,31},{8,16},{9,... | collective-permute-start | bytes 67592 | tf_op jit(solution)/shard_map/ppermute | solution.py:84
  6.7 0.6 collective-permute-start
  7.3 1.1 constant_dynamic-slice_fusion.3
  8.4 1.0 constant_dynamic-slice_fusion.2
  9.4 2.0 %collective-permute-done.1 = bf16[88,128]{1,0:T(8,128)(2,1)S(1)} collective-permute-done((bf16[88,128]{1,0:T(8,128)(2,1)S(1)}, bf16[88,128]{1,0:T(8,128)(2,1)S(1)}, u32[]{:S(2)}, u32[]{:S(2)}) %collective-permute-start.1) | collective-permute-done | bytes 22560 | tf_op jit(solution)/shard_map/ppermute | solution.py:84
  11.4 2.5 %collective-permute-start.5 = (bf16[352,128]{1,0:T(8,128)(2,1)S(1)}, bf16[352,128]{1,0:T(8,128)(2,1)S(1)}, u32[]{:S(2)}, u32[]{:S(2)}) collective-permute-start(bf16[352,128]{1,0:T(8,128)(2,1)S(1)} %pad_maximum_fusion.2.refs_0_), channel_id=1, source_target_pairs={{0,6},{1,7},{2,4},{3,5},{4,2},{5,3},{6,0},{7,1},{8,14},{9,15},{10,... | collective-permute-start | bytes 270344 | tf_op jit(solution)/shard_map/ppermute | solution.py:84
  15.0 2.8 %collective-permute-done.5.refs_3_ = bf16[352,128]{1,0:T(8,128)(2,1)S(1)} collective-permute-done((bf16[352,128]{1,0:T(8,128)(2,1)S(1)}, bf16[352,128]{1,0:T(8,128)(2,1)S(1)}, u32[]{:S(2)}, u32[]{:S(2)}) %collective-permute-start.5) | collective-permute-done | bytes 90144 | tf_op jit(solution)/shard_map/ppermute | solution.py:84
  17.9 0.8 collective-permute-done.4.refs_2_
  18.9 0.7 collective-permute-start.11
  19.7 1.9 %collective-permute-start.6 = (bf16[352,128]{1,0:T(8,128)(2,1)S(1)}, bf16[352,128]{1,0:T(8,128)(2,1)S(1)}, u32[]{:S(2)}, u32[]{:S(2)}) collective-permute-start(bf16[352,128]{1,0:T(8,128)(2,1)S(1)} %pad_maximum_fusion.2.refs_0_), channel_id=1, source_target_pairs={{0,1},{1,0},{2,3},{3,2},{4,5},{5,4},{6,7},{7,6},{8,9},{9,8},{10,11... | collective-permute-start | bytes 270344 | tf_op jit(solution)/shard_map/ppermute | solution.py:84
  23.1 0.7 convert_reduce_fusion.1
  23.8 2.5 %unpack.1 = (bf16[128,512]{1,0:T(8,128)(2,1)S(1)}, bf16[512,256]{1,0:T(8,128)(2,1)S(1)}, bf16[128,1024]{1,0:T(8,128)(2,1)S(1)}, bf16[16,1024]{1,0:T(8,128)(2,1)S...) custom-call(s32[340]{0:T(512)S(1)} %get-tuple-element.109.pos_ref, bf16[4,512,128]{2,1,0:T(8,128)(2,1)S(1)} %copy-done, ...), custom_call_target="tpu_custom_call" | custom-call | tf_op jit(solution)/shard_map/unpack/pallas_call | solution.py:189
  26.4 11.6 %all_to_all.15.stats_ref.stats1_ref = f32[32,1,128]{2,1,0:T(1,128)S(1)} all-to-all(f32[32,1,128]{2,1,0:T(1,128)S(1)} %get-tuple-element.51), channel_id=1, replica_groups=mesh['tm'=16,'src'=2] {'tm','src'}, dimensions={0} | all-to-all | bytes 32768 | tf_op jit(solution)/shard_map/all_to_all | solution.py:108
  38.0 7.8 %depth.1 = (f32[4,512,512]{2,1,0:T(8,128)}, f32[4,256,512]{2,1,0:T(8,128)}, f32[32,1,128]{2,1,0:T(1,128)}) custom-call(s32[1]{0:T(128)} %bitcast.me_ref, s32[4,8]{1,0:T(4,128)S(1)} %copy-done.9, f32[32,1,128]{2,1,0:T(1,128)S(1)} %all_to_all.15.stats_ref.stats1_ref, bf16[4,512,128]{2,1,0:T(8,128)(2,1)S(1)} %copy-done, ...), custom_call_target="tpu_custom_call" | custom-call | tf_op jit(solution)/shard_map/depth/pallas_call | solution.py:319
  45.8 2.5 %all-to-all-start.1 = ((f32[32,1,128]{2,1,0:T(1,128)}), f32[32,1,128]{2,1,0:T(1,128)S(1)}, u32[]{:S(2)}, u32[]{:S(2)}) async-start(f32[32,1,128]{2,1,0:T(1,128)} %get-tuple-element.56), calls=%async_computation.1 | async-start | bytes 32768 | tf_op jit(solution)/shard_map/all_to_all | solution.py:108
  48.3 7.1 %all-to-all-done.1.stats_ref.stats2_ref = f32[32,1,128]{2,1,0:T(1,128)S(1)} async-done(((f32[32,1,128]{2,1,0:T(1,128)}), f32[32,1,128]{2,1,0:T(1,128)S(1)}, u32[]{:S(2)}, u32[]{:S(2)}) %all-to-all-start.1) | async-done | bytes 16416 | tf_op jit(solution)/shard_map/all_to_all | solution.py:108
  55.4 14.1 %head.1 = (bf16[4,512,128]{2,1,0:T(8,128)(2,1)}, bf16[4,16,512]{2,1,0:T(8,128)(2,1)S(1)}, bf16[4,16,512]{2,1,0:T(8,128)(2,1)S(1)}, bf16[4,512,128]{2,1,0:T(8,128...) custom-call(s32[1]{0:T(128)} %bitcast.me_ref, ...), custom_call_target="tpu_custom_call" | custom-call | tf_op jit(solution)/shard_map/head/pallas_call | solution.py:522
  69.6 0.7 collective-permute-start.14
  70.2 2.0 %collective-permute-start.13 = (bf16[4,128,128]{2,1,0:T(8,128)(2,1)S(1)}, bf16[4,128,128]{2,1,0:T(8,128)(2,1)S(1)}, u32[]{:S(2)}, u32[]{:S(2)}) collective-permute-start(bf16[4,128,128]{2,1,0:T(8,128)(2,1)S(1)} %get-tuple-element.101), channel_id=1, source_target_pairs={{0,1},{1,0},{2,3},{3,2},{4,5},{5,4},{6,7},{7,6},{8,9},{9,8},{10,11... | collective-permute-start | bytes 393224 | tf_op jit(solution)/shard_map/ppermute | solution.py:84
  72.2 9.7 %all_to_all.16.stats3_ref = f32[32,1,128]{2,1,0:T(1,128)S(1)} all-to-all(f32[32,1,128]{2,1,0:T(1,128)S(1)} %get-tuple-element.63), channel_id=1, replica_groups=mesh['tm'=16,'src'=2] {'tm','src'}, dimensions={0} | all-to-all | bytes 32768 | tf_op jit(solution)/shard_map/all_to_all | solution.py:108
  81.9 14.4 %input_grad.1 = (bf16[4,512,128]{2,1,0:T(8,128)(2,1)}, f32[128,512]{1,0:T(8,128)S(1)}, f32[8,512]{1,0:T(8,128)S(1)}) custom-call(s32[1]{0:T(128)} %bitcast.me_ref, s32[4,8]{1,0:T(4,128)S(1)} %copy-done.9, f32[32,1,128]{2,1,0:T(1,128)S(1)} %all_to_all.15.stats_ref.stats1_ref, f32[32,1,128]{2,1,0:T(1,128)S(1)} %all-to-all-done.1.stats_ref.stats2_ref, ...), custom_call_target="tpu_custom_call" | custom-call | tf_op jit(solution)/shard_map/input_grad/pallas_call | solution.py:666
  96.3 1.3 %pack.1 = (f32[1408,128]{1,0:T(8,128)S(1)}, bf16[1408,128]{1,0:T(8,128)(2,1)S(1)}) custom-call(s32[340]{0:T(512)S(1)} %get-tuple-element.109.pos_ref, f32[128,512]{1,0:T(8,128)S(1)} %get-tuple-element.69.g_in, f32[256,512]{1,0:T(8,128)S(1)} %copy-done.2, f32[128,1024]{1,0:T(8,128)S(1)} %copy-done.3, f32[16,1024]{1,0:T(8,128)S(1)} %get-tuple-element.72.g_dec, ...), custom_call_target="tpu_custom_call" | custom-call | tf_op jit(solution)/shard_map/pack/pallas_call | solution.py:715
  98.2 1.2 %collective-permute-done.16.refs_1_ = bf16[1408,128]{1,0:T(8,128)(2,1)S(1)} collective-permute-done((bf16[1408,128]{1,0:T(8,128)(2,1)S(1)}, bf16[1408,128]{1,0:T(8,128)(2,1)S(1)}, u32[]{:S(2)}, u32[]{:S(2)}) %collective-permute-start.16) | collective-permute-done | bytes 360480 | tf_op jit(solution)/shard_map/ppermute | solution.py:84
  100.7 2.3 %collective-permute-start.19 = (bf16[352,128]{1,0:T(8,128)(2,1)S(1)}, bf16[352,128]{1,0:T(8,128)(2,1)S(1)}, u32[]{:S(2)}, u32[]{:S(2)}) collective-permute-start(bf16[352,128]{1,0:T(8,128)(2,1)S(1)} %get-tuple-element.80), channel_id=1, source_target_pairs={{0,6},{1,7},{2,4},{3,5},{4,2},{5,3},{6,0},{7,1},{8,14},{9,15},{10,... | collective-permute-start | bytes 270344 | tf_op jit(solution)/shard_map/ppermute | solution.py:84
  103.1 1.7 %collective-permute-done.17.refs_1_ = bf16[352,128]{1,0:T(8,128)(2,1)S(1)} collective-permute-done((bf16[352,128]{1,0:T(8,128)(2,1)S(1)}, bf16[352,128]{1,0:T(8,128)(2,1)S(1)}, u32[]{:S(2)}, u32[]{:S(2)}) %collective-permute-start.17) | collective-permute-done | bytes 90144 | tf_op jit(solution)/shard_map/ppermute | solution.py:84
  104.8 1.8 %collective-permute-done.18.refs_2_ = bf16[352,128]{1,0:T(8,128)(2,1)S(1)} collective-permute-done((bf16[352,128]{1,0:T(8,128)(2,1)S(1)}, bf16[352,128]{1,0:T(8,128)(2,1)S(1)}, u32[]{:S(2)}, u32[]{:S(2)}) %collective-permute-start.18) | collective-permute-done | bytes 90144 | tf_op jit(solution)/shard_map/ppermute | solution.py:84
  106.6 0.6 collective-permute-start.20
  107.8 3.3 %collective-permute-start.22 = (bf16[88,128]{1,0:T(8,128)(2,1)S(1)}, bf16[88,128]{1,0:T(8,128)(2,1)S(1)}, u32[]{:S(2)}, u32[]{:S(2)}) collective-permute-start(bf16[88,128]{1,0:T(8,128)(2,1)S(1)} %get-tuple-element.84), channel_id=1, source_target_pairs={{0,24},{1,25},{2,26},{3,27},{4,28},{5,29},{6,30},{7,31},{8,16},{9,... | collective-permute-start | bytes 67592 | tf_op jit(solution)/shard_map/ppermute | solution.py:84
  111.1 0.7 maximum_bitcast_fusion
  111.9 1.4 %collective-permute-done.22.refs_3_ = bf16[88,128]{1,0:T(8,128)(2,1)S(1)} collective-permute-done((bf16[88,128]{1,0:T(8,128)(2,1)S(1)}, bf16[88,128]{1,0:T(8,128)(2,1)S(1)}, u32[]{:S(2)}, u32[]{:S(2)}) %collective-permute-start.22) | collective-permute-done | bytes 22560 | tf_op jit(solution)/shard_map/ppermute | solution.py:84
  113.4 1.4 %adam.1 = (f32[11,1024]{1,0:T(8,128)}, f32[11,1024]{1,0:T(8,128)}, f32[11,1024]{1,0:T(8,128)}) custom-call(s32[1]{0:T(128)} %bitcast.6.count_ref, f32[88,128]{1,0:T(8,128)S(1)} %get-tuple-element.81.refs_0_, bf16[88,128]{1,0:T(8,128)(2,1)S(1)} %collective-permute-done.20.refs_1_, bf16[88,128]{1,0:T(8,128)(2,1)S(1)} %collective-permute-done.21.refs_2_, ...), custom_call_target="tpu_custom_call" | custom-call | tf_op jit(solution)/shard_map/adam/pallas_call | solution.py:786
  (59 shorter events, 5.8 us)
Async XLA Ops:
  0.6 23.2 %copy-start = (bf16[4,512,128]{2,1,0:T(8,128)(2,1)S(1)}, bf16[4,512,128]{2,1,0:T(8,128)(2,1)}, u32[]{:S(2)}) copy-start(bf16[4,512,128]{2,1,0:T(8,128)(2,1)} %x_ref.7) | copy-start | bytes 1572868
  1.5 18.1 %copy-start.10 = (s32[340,1]{0,1:T(1,128)S(1)}, s32[340,1]{0,1:T(1,128)}, u32[]{:S(2)}) copy-start(s32[340,1]{0,1:T(1,128)} %param.12) | copy-start | bytes 4084
  1.5 21.4 %copy-start.6 = (bf16[4,1,1024,16]{2,3,1,0:T(8,128)(2,1)S(1)}, bf16[4,1,1024,16]{2,3,1,0:T(8,128)(2,1)}, u32[]{:S(2)}) copy-start(bf16[4,1,1024,16]{2,3,1,0:T(8,128)(2,1)} %param.17) | copy-start | bytes 393220
  1.6 7.8 %collective-permute-start.2 = (bf16[88,128]{1,0:T(8,128)(2,1)S(1)}, bf16[88,128]{1,0:T(8,128)(2,1)S(1)}, u32[]{:S(2)}, u32[]{:S(2)}) collective-permute-start(bf16[88,128]{1,0:T(8,128)(2,1)S(1)} %to_tiles.1), channel_id=1, source_target_pairs={{0,24},{1,25},{2,26},{3,27},{4,28},{5,29},{6,30},{7,31},{8,16},{9,... | collective-permute-start | bytes 67592 | tf_op jit(solution)/shard_map/ppermute | solution.py:84
  6.7 4.7 %collective-permute-start.1 = (bf16[88,128]{1,0:T(8,128)(2,1)S(1)}, bf16[88,128]{1,0:T(8,128)(2,1)S(1)}, u32[]{:S(2)}, u32[]{:S(2)}) collective-permute-start(bf16[88,128]{1,0:T(8,128)(2,1)S(1)} %to_tiles.1), channel_id=1, source_target_pairs={{0,16},{1,17},{2,18},{3,19},{4,20},{5,21},{6,22},{7,23},{8,24},{9,... | collective-permute-start | bytes 67592 | tf_op jit(solution)/shard_map/ppermute | solution.py:84
  6.7 4.7 %collective-permute-start = (bf16[88,128]{1,0:T(8,128)(2,1)S(1)}, bf16[88,128]{1,0:T(8,128)(2,1)S(1)}, u32[]{:S(2)}, u32[]{:S(2)}) collective-permute-start(bf16[88,128]{1,0:T(8,128)(2,1)S(1)} %to_tiles.1), channel_id=1, source_target_pairs={{0,8},{1,9},{2,10},{3,11},{4,12},{5,13},{6,14},{7,15},{8,0},{9,1},... | collective-permute-start | bytes 67592 | tf_op jit(solution)/shard_map/ppermute | solution.py:84
  7.3 30.7 %copy-start.9 = (s32[4,8]{1,0:T(4,128)S(1)}, s32[4,8]{1,0:T(4,128)}, u32[]{:S(2)}) copy-start(s32[4,8]{1,0:T(4,128)} %seg_ref.5) | copy-start | bytes 388
  11.4 6.5 %collective-permute-start.5 = (bf16[352,128]{1,0:T(8,128)(2,1)S(1)}, bf16[352,128]{1,0:T(8,128)(2,1)S(1)}, u32[]{:S(2)}, u32[]{:S(2)}) collective-permute-start(bf16[352,128]{1,0:T(8,128)(2,1)S(1)} %pad_maximum_fusion.2.refs_0_), channel_id=1, source_target_pairs={{0,6},{1,7},{2,4},{3,5},{4,2},{5,3},{6,0},{7,1},{8,14},{9,15},{10,... | collective-permute-start | bytes 270344 | tf_op jit(solution)/shard_map/ppermute | solution.py:84
  13.9 4.7 %collective-permute-start.4 = (bf16[352,128]{1,0:T(8,128)(2,1)S(1)}, bf16[352,128]{1,0:T(8,128)(2,1)S(1)}, u32[]{:S(2)}, u32[]{:S(2)}) collective-permute-start(bf16[352,128]{1,0:T(8,128)(2,1)S(1)} %pad_maximum_fusion.2.refs_0_), channel_id=1, source_target_pairs={{0,4},{1,5},{2,6},{3,7},{4,0},{5,1},{6,2},{7,3},{8,12},{9,13},{10,... | collective-permute-start | bytes 270344 | tf_op jit(solution)/shard_map/ppermute | solution.py:84
  14.4 4.5 %collective-permute-start.3 = (bf16[352,128]{1,0:T(8,128)(2,1)S(1)}, bf16[352,128]{1,0:T(8,128)(2,1)S(1)}, u32[]{:S(2)}, u32[]{:S(2)}) collective-permute-start(bf16[352,128]{1,0:T(8,128)(2,1)S(1)} %pad_maximum_fusion.2.refs_0_), channel_id=1, source_target_pairs={{0,2},{1,3},{2,0},{3,1},{4,6},{5,7},{6,4},{7,5},{8,10},{9,11},{10,... | collective-permute-start | bytes 270344 | tf_op jit(solution)/shard_map/ppermute | solution.py:84
  18.9 19.0 %collective-permute-start.10 = (bf16[4,384,128]{2,1,0:T(8,128)(2,1)S(1)}, bf16[4,384,128]{2,1,0:T(8,128)(2,1)S(1)}, u32[]{:S(2)}, u32[]{:S(2)}) collective-permute-start(bf16[4,384,128]{2,1,0:T(8,128)(2,1)S(1)} %get-tuple-element.52), channel_id=1, source_target_pairs={{0,1},{1,0},{2,3},{3,2},{4,5},{5,4},{6,7},{7,6},{8,9},{9,8},{10,11... | collective-permute-start | bytes 1179656 | tf_op jit(solution)/shard_map/ppermute | solution.py:84
  18.9 19.0 %collective-permute-start.11 = (bf16[4,384,128]{2,1,0:T(8,128)(2,1)S(1)}, bf16[4,384,128]{2,1,0:T(8,128)(2,1)S(1)}, u32[]{:S(2)}, u32[]{:S(2)}) collective-permute-start(bf16[4,384,128]{2,1,0:T(8,128)(2,1)S(1)} %get-tuple-element.53), channel_id=1, source_target_pairs={{1,2},{3,4},{5,6},{7,8},{9,10},{11,12},{13,14},{15,16},{17,18},{19... | collective-permute-start | bytes 1179656 | tf_op jit(solution)/shard_map/ppermute | solution.py:820
  19.7 2.9 %collective-permute-start.6 = (bf16[352,128]{1,0:T(8,128)(2,1)S(1)}, bf16[352,128]{1,0:T(8,128)(2,1)S(1)}, u32[]{:S(2)}, u32[]{:S(2)}) collective-permute-start(bf16[352,128]{1,0:T(8,128)(2,1)S(1)} %pad_maximum_fusion.2.refs_0_), channel_id=1, source_target_pairs={{0,1},{1,0},{2,3},{3,2},{4,5},{5,4},{6,7},{7,6},{8,9},{9,8},{10,11... | collective-permute-start | bytes 270344 | tf_op jit(solution)/shard_map/ppermute | solution.py:84
  21.6 1.3 %collective-permute-start.7 = (bf16[352,128]{1,0:T(8,128)(2,1)S(1)}, bf16[352,128]{1,0:T(8,128)(2,1)S(1)}, u32[]{:S(2)}, u32[]{:S(2)}) collective-permute-start(bf16[352,128]{1,0:T(8,128)(2,1)S(1)} %collective-permute-done.3.refs_1_), channel_id=1, source_target_pairs={{0,1},{1,0},{2,3},{3,2},{4,5},{5,4},{6,7},{7,6},{8,9},{9,8},{10,11... | collective-permute-start | bytes 270344 | tf_op jit(solution)/shard_map/ppermute | solution.py:84
  21.9 1.9 %collective-permute-start.8 = (bf16[352,128]{1,0:T(8,128)(2,1)S(1)}, bf16[352,128]{1,0:T(8,128)(2,1)S(1)}, u32[]{:S(2)}, u32[]{:S(2)}) collective-permute-start(bf16[352,128]{1,0:T(8,128)(2,1)S(1)} %collective-permute-done.4.refs_2_), channel_id=1, source_target_pairs={{0,1},{1,0},{2,3},{3,2},{4,5},{5,4},{6,7},{7,6},{8,9},{9,8},{10,11... | collective-permute-start | bytes 270344 | tf_op jit(solution)/shard_map/ppermute | solution.py:84
  22.5 1.3 %collective-permute-start.9 = (bf16[352,128]{1,0:T(8,128)(2,1)S(1)}, bf16[352,128]{1,0:T(8,128)(2,1)S(1)}, u32[]{:S(2)}, u32[]{:S(2)}) collective-permute-start(bf16[352,128]{1,0:T(8,128)(2,1)S(1)} %collective-permute-done.5.refs_3_), channel_id=1, source_target_pairs={{0,1},{1,0},{2,3},{3,2},{4,5},{5,4},{6,7},{7,6},{8,9},{9,8},{10,11... | collective-permute-start | bytes 270344 | tf_op jit(solution)/shard_map/ppermute | solution.py:84
  22.9 25.4 %collective-permute-start.12 = (bf16[4,16,1024]{2,1,0:T(8,128)(2,1)S(1)}, bf16[4,16,1024]{2,1,0:T(8,128)(2,1)S(1)}, u32[]{:S(2)}, u32[]{:S(2)}) collective-permute-start(bf16[4,16,1024]{2,1,0:T(8,128)(2,1)S(1)} %bitcast.11), channel_id=1, source_target_pairs={{0,1},{1,0},{2,3},{3,2},{4,5},{5,4},{6,7},{7,6},{8,9},{9,8},{10,11... | collective-permute-start | bytes 393224 | tf_op jit(solution)/shard_map/ppermute | solution.py:84
  45.8 9.6 %all-to-all-start.1 = ((f32[32,1,128]{2,1,0:T(1,128)}), f32[32,1,128]{2,1,0:T(1,128)S(1)}, u32[]{:S(2)}, u32[]{:S(2)}) async-start(f32[32,1,128]{2,1,0:T(1,128)} %get-tuple-element.56), calls=%async_computation.1 | async-start | bytes 32768 | tf_op jit(solution)/shard_map/all_to_all | solution.py:108
  69.6 12.4 %collective-permute-start.14 = (bf16[4,128,128]{2,1,0:T(8,128)(2,1)S(1)}, bf16[4,128,128]{2,1,0:T(8,128)(2,1)S(1)}, u32[]{:S(2)}, u32[]{:S(2)}) collective-permute-start(bf16[4,128,128]{2,1,0:T(8,128)(2,1)S(1)} %get-tuple-element.100), channel_id=1, source_target_pairs={{1,2},{3,4},{5,6},{7,8},{9,10},{11,12},{13,14},{15,16},{17,18},{19... | collective-permute-start | bytes 393224 | tf_op jit(solution)/shard_map/ppermute | solution.py:840
  70.2 11.7 %collective-permute-start.13 = (bf16[4,128,128]{2,1,0:T(8,128)(2,1)S(1)}, bf16[4,128,128]{2,1,0:T(8,128)(2,1)S(1)}, u32[]{:S(2)}, u32[]{:S(2)}) collective-permute-start(bf16[4,128,128]{2,1,0:T(8,128)(2,1)S(1)} %get-tuple-element.101), channel_id=1, source_target_pairs={{0,1},{1,0},{2,3},{3,2},{4,5},{5,4},{6,7},{7,6},{8,9},{9,8},{10,11... | collective-permute-start | bytes 393224 | tf_op jit(solution)/shard_map/ppermute | solution.py:84
  81.9 14.4 %copy-start.2 = (f32[256,512]{1,0:T(8,128)S(1)}, f32[256,512]{1,0:T(8,128)}, u32[]{:S(2)}) copy-start(f32[256,512]{1,0:T(8,128)} %get-tuple-element.70.g_rs) | copy-start | bytes 1572868
  96.3 17.1 %copy-start.5 = (f32[11,1024]{1,0:T(8,128)S(1)}, f32[11,1024]{1,0:T(8,128)}, u32[]{:S(2)}) copy-start(f32[11,1024]{1,0:T(8,128)} %refs_4_.1) | copy-start | bytes 135172
  96.3 17.1 %copy-start.7 = (f32[11,1024]{1,0:T(8,128)S(1)}, f32[11,1024]{1,0:T(8,128)}, u32[]{:S(2)}) copy-start(f32[11,1024]{1,0:T(8,128)} %refs_5_.1) | copy-start | bytes 135172
  96.3 17.1 %copy-start.8 = (f32[11,1024]{1,0:T(8,128)S(1)}, f32[11,1024]{1,0:T(8,128)}, u32[]{:S(2)}) copy-start(f32[11,1024]{1,0:T(8,128)} %refs_6_.1) | copy-start | bytes 135172
  97.7 1.7 %collective-permute-start.16 = (bf16[1408,128]{1,0:T(8,128)(2,1)S(1)}, bf16[1408,128]{1,0:T(8,128)(2,1)S(1)}, u32[]{:S(2)}, u32[]{:S(2)}) collective-permute-start(bf16[1408,128]{1,0:T(8,128)(2,1)S(1)} %get-tuple-element.76), channel_id=1, source_target_pairs={{0,1},{1,0},{2,3},{3,2},{4,5},{5,4},{6,7},{7,6},{8,9},{9,8},{10,11... | collective-permute-start | bytes 1081352 | tf_op jit(solution)/shard_map/ppermute | solution.py:84
  97.7 5.3 %collective-permute-start.15 = (bf16[4,16,512]{2,1,0:T(8,128)(2,1)S(1)}, bf16[4,16,512]{2,1,0:T(8,128)(2,1)S(1)}, u32[]{:S(2)}, u32[]{:S(2)}) collective-permute-start(bf16[4,16,512]{2,1,0:T(8,128)(2,1)S(1)} %get-tuple-element.68), channel_id=1, source_target_pairs={{0,1},{1,0},{2,3},{3,2},{4,5},{5,4},{6,7},{7,6},{8,9},{9,8},{10,11... | collective-permute-start | bytes 196616 | tf_op jit(solution)/shard_map/ppermute | solution.py:84
  99.5 5.3 %collective-permute-start.17 = (bf16[352,128]{1,0:T(8,128)(2,1)S(1)}, bf16[352,128]{1,0:T(8,128)(2,1)S(1)}, u32[]{:S(2)}, u32[]{:S(2)}) collective-permute-start(bf16[352,128]{1,0:T(8,128)(2,1)S(1)} %get-tuple-element.78), channel_id=1, source_target_pairs={{0,2},{1,3},{2,0},{3,1},{4,6},{5,7},{6,4},{7,5},{8,10},{9,11},{10,... | collective-permute-start | bytes 270344 | tf_op jit(solution)/shard_map/ppermute | solution.py:84
  100.1 6.5 %collective-permute-start.18 = (bf16[352,128]{1,0:T(8,128)(2,1)S(1)}, bf16[352,128]{1,0:T(8,128)(2,1)S(1)}, u32[]{:S(2)}, u32[]{:S(2)}) collective-permute-start(bf16[352,128]{1,0:T(8,128)(2,1)S(1)} %get-tuple-element.79), channel_id=1, source_target_pairs={{0,4},{1,5},{2,6},{3,7},{4,0},{5,1},{6,2},{7,3},{8,12},{9,13},{10,... | collective-permute-start | bytes 270344 | tf_op jit(solution)/shard_map/ppermute | solution.py:84
  100.7 5.8 %collective-permute-start.19 = (bf16[352,128]{1,0:T(8,128)(2,1)S(1)}, bf16[352,128]{1,0:T(8,128)(2,1)S(1)}, u32[]{:S(2)}, u32[]{:S(2)}) collective-permute-start(bf16[352,128]{1,0:T(8,128)(2,1)S(1)} %get-tuple-element.80), channel_id=1, source_target_pairs={{0,6},{1,7},{2,4},{3,5},{4,2},{5,3},{6,0},{7,1},{8,14},{9,15},{10,... | collective-permute-start | bytes 270344 | tf_op jit(solution)/shard_map/ppermute | solution.py:84
  106.6 5.1 %collective-permute-start.20 = (bf16[88,128]{1,0:T(8,128)(2,1)S(1)}, bf16[88,128]{1,0:T(8,128)(2,1)S(1)}, u32[]{:S(2)}, u32[]{:S(2)}) collective-permute-start(bf16[88,128]{1,0:T(8,128)(2,1)S(1)} %get-tuple-element.82), channel_id=1, source_target_pairs={{0,8},{1,9},{2,10},{3,11},{4,12},{5,13},{6,14},{7,15},{8,0},{9,1},... | collective-permute-start | bytes 67592 | tf_op jit(solution)/shard_map/ppermute | solution.py:84
  107.2 4.7 %collective-permute-start.21 = (bf16[88,128]{1,0:T(8,128)(2,1)S(1)}, bf16[88,128]{1,0:T(8,128)(2,1)S(1)}, u32[]{:S(2)}, u32[]{:S(2)}) collective-permute-start(bf16[88,128]{1,0:T(8,128)(2,1)S(1)} %get-tuple-element.83), channel_id=1, source_target_pairs={{0,16},{1,17},{2,18},{3,19},{4,20},{5,21},{6,22},{7,23},{8,24},{9,... | collective-permute-start | bytes 67592 | tf_op jit(solution)/shard_map/ppermute | solution.py:84
  107.8 5.6 %collective-permute-start.22 = (bf16[88,128]{1,0:T(8,128)(2,1)S(1)}, bf16[88,128]{1,0:T(8,128)(2,1)S(1)}, u32[]{:S(2)}, u32[]{:S(2)}) collective-permute-start(bf16[88,128]{1,0:T(8,128)(2,1)S(1)} %get-tuple-element.84), channel_id=1, source_target_pairs={{0,24},{1,25},{2,26},{3,27},{4,28},{5,29},{6,30},{7,31},{8,16},{9,... | collective-permute-start | bytes 67592 | tf_op jit(solution)/shard_map/ppermute | solution.py:84
  (3 other events, 27.7 us)

commit v3 on v2

v3 whole, which is shorter than its diff:
```python
import functools

import jax
import jax.numpy as jnp
from jax import lax
from jax.experimental import pallas as pl
from jax.experimental.pallas import tpu as pltpu
from jax.sharding import PartitionSpec as P

N = 512
L = 16
B = 128
SC = 128
HW = 512
C = 2
DIL = 128
ROW = 1024
SEGS = 8
MICRO = 4
STEP = 10
NCH = 340
BLK = 256
KINDS = 8
CHUNK = 16
LANES, ROWS = 256, 16
HALF_W = 256

norm_eps = 1e-05
adam_eps = 1e-08
beta_one = 0.9
beta_two = 0.999
learn_rate = 0.2
weight_decay = 0.01

AXES = ("tm", "src")
f32 = jnp.float32
bf16 = jnp.bfloat16
MIB = 1024 * 1024
DEPTH_MIB = HEAD_MIB = INPUT_MIB = 20

R_IN, R_RES, R_SKIP, R_MASK, R_DEC, R_VEC = 0, 512, 1024, 1536, 2560, 2688
ROWS_ALL = 2720


def mm(a, b):
    return lax.dot_general(a, b, (((1,), (0,)), ((), ())), preferred_element_type=f32)


def mm_t(a, b):
    return lax.dot_general(a, b, (((1,), (1,)), ((), ())), preferred_element_type=f32)


def mm_rows(a, b):
    return lax.dot_general(a, b, (((0,), (0,)), ((), ())), preferred_element_type=f32)


def sigmoid(v):
    return 0.5 * jnp.tanh(0.5 * v) + 0.5


def fold_rows(v):
    return functools.reduce(lambda p, q: p + q, [v[i : i + 8, :] for i in range(0, v.shape[0], 8)])


def slope_parts(half, t):
    w = half * t
    return half + w, (1.0 + t) + (half - w * t)


def weave(first, second):
    steps = [((i + 0.5) / len(first), 0, i) for i in range(len(first))]
    steps += [((i + 0.5) / len(second), 1, i) for i in range(len(second))]
    for _, which, i in sorted(steps):
        (first, second)[which][i]()


def run(steps):
    for step in steps:
        step()


def tiles_of(halves):
    return [(h, slice(c, c + LANES)) for h in halves for c in range(0, HW, LANES)]


def loop(count, body, carry):
    def pair(i, carry):
        return body(2 * i + 1, 1, body(2 * i, 0, carry))

    return lax.fori_loop(0, count // 2, pair, carry)


def row_sum(v):
    return jnp.sum(v, axis=0, keepdims=True)


def vmem():
    return pl.BlockSpec(memory_space=pltpu.VMEM)


def smem():
    return pl.BlockSpec(memory_space=pltpu.SMEM)


def stages(n_dev):
    bits = n_dev.bit_length() - 1
    groups = []
    hi = bits - 1
    while hi >= 1:
        lo = max(1, hi - 1)
        groups.append(tuple(range(lo, hi + 1)))
        hi = lo - 1
    groups.append((0,))
    return groups


def spread(bits, k):
    return sum(((k >> j) & 1) << b for j, b in enumerate(bits))


def swap(value, mask, n_dev):
    return lax.ppermute(value, AXES, [(i, i ^ mask) for i in range(n_dev)])


def gather_tiles(tiles, n_dev, early, late):
    parts = [tiles]
    for k, bits in enumerate(stages(n_dev)[:-1]):
        if k == 1:
            parts, early = lax.optimization_barrier((parts, early))
        z = parts[0] if len(parts) == 1 else jnp.concatenate(parts, axis=0)
        parts = [z] + [swap(z, spread(bits, q), n_dev) for q in range(1, 1 << len(bits))]
    parts, late = lax.optimization_barrier((parts, late))
    return parts + [swap(z, 1, n_dev) for z in parts], early, late


def relative_block(owner, me, n_dev):
    q = owner ^ me
    index = jnp.zeros_like(q)
    size = 1
    for bits in stages(n_dev):
        digit = sum(((q >> b) & 1) << j for j, b in enumerate(bits))
        index = index + digit * size
        size = size << len(bits)
    return index


def share_sums(rows, n_dev):
    return lax.all_to_all(rows, AXES, 0, 0, tiled=True)


def tile_kernel(m_ref, out_ref, buf):
    slots = m_ref.shape[0]
    for j in range(8):
        buf[pl.ds(j, slots, stride=8), :] = m_ref[:, 128 * j : 128 * j + 128]
    out_ref[...] = buf[...].astype(bf16)


def to_tiles(master):
    slots = master.shape[0]
    return pl.pallas_call(
        tile_kernel,
        out_shape=jax.ShapeDtypeStruct((slots * 8, 128), bf16),
        in_specs=[vmem()],
        out_specs=vmem(),
        scratch_shapes=[pltpu.VMEM((slots * 8, 128), f32)],
        compiler_params=pltpu.CompilerParams(vmem_limit_bytes=4 * MIB),
        name="to_tiles",
    )(master)


def stat_rows(values, shape):
    lane = lax.broadcasted_iota(jnp.int32, shape, 1)
    row = jnp.zeros(shape, f32)
    for where, v in values.items():
        row = jnp.where(lane == where, v, row)
    return row


def unpack_kernel(n_parts, pos_ref, x_ref, *refs):
    parts, refs = refs[:n_parts], refs[n_parts:]
    w_in, w_rs, w_mask, w_dect, vec, stats, g, t, wd = refs
    size = parts[0].shape[0]
    for k, part in enumerate(parts):
        g[k * size : (k + 1) * size, :] = part[...].astype(f32)
    for i in range(NCH):
        start = pl.multiple_of(pos_ref[i] * 8, 8)
        t[8 * i : 8 * i + 8, :] = g[pl.ds(start, 8), :]
    for k in range(4):
        cols = slice(128 * k, 128 * k + 128)
        w_in[:, cols] = (0.5 * t[pl.ds(R_IN + k, 128, stride=4), :]).astype(bf16)
        for c in range(C):
            w_mask[:, 512 * c + 128 * k : 512 * c + 128 * k + 128] = (
                0.5 * t[pl.ds(R_MASK + 512 * c + k, 128, stride=4), :]
            ).astype(bf16)
        vec[:, cols] = t[pl.ds(R_VEC + k, 8, stride=4), :]
    w_rs[:, 0:128] = t[R_RES : R_RES + 512, :].astype(bf16)
    w_rs[:, 128:256] = t[R_SKIP : R_SKIP + 512, :].astype(bf16)
    part = lax.broadcasted_iota(jnp.int32, (64, 128), 1) // L
    for s in range(8):
        for c in range(C):
            rows = t[R_DEC + 64 * c : R_DEC + 64 * c + 64, :]
            rows = pltpu.roll(rows, (-L * s) % 128, 1)
            wd[pl.ds(512 * c + s, 64, stride=8), :] = jnp.where(part == 0, rows, 0.0)
    w_dect[...] = (0.5 * wd[...].T[0:L, :]).astype(bf16)
    micro, frames, _ = x_ref.shape
    nb = frames // BLK
    sums = {}
    for m in range(micro):
        for b in range(nb):
            half = mm(x_ref[m, b * BLK : (b + 1) * BLK, :], w_in[...])
            u = half + half * jnp.tanh(half)
            first = jnp.sum(jnp.sum(u, axis=0, keepdims=True), axis=1, keepdims=True)
            second = jnp.sum(jnp.sum(u * u, axis=0, keepdims=True), axis=1, keepdims=True)
            sums[(m * nb + b) * KINDS] = first
            sums[(m * nb + b) * KINDS + 1] = second
    row = stat_rows(sums, (1, 128))
    stats[...] = jnp.broadcast_to(row[None], stats.shape)


def unpack(pos, parts, feats, n_dev):
    outs = (
        jax.ShapeDtypeStruct((B, HW), bf16),
        jax.ShapeDtypeStruct((HW, B + SC), bf16),
        jax.ShapeDtypeStruct((SC, C * N), bf16),
        jax.ShapeDtypeStruct((L, C * N), bf16),
        jax.ShapeDtypeStruct((8, HW), f32),
        jax.ShapeDtypeStruct((n_dev, 1, 128), f32),
    )
    return pl.pallas_call(
        functools.partial(unpack_kernel, len(parts)),
        out_shape=outs,
        in_specs=[smem()] + [vmem()] * (1 + len(parts)),
        out_specs=tuple(vmem() for _ in outs),
        scratch_shapes=[
            pltpu.VMEM((len(parts) * parts[0].shape[0], 128), f32),
            pltpu.VMEM((ROWS_ALL, 128), f32),
            pltpu.VMEM((C * N, 128), f32),
        ],
        compiler_params=pltpu.CompilerParams(vmem_limit_bytes=16 * MIB),
        name="unpack",
    )(pos, feats, *parts)


class Segments:
    def __init__(self, seg_ref, me_ref, micro, nb, n_dev):
        self.seg_ref, self.micro, self.nb, self.n_dev = seg_ref, micro, nb, n_dev
        self.bounds, self.here, self.same = [], [], []
        for m in range(micro):
            bounds, total = [], 0
            for k in range(SEGS):
                total = total + seg_ref[m, k]
                bounds.append(total)
            here = []
            for o in range(-1, nb + 1):
                at = (me_ref[0] * nb + o) * BLK
                here.append(functools.reduce(lambda p, q: p + q, [jnp.where(at >= k, 1, 0) for k in bounds]))
            start, end = me_ref[0] * nb, me_ref[0] * nb + nb
            same = [jnp.where(p == q, 1.0, 0.0).astype(f32) for p, q in zip(here[:-1], here[1:])]
            same[0] = jnp.where(start > 0, same[0], 0.0)
            same[-1] = jnp.where(end < n_dev * nb, same[-1], 0.0)
            self.bounds.append(bounds)
            self.here.append([jnp.minimum(h, SEGS - 1) for h in here])
            self.same.append(same)
        lane = lax.broadcasted_iota(jnp.int32, (1, 128), 1)
        self.lane_micro = lane // (KINDS * nb)
        start = lax.broadcasted_iota(jnp.int32, (n_dev, 128), 0) * nb
        start = (start + (lax.broadcasted_iota(jnp.int32, (n_dev, 128), 1) // KINDS) % nb) * BLK
        self.ids = jnp.zeros((n_dev, 128), jnp.int32)
        for k in range(SEGS - 1):
            bound = self.by_micro([b[k] for b in self.bounds])
            self.ids = self.ids + jnp.where(start >= bound, 1, 0)
        lengths = self.rows([self.by_micro([seg_ref[m, k] for m in range(micro)]) for k in range(SEGS)])
        self.inverse = 1.0 / (lengths.astype(f32) * HW)

    def by_micro(self, values):
        out = jnp.full((1, 128), values[0], jnp.int32)
        for m in range(1, self.micro):
            out = jnp.where(self.lane_micro == m, values[m], out)
        return out

    def rows(self, values):
        at = lax.broadcasted_iota(jnp.int32, (SEGS, 128), 0)
        out = jnp.broadcast_to(values[0], (SEGS, 128))
        for k in range(1, SEGS):
            out = jnp.where(at == k, values[k], out)
        return out

    def means(self, stats):
        sums = self.rows(
            [row_sum(fold_rows(jnp.where(self.ids == k, stats, 0.0))) for k in range(SEGS)]
        )
        total = sums
        for b in range(1, self.nb):
            total = total + pltpu.roll(sums, 128 - b * KINDS, 1)
        return total * self.inverse

    def norm(self, stats):
        mean = self.means(stats)
        factor = lax.rsqrt(pltpu.roll(mean, 127, 1) - mean * mean + norm_eps)
        return mean, factor

    def pick(self, ref, m, o):
        at = m * self.nb * KINDS
        return ref[pl.ds(self.here[m][o], 1), :][:, at : at + 1]

    def taps(self, vec, m, h):
        k0, k2 = vec[4:5, :], vec[6:7, :]
        lo = k0 * self.same[m][h // 2 - 1] if h % 2 == 0 else k0
        hi = k2 if h % 2 == 0 else k2 * self.same[m][h // 2]
        return lo, hi


def depth_kernel(
    me_ref, seg_ref, stats_ref, x_ref, near_ref, far_ref, w_in, vec, d_ref, edge_ref, out_stats, tab, par, a_s, n_s
):
    micro, frames, _ = x_ref.shape
    nb = frames // BLK
    even = me_ref[0] % 2 == 0
    g1, b1 = 1.0 + vec[0:1, :], vec[1:2, :]
    lane = lax.broadcasted_iota(jnp.int32, (1, 128), 1)

    def project(m, slot):
        def side(at, first):
            near, far = near_ref[m, 0:BLK, :], far_ref[m, 0:BLK, :]
            a_s[slot, at : at + BLK, :] = mm(jnp.where(even == first, far, near), w_in[...])

        def main(c):
            cols = slice(c, c + HALF_W)
            a_s[slot, BLK : BLK + frames, cols] = mm(x_ref[m], w_in[:, cols])

        steps = [functools.partial(main, c) for c in range(0, HW, HALF_W)]
        return steps + [
            functools.partial(side, 0, True),
            functools.partial(side, BLK + frames, False),
        ]

    def body(m, slot, row):
        def normed(h, cols):
            o = h // 2
            scale, shift = par[m, 0, o : o + 1, cols], par[m, 1, o : o + 1, cols]
            for r in range(h * DIL, (h + 1) * DIL, ROWS):
                half = a_s[slot, r : r + ROWS, cols]
                u = half + half * jnp.tanh(half)
                n_s[r : r + ROWS, cols] = (u * scale + shift).astype(bf16).astype(f32)

        totals = {b: [0.0, 0.0] for b in range(nb)}

        def conv(h, cols):
            lo, hi = par[m, 2, h : h + 1, cols], par[m, 3, h : h + 1, cols]
            k1, kb = 0.5 * vec[5:6, cols], 0.5 * vec[7:8, cols]
            first = second = jnp.zeros((8, LANES), f32)
            for r in range(0, DIL, ROWS):
                at = h * DIL + r
                half = (
                    lo * n_s[at - DIL : at - DIL + ROWS, cols]
                    + k1 * n_s[at : at + ROWS, cols]
                    + hi * n_s[at + DIL : at + DIL + ROWS, cols]
                    + kb
                )
                if h == 1:
                    edge_ref[m, r : r + ROWS, cols] = half
                elif h == 2 * nb + 2:
                    edge_ref[m, DIL + r : DIL + r + ROWS, cols] = half
                else:
                    d_ref[m, at - BLK : at - BLK + ROWS, cols] = half
                    v = half + half * jnp.tanh(half)
                    first = first + fold_rows(v)
                    second = second + fold_rows(v * v)
            if 2 <= h < 2 * nb + 2:
                total = totals[h // 2 - 1]
                total[0] = total[0] + first
                total[1] = total[1] + second

        work = [functools.partial(normed, *t) for t in tiles_of(range(2 * nb + 4))]
        work += [functools.partial(conv, *t) for t in tiles_of(range(1, 2 * nb + 3))]
        weave(project(jnp.minimum(m + 1, micro - 1), 1 - slot), work)
        for b, total in totals.items():
            for k, val in enumerate(total):
                val = jnp.sum(row_sum(val), axis=1, keepdims=True)
                row = jnp.where(lane == (m * nb + b) * KINDS + k, val, row)
        return row

    seg = Segments(seg_ref, me_ref, micro, nb, stats_ref.shape[0])
    tab[0], tab[1] = seg.norm(stats_ref[:, 0, :])
    for m in range(micro):
        for o in range(nb + 2):
            scale = seg.pick(tab.at[1], m, o) * g1
            par[m, 0, o : o + 1, :] = scale
            par[m, 1, o : o + 1, :] = b1 - seg.pick(tab.at[0], m, o) * scale
        for h in range(1, 2 * nb + 3):
            lo, hi = seg.taps(vec, m, h)
            par[m, 2, h : h + 1, :] = 0.5 * lo
            par[m, 3, h : h + 1, :] = 0.5 * hi
    for step in project(0, 0):
        step()
    row = loop(micro, body, jnp.zeros((1, 128), f32))
    out_stats[...] = jnp.broadcast_to(row[None], out_stats.shape)


def depth(me, lengths, stats, feats, near, far, w_in, vec):
    micro, frames, _ = feats.shape
    return pl.pallas_call(
        depth_kernel,
        out_shape=(
            jax.ShapeDtypeStruct((micro, frames, HW), f32),
            jax.ShapeDtypeStruct((micro, 2 * DIL, HW), f32),
            jax.ShapeDtypeStruct(stats.shape, f32),
        ),
        in_specs=[smem(), smem()] + [vmem()] * 6,
        out_specs=(vmem(),) * 3,
        scratch_shapes=[
            pltpu.VMEM((2, SEGS, 128), f32),
            pltpu.VMEM((micro, 4, 8, HW), f32),
            pltpu.VMEM((2, frames + 2 * BLK, HW), f32),
            pltpu.VMEM((frames + 2 * BLK, HW), f32),
        ],
        compiler_params=pltpu.CompilerParams(vmem_limit_bytes=DEPTH_MIB * MIB),
        name="depth",
    )(me, lengths, stats, feats, near, far, w_in, vec)


def head_kernel(
    me_ref,
    seg_ref,
    stats_ref,
    d_ref,
    x_ref,
    enc_ref,
    dy_ref,
    own_ref,
    other_ref,
    w_rs,
    w_mask,
    w_dect,
    vec,
    block_ref,
    wave_own_ref,
    wave_other_ref,
    ds_ref,
    out_stats,
    g_rs,
    g_mask,
    g_dec,
    g_vec,
    tab,
    par,
    sums,
    ends,
    n2_s,
    v_s,
    sd_s,
    z_s,
    slope_s,
    dys_s,
    q_s,
    gm_s,
    e_s,
    dq_s,
    dz_s,
    dn2_s,
    dw_s,
    wave_s,
):
    micro, frames, _ = d_ref.shape
    nb = frames // BLK
    halves = 2 * nb
    for ref in (g_rs, g_mask, g_dec, g_vec):
        ref[...] = jnp.zeros_like(ref)
    core = me_ref[0] % 2
    ours = pl.ds(pl.multiple_of(core * frames, BLK), frames)
    lane = lax.broadcasted_iota(jnp.int32, (1, 128), 1)
    seg = Segments(seg_ref, me_ref, micro, nb, stats_ref.shape[0])
    tab[0], tab[1] = seg.norm(stats_ref[:, 0, :])
    for m in range(micro):
        means = [seg.pick(tab.at[0], m, o) for o in range(nb + 1)]
        factors = [seg.pick(tab.at[1], m, o) for o in range(nb + 1)]
        for h in range(halves):
            o = 1 + h // 2
            scale = factors[o] * (1.0 + vec[2:3, :])
            lo, hi = seg.taps(vec, m, h + 2)
            rows = (
                scale,
                vec[3:4, :] - means[o] * scale,
                jnp.broadcast_to(means[o], (1, HW)),
                jnp.broadcast_to(factors[o], (1, HW)),
                vec[5:6, :] + lo + hi,
            )
            for k, v in enumerate(rows):
                par[m, k, h : h + 1, :] = v

    def norm_steps(m, slot):
        def step(h, cols):
            scale, shift = par[m, 0, h : h + 1, cols], par[m, 1, h : h + 1, cols]
            s0 = s1 = c0 = c1 = jnp.zeros((8, LANES), f32)
            for r in range(h * DIL, (h + 1) * DIL, ROWS):
                rows = slice(r, r + ROWS)
                half = d_ref[m, rows, cols]
                v, sd = slope_parts(half, jnp.tanh(half))
                n2_s[slot, rows, cols] = (v * scale + shift).astype(bf16)
                v_s[slot, rows, cols] = v
                sd_s[slot, rows, cols] = sd
                cv = v * sd
                s0 = s0 + fold_rows(sd)
                s1 = s1 + fold_rows(sd * half)
                c0 = c0 + fold_rows(cv)
                c1 = c1 + fold_rows(cv * half)
            for k, v in enumerate((s0, s1, c0, c1)):
                sums[slot, k, h : h + 1, cols] = row_sum(v)

        return [functools.partial(step, *t) for t in tiles_of(range(halves))]

    def end_steps(m, slot):
        def step(h, cols):
            sum_d = sum_dv = a0 = a1 = jnp.zeros((8, LANES), f32)
            for r in range(h * DIL, (h + 1) * DIL, ROWS):
                rows = slice(r, r + ROWS)
                dn2 = dn2_s[rows, cols]
                a = dn2 * sd_s[slot, rows, cols]
                sum_d = sum_d + fold_rows(dn2)
                sum_dv = sum_dv + fold_rows(dn2 * v_s[slot, rows, cols])
                a0 = a0 + fold_rows(a)
                a1 = a1 + fold_rows(a * d_ref[m, rows, cols])
            for k, v in enumerate((sum_d, sum_dv, a0, a1)):
                ends[k, h : h + 1, cols] = row_sum(v)

        return [functools.partial(step, *t) for t in tiles_of(range(halves))]

    def end_row(m, at, slot, row, valid):
        scale, _, mean, factor, kappa = [par[m, k, 0:halves, :] for k in range(5)]
        s0, s1, c0, c1 = [sums[slot, k, 0:halves, :] for k in range(4)]
        sum_d, sum_dv, a0, a1 = [ends[k, 0:halves, :] for k in range(4)]
        g1, g2 = 1.0 + vec[0:1, :], 1.0 + vec[2:3, :]
        gain = (sum_dv - mean * sum_d) * factor
        g_vec[2:3, :] += jnp.where(valid, row_sum(gain), 0.0)
        g_vec[3:4, :] += jnp.where(valid, row_sum(sum_d), 0.0)
        vw = g1 * kappa
        delta = vec[7:8, :] + vec[1:2, :] * kappa
        a0, a1 = 0.5 * a0 * scale, a1 * scale
        s0, s1 = 0.5 * s0 * factor, s1 * factor
        c0 = 0.5 * c0 * factor * factor - mean * factor * s0
        c1 = c1 * factor * factor - mean * factor * s1
        vals = (
            sum_d * g2,
            gain * g2,
            vw * a0,
            vw * s0,
            vw * c0,
            a1 - delta * a0,
            s1 - delta * s0,
            c1 - delta * c0,
        )
        for k, val in enumerate(vals):
            val = jnp.sum(val, axis=1, keepdims=True)
            for b in range(nb):
                two = val[2 * b : 2 * b + 1, :] + val[2 * b + 1 : 2 * b + 2, :]
                row = jnp.where(lane == at + b * KINDS + k, two, row)
        return row

    def body(m, slot, row):
        later, before = min(m + 1, micro - 1), max(m - 1, 0)
        own, other = own_ref[m, :, ours], other_ref[m, :, ours]
        dw_s[slot, 0] = jnp.where(core == 0, own, other)
        dw_s[slot, 1] = jnp.where(core == 0, other, own)
        ahead = norm_steps(later, 1 - slot)

        def skip():
            rows = slice(0, frames)
            ys = mm(n2_s[slot, rows, :], w_rs[...])
            block_ref[m, rows, :] = (x_ref[m, rows, :].astype(f32) + ys[:, 0:B]).astype(bf16)
            half = 0.5 * ys[:, B : B + SC]
            z, slope = slope_parts(half, jnp.tanh(half))
            z_s[rows, :] = z.astype(bf16)
            slope_s[rows, :] = slope

        def logits(k, c):
            cols = slice(k * N + c, k * N + c + HALF_W)
            q_s[k, :, c : c + HALF_W] = mm(z_s[...], w_mask[:, cols])

        def back(k, c):
            cols = slice(k * N + c, k * N + c + HALF_W)
            gm_s[k, :, c : c + HALF_W] = mm_rows(dw_s[slot, k], w_dect[:, cols])

        def masked(k, h, cols):
            for r in range(h * DIL, (h + 1) * DIL, ROWS):
                rows = slice(r, r + ROWS)
                t = jnp.tanh(q_s[k, rows, cols])
                pe = (0.5 * t + 0.5) * enc_ref[m, rows, cols].astype(f32)
                e_s[k, rows, cols] = pe.astype(bf16)
                dq_s[k, rows, cols] = (gm_s[k, rows, cols] * (pe * (1.0 - t))).astype(bf16)

        def wave(k):
            cols = slice(k * N, (k + 1) * N)
            wave_s[k] = (2.0 * mm_t(w_dect[:, cols], e_s[k])).astype(bf16)

        def gated(k):
            cols = slice(k * N, (k + 1) * N)
            rows = slice(0, frames)
            part = mm_t(dq_s[k, rows, :], w_mask[:, cols])
            dz_s[rows, :] = part if k == 0 else dz_s[rows, :] + part

        def dec_grad(k):
            cols = slice(k * N, (k + 1) * N)
            g_dec[:, cols] += mm(dw_s[slot, k], e_s[k])

        def mask_grad(k, c):
            cols = slice(k * N + c, k * N + c + HALF_W)
            g_mask[:, cols] += mm_rows(z_s[...], dq_s[k, :, c : c + HALF_W])

        def norm_back(c):
            dn2_s[:, c : c + HALF_W] = mm_t(dys_s[...], w_rs[c : c + HALF_W, :])

        def out_grad(c):
            g_rs[:, c : c + HALF_W] += mm_rows(dys_s[...], n2_s[slot, :, c : c + HALF_W])

        part = functools.partial
        wide = range(0, HW, HALF_W)
        third = len(ahead) // 3

        def ups(k):
            return [part(logits, k, c) for c in wide] + [part(back, k, c) for c in wide]

        def elementwise(k):
            return [part(masked, k, *t) for t in tiles_of(range(halves))]

        def downs(k):
            return (
                [part(gated, k)]
                + [part(mask_grad, k, c) for c in wide]
                + [part(wave, k), part(dec_grad, k)]
            )

        weave([skip], end_steps(before, 1 - slot))
        row = end_row(before, (m - 1) * nb * KINDS, 1 - slot, row, m > 0)
        weave(ups(0), ahead[:third])
        weave(ups(1), elementwise(0))
        weave(downs(0), elementwise(1))
        weave(downs(1), ahead[third : 2 * third])
        wave_own_ref[m] = jnp.where(core == 0, wave_s[0], wave_s[1])
        wave_other_ref[m] = jnp.where(core == 0, wave_s[1], wave_s[0])
        ds = (dz_s[...] * slope_s[...]).astype(bf16)
        ds_ref[m] = ds
        dys_s[:, 0:B] = dy_ref[m]
        dys_s[:, B : B + SC] = ds
        weave([part(norm_back, c) for c in wide] + [part(out_grad, c) for c in wide], ahead[2 * third :])
        return row

    for step in norm_steps(0, 0):
        step()
    row = jnp.zeros((1, 128), f32)
    for m in range(micro):
        row = body(m, m % 2, row)
    last = micro - 1
    for step in end_steps(last, last % 2):
        step()
    row = end_row(last, last * nb * KINDS, last % 2, row, True)
    out_stats[...] = jnp.broadcast_to(row[None], out_stats.shape)


def head(me, lengths, stats, d, feats, enc, dy, own, other, w_rs, w_mask, w_dect, vec):
    micro, frames, _ = feats.shape
    outs = (
        (feats.shape, bf16),
        ((micro, L, frames), bf16),
        ((micro, L, frames), bf16),
        ((micro, frames, SC), bf16),
        (stats.shape, f32),
        ((B + SC, HW), f32),
        ((SC, C * N), f32),
        ((L, C * N), f32),
        ((8, HW), f32),
    )
    return pl.pallas_call(
        head_kernel,
        in_specs=[smem(), smem()] + [vmem()] * 11,
        out_specs=(vmem(),) * len(outs),
        scratch_shapes=[
            pltpu.VMEM((2, SEGS, 128), f32),
            pltpu.VMEM((micro, 5, 8, HW), f32),
            pltpu.VMEM((2, 4, 8, HW), f32),
            pltpu.VMEM((4, 8, HW), f32),
            pltpu.VMEM((2, frames, HW), bf16),
            pltpu.VMEM((2, frames, HW), f32),
            pltpu.VMEM((2, frames, HW), f32),
            pltpu.VMEM((frames, SC), bf16),
            pltpu.VMEM((frames, SC), f32),
            pltpu.VMEM((frames, B + SC), bf16),
            pltpu.VMEM((C, frames, N), f32),
            pltpu.VMEM((C, frames, N), f32),
            pltpu.VMEM((C, frames, N), bf16),
            pltpu.VMEM((C, frames, N), bf16),
            pltpu.VMEM((frames, SC), f32),
            pltpu.VMEM((frames, HW), f32),
            pltpu.VMEM((2, C, L, frames), bf16),
            pltpu.VMEM((C, L, frames), bf16),
        ],
        out_shape=tuple(jax.ShapeDtypeStruct(s, t) for s, t in outs),
        compiler_params=pltpu.CompilerParams(vmem_limit_bytes=HEAD_MIB * MIB),
        name="head",
    )(me, lengths, stats, d, feats, enc, dy, own, other, w_rs, w_mask, w_dect, vec)


def back_means(seg, stats):
    v = seg.means(stats)
    w = [v] + [pltpu.roll(v, 128 - k, 1) for k in range(1, KINDS)]
    p2, q2 = w[0], w[1]
    return p2, q2, w[2] - p2 * w[3] - q2 * w[4], w[5] - p2 * w[6] - q2 * w[7]


def input_kernel(
    me_ref,
    seg_ref,
    stats1_ref,
    stats2_ref,
    stats3_ref,
    d_ref,
    edge_ref,
    x_ref,
    dy_ref,
    dy_near,
    dy_far,
    ds_ref,
    ds_near,
    ds_far,
    w_in,
    w_rs,
    vec,
    feats_ref,
    g_in,
    g_vec,
    tab,
    par2,
    par1,
    col_s,
    dn2_s,
    dd_s,
    a_s,
    da_s,
):
    micro, frames, _ = d_ref.shape
    nb = frames // BLK
    halves = 2 * nb
    part = functools.partial
    for ref in (g_in, g_vec):
        ref[...] = jnp.zeros_like(ref)
    even = me_ref[0] % 2 == 0
    halo = slice(BLK, BLK + DIL)
    g1, g2 = 1.0 + vec[0:1, :], 1.0 + vec[2:3, :]
    seg = Segments(seg_ref, me_ref, micro, nb, stats1_ref.shape[0])
    tables = seg.norm(stats1_ref[:, 0, :]) + seg.norm(stats2_ref[:, 0, :])
    for k, table in enumerate(tables + back_means(seg, stats3_ref[:, 0, :])):
        tab[k] = table
    for m in range(micro):
        mean1, factor1, mean2, factor2, p2, q2, p1, q1 = [
            [seg.pick(tab.at[k], m, o) for o in range(nb + 2)] for k in range(8)
        ]
        for o in range(nb + 2):
            slope = 0.5 * factor2[o] * factor2[o] * q2[o]
            shift = 0.5 * factor2[o] * p2[o] - slope * mean2[o]
            rows = ((0.5 * factor2[o]) * g2, slope, shift)
            for k, v in enumerate(rows):
                par2[m, k, o : o + 1, :] = jnp.broadcast_to(v, (1, HW))
        for b in range(nb):
            o = b + 1
            scale = factor1[o] * g1
            slope = 0.5 * factor1[o] * factor1[o] * q1[o]
            rows = (
                scale,
                vec[1:2, :] - mean1[o] * scale,
                slope,
                0.5 * factor1[o] * p1[o] - slope * mean1[o],
                mean1[o],
                factor1[o],
                vec[4:5, :] * seg.same[m][o],
                vec[6:7, :] * seg.same[m][o - 1],
                seg.same[m][o],
                seg.same[m][o - 1],
            )
            for k, v in enumerate(rows):
                par1[m, k, b : b + 1, :] = jnp.broadcast_to(v, (1, HW))

    def project(m, slot):
        def side(at, first):
            near = jnp.concatenate([dy_near[m, halo, :], ds_near[m]], axis=1)
            far = jnp.concatenate([dy_far[m, halo, :], ds_far[m]], axis=1)
            dn2_s[at : at + DIL, :] = mm_t(jnp.where(even == first, far, near), w_rs[...])

        def main(c):
            dys = jnp.concatenate([dy_ref[m], ds_ref[m]], axis=1)
            dn2_s[DIL : DIL + frames, c : c + HALF_W] = mm_t(dys, w_rs[c : c + HALF_W, :])

        def hidden(c):
            a_s[slot, :, c : c + HALF_W] = mm(x_ref[m], w_in[:, c : c + HALF_W])

        wide = range(0, HW, HALF_W)
        return (
            [part(main, c) for c in wide]
            + [part(side, 0, True), part(side, DIL + frames, False)]
            + [part(hidden, c) for c in wide]
        )

    def depth_steps(m):
        def step(h, cols):
            o = (h + 1) // 2
            scale, slope, shift = [par2[m, k, o : o + 1, cols] for k in range(3)]
            total = jnp.zeros((8, LANES), f32)
            for r in range(0, DIL, ROWS):
                at = h * DIL + r
                if h == 0:
                    half = edge_ref[m, r : r + ROWS, cols]
                elif h == halves + 1:
                    half = edge_ref[m, DIL + r : DIL + r + ROWS, cols]
                else:
                    half = d_ref[m, at - DIL : at - DIL + ROWS, cols]
                v, sd = slope_parts(half, jnp.tanh(half))
                rows = slice(at, at + ROWS)
                dd = (sd * (dn2_s[rows, cols] * scale - v * slope - shift)).astype(bf16).astype(f32)
                dd_s[rows, cols] = dd
                total = total + fold_rows(dd)
            col_s[h : h + 1, cols] = row_sum(total)

        return [part(step, *t) for t in tiles_of(range(halves + 2))]

    def hidden_steps(m, slot):
        def step(h, cols):
            b = h // 2
            scale, shift, slope, base, mean, factor, k0, k2, hi, lo = [
                par1[m, k, b : b + 1, cols] for k in range(10)
            ]
            k1 = vec[5:6, cols]
            if h % 2 == 0:
                k0, hi = vec[4:5, cols], 1.0
            else:
                k2, lo = vec[6:7, cols], 1.0
            half_scale = 0.5 * scale
            s0 = s1 = s2 = jnp.zeros((8, LANES), f32)
            for r in range(h * DIL, (h + 1) * DIL, ROWS):
                prev, here, nxt = [dd_s[r + q * DIL : r + q * DIL + ROWS, cols] for q in range(3)]
                half = a_s[slot, r : r + ROWS, cols]
                u, su = slope_parts(half, jnp.tanh(half))
                n1 = (u * scale + shift).astype(bf16).astype(f32)
                s0 = s0 + fold_rows(nxt * n1)
                s1 = s1 + fold_rows(here * n1)
                s2 = s2 + fold_rows(prev * n1)
                dn1 = k1 * here + k0 * nxt + k2 * prev
                du = dn1 * half_scale - u * slope - base
                da_s[r : r + ROWS, cols] = (du * su).astype(bf16)
            s0, s1, s2 = [row_sum(v) for v in (s0, s1, s2)]
            prev, here, nxt = [col_s[h + q : h + q + 1, cols] for q in range(3)]
            dn1 = k1 * here + k0 * nxt + k2 * prev
            dn1_u = (k1 * s1 + k0 * s0 + k2 * s2 - shift * dn1) / scale
            rows = (
                (0, (dn1_u - mean * dn1) * factor),
                (1, dn1),
                (4, s0 * hi),
                (5, s1),
                (6, s2 * lo),
                (7, here),
            )
            for k, v in rows:
                g_vec[k : k + 1, cols] += v

        return [part(step, *t) for t in tiles_of(range(halves))]

    def last_steps(m):
        def weight(c):
            g_in[:, c : c + HALF_W] += mm_rows(x_ref[m], da_s[:, c : c + HALF_W])

        def feats(r):
            rows = slice(r, r + BLK)
            grad = dy_ref[m, rows, :].astype(f32) + 2.0 * mm_t(da_s[rows, :], w_in[...])
            feats_ref[m, rows, :] = grad.astype(bf16)

        return [part(weight, c) for c in range(0, HW, HALF_W)] + [
            part(feats, r) for r in range(0, frames, BLK)
        ]

    def body(m, slot, carry):
        run(project(m, 0) + depth_steps(m) + hidden_steps(m, 0) + last_steps(m))
        return carry

    lax.fori_loop(0, micro, lambda m, c: body(m, 0, c), 0)


def input_grad(me, lengths, stats, d, edge, feats, dy, near, far, ds, ds_near, ds_far, w_in, w_rs, vec):
    micro, frames, _ = d.shape
    return pl.pallas_call(
        input_kernel,
        out_shape=(
            jax.ShapeDtypeStruct(feats.shape, bf16),
            jax.ShapeDtypeStruct((B, HW), f32),
            jax.ShapeDtypeStruct((8, HW), f32),
        ),
        in_specs=[smem(), smem()] + [vmem()] * 15,
        out_specs=(vmem(),) * 3,
        scratch_shapes=[
            pltpu.VMEM((8, SEGS, 128), f32),
            pltpu.VMEM((micro, 3, 8, HW), f32),
            pltpu.VMEM((micro, 10, 8, HW), f32),
            pltpu.VMEM((8, HW), f32),
            pltpu.VMEM((frames + 2 * DIL, HW), f32),
            pltpu.VMEM((frames + 2 * DIL, HW), f32),
            pltpu.VMEM((2, frames, HW), f32),
            pltpu.VMEM((frames, HW), bf16),
        ],
        compiler_params=pltpu.CompilerParams(vmem_limit_bytes=INPUT_MIB * MIB),
        name="input_grad",
    )(me, lengths, *stats, d, edge, feats, dy, near, far, ds, ds_near, ds_far, w_in, w_rs, vec)


def pack_kernel(pos_ref, g_in, g_rs, g_mask, g_dec, vec_a, vec_b, keep_ref, send_ref, t, out, wd):
    for k in range(4):
        cols = slice(128 * k, 128 * k + 128)
        t[pl.ds(R_IN + k, 128, stride=4), :] = g_in[:, cols]
        for c in range(C):
            t[pl.ds(R_MASK + 512 * c + k, 128, stride=4), :] = g_mask[
                :, 512 * c + 128 * k : 512 * c + 128 * k + 128
            ]
        t[pl.ds(R_VEC + k, 8, stride=4), :] = vec_a[:, cols] + vec_b[:, cols]
    t[R_RES : R_RES + 512, :] = g_rs[0:128, :].T
    t[R_SKIP : R_SKIP + 512, :] = g_rs[128:256, :].T
    wd[...] = jnp.concatenate([g_dec[...], jnp.zeros((128 - L, C * N), f32)], axis=0).T
    part = lax.broadcasted_iota(jnp.int32, (64, 128), 1) // L
    for c in range(C):
        rows = jnp.zeros((64, 128), f32)
        for s in range(8):
            piece = pltpu.roll(wd[pl.ds(512 * c + s, 64, stride=8), :], L * s, 1)
            rows = jnp.where(part == s, piece, rows)
        t[R_DEC + 64 * c : R_DEC + 64 * c + 64, :] = rows
    out[...] = jnp.zeros_like(out)
    for i in range(NCH):
        start = pl.multiple_of(pos_ref[i] * 8, 8)
        out[pl.ds(start, 8), :] = t[8 * i : 8 * i + 8, :]
    half = keep_ref.shape[0]
    keep_ref[...] = out[0:half, :]
    send_ref[...] = out[half : 2 * half, :].astype(bf16)


def pack(pos, g_in, g_rs, g_mask, g_dec, vec_a, vec_b, rows):
    return pl.pallas_call(
        pack_kernel,
        out_shape=(
            jax.ShapeDtypeStruct((rows // 2, 128), f32),
            jax.ShapeDtypeStruct((rows // 2, 128), bf16),
        ),
        in_specs=[smem()] + [vmem()] * 6,
        out_specs=(vmem(), vmem()),
        scratch_shapes=[
            pltpu.VMEM((ROWS_ALL, 128), f32),
            pltpu.VMEM((rows, 128), f32),
            pltpu.VMEM((C * N, 128), f32),
        ],
        compiler_params=pltpu.CompilerParams(vmem_limit_bytes=16 * MIB),
        name="pack",
    )(pos, g_in, g_rs, g_mask, g_dec, vec_a, vec_b)


def fold_kernel(n_got, n_next, *refs):
    keep_ref, got = refs[0], refs[1 : 1 + n_got]
    outs = refs[1 + n_got :]
    total = keep_ref[...]
    for g in got:
        total = total + g[...].astype(f32)
    size = total.shape[0] // n_next
    outs[0][...] = total[0:size, :]
    for q in range(1, n_next):
        outs[q][...] = total[q * size : (q + 1) * size, :].astype(bf16)


def fold(keep, got, n_next):
    size = keep.shape[0] // n_next
    outs = [jax.ShapeDtypeStruct((size, 128), f32)]
    outs += [jax.ShapeDtypeStruct((size, 128), bf16)] * (n_next - 1)
    return pl.pallas_call(
        functools.partial(fold_kernel, len(got), n_next),
        out_shape=tuple(outs),
        in_specs=[vmem()] * (1 + len(got)),
        out_specs=tuple(vmem() for _ in outs),
        compiler_params=pltpu.CompilerParams(vmem_limit_bytes=8 * MIB),
        name="fold",
    )(keep, *got)


def adam_kernel(n_got, count_ref, *refs):
    keep_ref, got = refs[0], refs[1 : 1 + n_got]
    master_ref, one_ref, two_ref, new_master, new_one, new_two, buf = refs[1 + n_got :]
    total = keep_ref[...]
    for g in got:
        total = total + g[...].astype(f32)
    buf[...] = total
    slots = master_ref.shape[0]
    used = lax.broadcasted_iota(jnp.int32, (slots, 128), 0) < count_ref[0]
    for j in range(8):
        cols = slice(128 * j, 128 * j + 128)
        grad = buf[pl.ds(j, slots, stride=8), :]
        master = master_ref[:, cols]
        one = beta_one * one_ref[:, cols] + (1.0 - beta_one) * grad
        two = beta_two * two_ref[:, cols] + (1.0 - beta_two) * grad * grad
        unbias_one = one / (1.0 - beta_one**STEP)
        unbias_two = two / (1.0 - beta_two**STEP)
        new = master - learn_rate * (
            unbias_one / (jnp.sqrt(unbias_two) + adam_eps) + weight_decay * master
        )
        new_master[:, cols] = jnp.where(used, new, 0.0)
        new_one[:, cols] = jnp.where(used, one, 0.0)
        new_two[:, cols] = jnp.where(used, two, 0.0)


def adam(count, keep, got, master, one, two):
    out = jax.ShapeDtypeStruct(master.shape, f32)
    return pl.pallas_call(
        functools.partial(adam_kernel, len(got)),
        out_shape=(out, out, out),
        in_specs=[smem()] + [vmem()] * (4 + len(got)),
        out_specs=(vmem(), vmem(), vmem()),
        scratch_shapes=[pltpu.VMEM(keep.shape, f32)],
        compiler_params=pltpu.CompilerParams(vmem_limit_bytes=4 * MIB),
        name="adam",
    )(count, keep, *got, master, one, two)


def local(n_tm, n_src, feats, encoded, seg_lengths, owners, master, moment_one, moment_two, out_cot, wave_cot):
    n_dev = n_tm * n_src
    me = lax.axis_index(AXES)
    core = lax.axis_index("src")
    micro, frames, _ = feats.shape
    nb = frames // BLK
    slots = master.shape[0]


    across = [(i, i + 1) for i in range(1, n_dev - 1, 2)]
    across = across + [(j, i) for i, j in across]

    def ends(at_end, *arrays):
        size = [jnp.where(at_end, v.shape[1] - w, 0) for v, w in arrays]
        rows = [lax.dynamic_slice_in_dim(v, at, w, axis=1) for (v, w), at in zip(arrays, size)]
        return rows[0] if len(rows) == 1 else jnp.concatenate(rows, axis=1)

    owner_ids = owners[:, 0]
    order = jnp.arange(NCH, dtype=jnp.int32)
    earlier = (owner_ids[:, None] == owner_ids[None, :]) & (order[None, :] < order[:, None])
    rank = jnp.sum(earlier.astype(jnp.int32), axis=1)
    pos = relative_block(owner_ids, me, n_dev) * slots + rank
    count = jnp.sum((owner_ids == me).astype(jnp.int32)).reshape(1)
    here = me.astype(jnp.int32).reshape(1)

    cot = jnp.transpose(wave_cot[:, 0], (0, 2, 1))
    halo = (feats, BLK), (out_cot, DIL)
    sides = ends(core == 0, *halo), ends(core == 1, *halo)
    parts, (pos, here, count), (near, far, cot_other) = gather_tiles(
        to_tiles(master), n_dev, (pos, here, count), (*sides, cot)
    )
    near = swap(near, 1, n_dev)
    far = lax.ppermute(far, AXES, across)
    cot_other = swap(cot_other, 1, n_dev)

    w_in, w_rs, w_mask, w_dect, vec, stats = unpack(pos, parts, feats, n_dev)
    stats1 = share_sums(stats, n_dev)
    stats1, near, far, cot_other = lax.optimization_barrier((stats1, near, far, cot_other))
    d, edge, stats = depth(here, seg_lengths, stats1, feats, near, far, w_in, vec)
    stats2 = share_sums(stats, n_dev)
    block_out, wave_own, wave_other, ds, stats, g_rs, g_mask, g_dec, vec_a = head(
        here, seg_lengths, stats2, d, feats, encoded, out_cot, cot, cot_other, w_rs, w_mask, w_dect, vec
    )
    stats3 = share_sums(stats, n_dev)
    ds_near = swap(ends(core == 0, (ds, DIL)), 1, n_dev)
    ds_far = lax.ppermute(ends(core == 1, (ds, DIL)), AXES, across)

    wave_got = swap(wave_other, 1, n_dev)
    waves = jnp.concatenate(
        [jnp.where(core == 0, wave_own, wave_got), jnp.where(core == 0, wave_got, wave_own)], axis=2
    )
    waves = jnp.transpose(waves, (0, 2, 1))[:, None]

    feats_grad, g_in, vec_b = input_grad(
        here, seg_lengths, (stats1, stats2, stats3), d, edge, feats, out_cot, near, far, ds, ds_near, ds_far, w_in, w_rs, vec
    )

    keep, send = pack(pos, g_in, g_rs, g_mask, g_dec, vec_a, vec_b, n_dev * slots * 8)
    received = [swap(send, 1, n_dev)]
    for bits in reversed(stages(n_dev)[:-1]):
        n_next = 1 << len(bits)
        keep, *sends = fold(keep, received, n_next)
        received = [swap(s, spread(bits, k + 1), n_dev) for k, s in enumerate(sends)]
    new_master, new_one, new_two = adam(count, keep, received, master, moment_one, moment_two)
    return block_out, feats_grad, waves, new_master, new_one, new_two


def solution(mesh):
    n_tm, n_src = mesh.shape["tm"], mesh.shape["src"]
    return jax.shard_map(
        functools.partial(local, n_tm, n_src),
        mesh=mesh,
        in_specs=(
            P(None, AXES, None),
            P(None, AXES, None),
            P(),
            P(),
            P(AXES, None),
            P(AXES, None),
            P(AXES, None),
            P(None, AXES, None),
            P(None, "src", "tm", None),
        ),
        out_specs=(
            P(None, AXES, None),
            P(None, AXES, None),
            P(None, "src", "tm", None),
            P(AXES, None),
            P(AXES, None),
            P(AXES, None),
        ),
        check_vma=False,
    )
```

time: 115 us -> 110 us (0.957)
  blocking collectives: 21.3 us -> 31.3 us
  waiting for transfers between devices: 19.5 us -> 12.1 us
  Pallas kernels: 41.7 us -> 35.6 us
  starting transfers between devices: 26.7 us -> 24.3 us
    all_to_all x2 -> x3, blocking collectives: 21.3 us -> 31.3 us  [share_sums(): return lax.all_to_all(rows, AXES, 0, 0, tiled=True)]
    all_to_all x1 -> x0, waiting for transfers between devices: 7.06 us -> none  [share_sums(): return lax.all_to_all(rows, AXES, 0, 0, tiled=True)]
    pallas_call x3, Pallas kernels: 36.3 us -> 30.4 us  [the longest x1 12.9 us: head(): pl.pallas_call(head_kernel, in_specs=[smem(), smem()] + [vmem()] * 11, ou...]
    all_to_all x1 -> x0, starting transfers between devices: 2.54 us -> none  [share_sums(): return lax.all_to_all(rows, AXES, 0, 0, tiled=True)]
  transfers between devices with their start and end apart: 24 -> 23, of which waited for: 12 -> 12; matrix products, arithmetic and copies ran while one was open for 3% -> 4% of each run, Pallas kernels for 9% -> 2%
where the time goes in v3:
time: 110 us; the launch traced here: 109 us
  Pallas kernels  35.6 us (32%)
  blocking collectives  31.3 us (28%)
  starting transfers between devices  24.3 us (22%)
  waiting for transfers between devices  12.1 us (11%)
  local copies, waits for them, and re-layouts  3.05 us (3%)
  other arithmetic  2.36 us (2%)
    all_to_all x3, blocking collectives, share_sums(): return lax.all_to_all(rows, AXES, 0, 0, tiled=True)  31.3 us
    ppermute x21, starting transfers between devices, swap(): return lax.ppermute(value, AXES, [(i, i ^ mask) for i in range(n_dev)])  22.9 us
    pallas_call x1, Pallas kernels, head(): pl.pallas_call(head_kernel, in_specs=[smem(), smem()] + [vmem()] * 11, ou...  12.9 us
    ppermute x21, waiting for transfers between devices, swap(): return lax.ppermute(value, AXES, [(i, i ^ mask) for i in range(n_dev)])  12.1 us
    pallas_call x1, Pallas kernels, input_grad(): pl.pallas_call(input_kernel, out_shape=(jax.ShapeDtypeStruct(feats.shape,...  11.6 us
    pallas_call x1, Pallas kernels, depth(): pl.pallas_call(depth_kernel, out_shape=(jax.ShapeDtypeStruct((micro, fram...  5.92 us
    pallas_call x1, Pallas kernels, unpack(): pl.pallas_call(functools.partial(unpack_kernel, len(parts)), out_shape=ou...  2.4 us
  transfers between devices with their start and end apart: 23, of which 12 were waited for; matrix products, arithmetic and copies ran while one was open for 4% of the time, Pallas kernels for 2%

profile of v3, /device:TPU:0, one launch (start us, length us, event | category | flops | bytes accessed | tf_op | source)
XLA Modules:
  0.0 109.5 jit_solution(4772105597669818534)
XLA Ops:
  0.7 0.9 copy-done.3
  1.6 5.1 %collective-permute-start.2 = (bf16[88,128]{1,0:T(8,128)(2,1)S(1)}, bf16[88,128]{1,0:T(8,128)(2,1)S(1)}, u32[]{:S(2)}, u32[]{:S(2)}) collective-permute-start(bf16[88,128]{1,0:T(8,128)(2,1)S(1)} %to_tiles.1), channel_id=1, source_target_pairs={{0,24},{1,25},{2,26},{3,27},{4,28},{5,29},{6,30},{7,31},{8,16},{9,... | collective-permute-start | bytes 67592 | tf_op jit(solution)/shard_map/ppermute | solution.py:122
  6.7 0.6 collective-permute-start
  7.3 0.7 reduce
  8.2 0.7 convert_reduce_fusion.1
  9.0 1.1 constant_dynamic-slice_fusion.3
  10.0 1.0 constant_dynamic-slice_fusion.2
  11.4 2.5 %collective-permute-start.5 = (bf16[352,128]{1,0:T(8,128)(2,1)S(1)}, bf16[352,128]{1,0:T(8,128)(2,1)S(1)}, u32[]{:S(2)}, u32[]{:S(2)}) collective-permute-start(bf16[352,128]{1,0:T(8,128)(2,1)S(1)} %constant_dynamic-update-slice_fusion.refs_0_), channel_id=1, source_target_pairs={{0,6},{1,7},{2,4},{3,5},{4,2},{5,3},{6,0},{7,1},{8,14},{9,15},{10,... | collective-permute-start | bytes 270344 | tf_op jit(solution)/shard_map/ppermute | solution.py:122
  15.0 2.5 %collective-permute-done.5.refs_3_ = bf16[352,128]{1,0:T(8,128)(2,1)S(1)} collective-permute-done((bf16[352,128]{1,0:T(8,128)(2,1)S(1)}, bf16[352,128]{1,0:T(8,128)(2,1)S(1)}, u32[]{:S(2)}, u32[]{:S(2)}) %collective-permute-start.5) | collective-permute-done | bytes 90144 | tf_op jit(solution)/shard_map/ppermute | solution.py:122
  17.5 1.0 collective-permute-done.4.refs_2_
  19.0 0.7 collective-permute-start.11
  19.7 2.1 %collective-permute-start.6 = (bf16[352,128]{1,0:T(8,128)(2,1)S(1)}, bf16[352,128]{1,0:T(8,128)(2,1)S(1)}, u32[]{:S(2)}, u32[]{:S(2)}) collective-permute-start(bf16[352,128]{1,0:T(8,128)(2,1)S(1)} %constant_dynamic-update-slice_fusion.refs_0_), channel_id=1, source_target_pairs={{0,1},{1,0},{2,3},{3,2},{4,5},{5,4},{6,7},{7,6},{8,9},{9,8},{10,11... | collective-permute-start | bytes 270344 | tf_op jit(solution)/shard_map/ppermute | solution.py:122
  23.2 0.8 collective-permute-done.8.refs_6_
  24.3 2.4 %unpack.1 = (bf16[128,512]{1,0:T(8,128)(2,1)S(1)}, bf16[512,256]{1,0:T(8,128)(2,1)S(1)}, bf16[128,1024]{1,0:T(8,128)(2,1)S(1)}, bf16[16,1024]{1,0:T(8,128)(2,1)S...) custom-call(s32[340]{0:T(512)S(1)} %get-tuple-element.59.pos_ref, bf16[4,512,128]{2,1,0:T(8,128)(2,1)S(1)} %copy-done, ...), custom_call_target="tpu_custom_call" | custom-call | tf_op jit(solution)/shard_map/unpack/pallas_call | solution.py:229
  26.7 12.7 %all_to_all.15.stats_ref.stats1_ref = f32[32,1,128]{2,1,0:T(1,128)S(1)} all-to-all(f32[32,1,128]{2,1,0:T(1,128)S(1)} %get-tuple-element.68), channel_id=1, replica_groups=mesh['tm'=16,'src'=2] {'tm','src'}, dimensions={0} | all-to-all | bytes 32768 | tf_op jit(solution)/shard_map/all_to_all | solution.py:148
  39.4 5.9 %depth.1 = (f32[4,512,512]{2,1,0:T(8,128)S(1)}, f32[4,256,512]{2,1,0:T(8,128)S(1)}, f32[32,1,128]{2,1,0:T(1,128)S(1)}) custom-call(s32[1]{0:T(128)} %bitcast.me_ref, s32[4,8]{1,0:T(4,128)S(1)} %copy-done.8, f32[32,1,128]{2,1,0:T(1,128)S(1)} %all_to_all.15.stats_ref.stats1_ref, bf16[4,512,128]{2,1,0:T(8,128)(2,1)S(1)} %copy-done, ...), custom_call_target="tpu_custom_call" | custom-call | tf_op jit(solution)/shard_map/depth/pallas_call | solution.py:402
  45.3 8.8 %all_to_all.16.stats_ref.stats2_ref = f32[32,1,128]{2,1,0:T(1,128)S(1)} all-to-all(f32[32,1,128]{2,1,0:T(1,128)S(1)} %get-tuple-element.77), channel_id=1, replica_groups=mesh['tm'=16,'src'=2] {'tm','src'}, dimensions={0} | all-to-all | bytes 32768 | tf_op jit(solution)/shard_map/all_to_all | solution.py:148
  54.2 12.9 %head.1 = (bf16[4,512,128]{2,1,0:T(8,128)(2,1)}, bf16[4,16,512]{2,1,0:T(8,128)(2,1)S(1)}, bf16[4,16,512]{2,1,0:T(8,128)(2,1)S(1)}, bf16[4,512,128]{2,1,0:T(8,128...) custom-call(s32[1]{0:T(128)} %bitcast.me_ref, ...), custom_call_target="tpu_custom_call" | custom-call | tf_op jit(solution)/shard_map/head/pallas_call | solution.py:672
  67.1 0.7 collective-permute-start.14
  67.8 2.0 %collective-permute-start.13 = (bf16[4,128,128]{2,1,0:T(8,128)(2,1)S(1)}, bf16[4,128,128]{2,1,0:T(8,128)(2,1)S(1)}, u32[]{:S(2)}, u32[]{:S(2)}) collective-permute-start(bf16[4,128,128]{2,1,0:T(8,128)(2,1)S(1)} %get-tuple-element.123), channel_id=1, source_target_pairs={{0,1},{1,0},{2,3},{3,2},{4,5},{5,4},{6,7},{7,6},{8,9},{9,8},{10,11... | collective-permute-start | bytes 393224 | tf_op jit(solution)/shard_map/ppermute | solution.py:122
  69.8 9.7 %all_to_all.17.stats3_ref = f32[32,1,128]{2,1,0:T(1,128)S(1)} all-to-all(f32[32,1,128]{2,1,0:T(1,128)S(1)} %get-tuple-element.84), channel_id=1, replica_groups=mesh['tm'=16,'src'=2] {'tm','src'}, dimensions={0} | all-to-all | bytes 32768 | tf_op jit(solution)/shard_map/all_to_all | solution.py:148
  79.5 11.6 %input_grad.1 = (bf16[4,512,128]{2,1,0:T(8,128)(2,1)}, f32[128,512]{1,0:T(8,128)S(1)}, f32[8,512]{1,0:T(8,128)S(1)}) custom-call(s32[1]{0:T(128)} %bitcast.me_ref, s32[4,8]{1,0:T(4,128)S(1)} %copy-done.8, f32[32,1,128]{2,1,0:T(1,128)S(1)} %all_to_all.15.stats_ref.stats1_ref, f32[32,1,128]{2,1,0:T(1,128)S(1)} %all_to_all.16.stats_ref.stats2_ref, ...), custom_call_target="tpu_custom_call" | custom-call | tf_op jit(solution)/shard_map/input_grad/pallas_call | solution.py:886
  91.1 1.3 %pack.1 = (f32[1408,128]{1,0:T(8,128)S(1)}, bf16[1408,128]{1,0:T(8,128)(2,1)S(1)}) custom-call(s32[340]{0:T(512)S(1)} %get-tuple-element.59.pos_ref, f32[128,512]{1,0:T(8,128)S(1)} %get-tuple-element.91.g_in, f32[256,512]{1,0:T(8,128)S(1)} %get-tuple-element.92.g_rs, f32[128,1024]{1,0:T(8,128)S(1)} %get-tuple-element.93.g_mask, ...), custom_call_target="tpu_custom_call" | custom-call | tf_op jit(solution)/shard_map/pack/pallas_call | solution.py:939
  92.9 1.2 %collective-permute-done.16.refs_1_ = bf16[1408,128]{1,0:T(8,128)(2,1)S(1)} collective-permute-done((bf16[1408,128]{1,0:T(8,128)(2,1)S(1)}, bf16[1408,128]{1,0:T(8,128)(2,1)S(1)}, u32[]{:S(2)}, u32[]{:S(2)}) %collective-permute-start.16) | collective-permute-done | bytes 360480 | tf_op jit(solution)/shard_map/ppermute | solution.py:122
  95.4 2.3 %collective-permute-start.19 = (bf16[352,128]{1,0:T(8,128)(2,1)S(1)}, bf16[352,128]{1,0:T(8,128)(2,1)S(1)}, u32[]{:S(2)}, u32[]{:S(2)}) collective-permute-start(bf16[352,128]{1,0:T(8,128)(2,1)S(1)} %get-tuple-element.102), channel_id=1, source_target_pairs={{0,6},{1,7},{2,4},{3,5},{4,2},{5,3},{6,0},{7,1},{8,14},{9,15},{10,... | collective-permute-start | bytes 270344 | tf_op jit(solution)/shard_map/ppermute | solution.py:122
  97.8 1.7 %collective-permute-done.17.refs_1_ = bf16[352,128]{1,0:T(8,128)(2,1)S(1)} collective-permute-done((bf16[352,128]{1,0:T(8,128)(2,1)S(1)}, bf16[352,128]{1,0:T(8,128)(2,1)S(1)}, u32[]{:S(2)}, u32[]{:S(2)}) %collective-permute-start.17) | collective-permute-done | bytes 90144 | tf_op jit(solution)/shard_map/ppermute | solution.py:122
  99.5 1.8 %collective-permute-done.18.refs_2_ = bf16[352,128]{1,0:T(8,128)(2,1)S(1)} collective-permute-done((bf16[352,128]{1,0:T(8,128)(2,1)S(1)}, bf16[352,128]{1,0:T(8,128)(2,1)S(1)}, u32[]{:S(2)}, u32[]{:S(2)}) %collective-permute-start.18) | collective-permute-done | bytes 90144 | tf_op jit(solution)/shard_map/ppermute | solution.py:122
  101.3 0.6 collective-permute-start.20
  102.5 3.3 %collective-permute-start.22 = (bf16[88,128]{1,0:T(8,128)(2,1)S(1)}, bf16[88,128]{1,0:T(8,128)(2,1)S(1)}, u32[]{:S(2)}, u32[]{:S(2)}) collective-permute-start(bf16[88,128]{1,0:T(8,128)(2,1)S(1)} %get-tuple-element.106), channel_id=1, source_target_pairs={{0,24},{1,25},{2,26},{3,27},{4,28},{5,29},{6,30},{7,31},{8,16},{9,... | collective-permute-start | bytes 67592 | tf_op jit(solution)/shard_map/ppermute | solution.py:122
  105.8 0.7 maximum_bitcast_fusion
  106.6 1.4 %collective-permute-done.22.refs_3_ = bf16[88,128]{1,0:T(8,128)(2,1)S(1)} collective-permute-done((bf16[88,128]{1,0:T(8,128)(2,1)S(1)}, bf16[88,128]{1,0:T(8,128)(2,1)S(1)}, u32[]{:S(2)}, u32[]{:S(2)}) %collective-permute-start.22) | collective-permute-done | bytes 22560 | tf_op jit(solution)/shard_map/ppermute | solution.py:122
  108.1 1.4 %adam.1 = (f32[11,1024]{1,0:T(8,128)}, f32[11,1024]{1,0:T(8,128)}, f32[11,1024]{1,0:T(8,128)}) custom-call(s32[1]{0:T(128)} %bitcast.1.count_ref, f32[88,128]{1,0:T(8,128)S(1)} %get-tuple-element.103.refs_0_, bf16[88,128]{1,0:T(8,128)(2,1)S(1)} %collective-permute-done.20.refs_1_, bf16[88,128]{1,0:T(8,128)(2,1)S(1)} %collective-permute-done.21.refs_2_, ...), custom_call_target="tpu_custom_call" | custom-call | tf_op jit(solution)/shard_map/adam/pallas_call | solution.py:1010
  (57 shorter events, 6.8 us)
Async XLA Ops:
  0.6 23.7 %copy-start = (bf16[4,512,128]{2,1,0:T(8,128)(2,1)S(1)}, bf16[4,512,128]{2,1,0:T(8,128)(2,1)}, u32[]{:S(2)}) copy-start(bf16[4,512,128]{2,1,0:T(8,128)(2,1)} %x_ref.7) | copy-start | bytes 1572868
  0.6 0.9 copy-start.3
  1.5 20.3 %copy-start.5 = (bf16[4,1,1024,16]{2,3,1,0:T(8,128)(2,1)S(1)}, bf16[4,1,1024,16]{2,3,1,0:T(8,128)(2,1)}, u32[]{:S(2)}) copy-start(bf16[4,1,1024,16]{2,3,1,0:T(8,128)(2,1)} %param.17) | copy-start | bytes 393220
  1.6 9.5 %collective-permute-start.2 = (bf16[88,128]{1,0:T(8,128)(2,1)S(1)}, bf16[88,128]{1,0:T(8,128)(2,1)S(1)}, u32[]{:S(2)}, u32[]{:S(2)}) collective-permute-start(bf16[88,128]{1,0:T(8,128)(2,1)S(1)} %to_tiles.1), channel_id=1, source_target_pairs={{0,24},{1,25},{2,26},{3,27},{4,28},{5,29},{6,30},{7,31},{8,16},{9,... | collective-permute-start | bytes 67592 | tf_op jit(solution)/shard_map/ppermute | solution.py:122
  6.7 4.7 %collective-permute-start.1 = (bf16[88,128]{1,0:T(8,128)(2,1)S(1)}, bf16[88,128]{1,0:T(8,128)(2,1)S(1)}, u32[]{:S(2)}, u32[]{:S(2)}) collective-permute-start(bf16[88,128]{1,0:T(8,128)(2,1)S(1)} %to_tiles.1), channel_id=1, source_target_pairs={{0,16},{1,17},{2,18},{3,19},{4,20},{5,21},{6,22},{7,23},{8,24},{9,... | collective-permute-start | bytes 67592 | tf_op jit(solution)/shard_map/ppermute | solution.py:122
  6.7 4.7 %collective-permute-start = (bf16[88,128]{1,0:T(8,128)(2,1)S(1)}, bf16[88,128]{1,0:T(8,128)(2,1)S(1)}, u32[]{:S(2)}, u32[]{:S(2)}) collective-permute-start(bf16[88,128]{1,0:T(8,128)(2,1)S(1)} %to_tiles.1), channel_id=1, source_target_pairs={{0,8},{1,9},{2,10},{3,11},{4,12},{5,13},{6,14},{7,15},{8,0},{9,1},... | collective-permute-start | bytes 67592 | tf_op jit(solution)/shard_map/ppermute | solution.py:122
  8.9 30.5 %copy-start.8 = (s32[4,8]{1,0:T(4,128)S(1)}, s32[4,8]{1,0:T(4,128)}, u32[]{:S(2)}) copy-start(s32[4,8]{1,0:T(4,128)} %seg_ref.5) | copy-start | bytes 388
  11.4 6.1 %collective-permute-start.5 = (bf16[352,128]{1,0:T(8,128)(2,1)S(1)}, bf16[352,128]{1,0:T(8,128)(2,1)S(1)}, u32[]{:S(2)}, u32[]{:S(2)}) collective-permute-start(bf16[352,128]{1,0:T(8,128)(2,1)S(1)} %constant_dynamic-update-slice_fusion.refs_0_), channel_id=1, source_target_pairs={{0,6},{1,7},{2,4},{3,5},{4,2},{5,3},{6,0},{7,1},{8,14},{9,15},{10,... | collective-permute-start | bytes 270344 | tf_op jit(solution)/shard_map/ppermute | solution.py:122
  13.9 4.5 %collective-permute-start.4 = (bf16[352,128]{1,0:T(8,128)(2,1)S(1)}, bf16[352,128]{1,0:T(8,128)(2,1)S(1)}, u32[]{:S(2)}, u32[]{:S(2)}) collective-permute-start(bf16[352,128]{1,0:T(8,128)(2,1)S(1)} %constant_dynamic-update-slice_fusion.refs_0_), channel_id=1, source_target_pairs={{0,4},{1,5},{2,6},{3,7},{4,0},{5,1},{6,2},{7,3},{8,12},{9,13},{10,... | collective-permute-start | bytes 270344 | tf_op jit(solution)/shard_map/ppermute | solution.py:122
  14.4 4.5 %collective-permute-start.3 = (bf16[352,128]{1,0:T(8,128)(2,1)S(1)}, bf16[352,128]{1,0:T(8,128)(2,1)S(1)}, u32[]{:S(2)}, u32[]{:S(2)}) collective-permute-start(bf16[352,128]{1,0:T(8,128)(2,1)S(1)} %constant_dynamic-update-slice_fusion.refs_0_), channel_id=1, source_target_pairs={{0,2},{1,3},{2,0},{3,1},{4,6},{5,7},{6,4},{7,5},{8,10},{9,11},{10,... | collective-permute-start | bytes 270344 | tf_op jit(solution)/shard_map/ppermute | solution.py:122
  15.0 39.2 %copy-start.1 = (bf16[4,512,128]{2,1,0:T(8,128)(2,1)S(1)}, bf16[4,512,128]{2,1,0:T(8,128)(2,1)}, u32[]{:S(2)}) copy-start(bf16[4,512,128]{2,1,0:T(8,128)(2,1)} %dy_ref.3) | copy-start | bytes 1572868
  15.0 39.2 %copy-start.2 = (bf16[4,512,512]{2,1,0:T(8,128)(2,1)S(1)}, bf16[4,512,512]{2,1,0:T(8,128)(2,1)}, u32[]{:S(2)}) copy-start(bf16[4,512,512]{2,1,0:T(8,128)(2,1)} %enc_ref.1) | copy-start | bytes 6291460
  19.0 20.4 %collective-permute-start.10 = (bf16[4,384,128]{2,1,0:T(8,128)(2,1)S(1)}, bf16[4,384,128]{2,1,0:T(8,128)(2,1)S(1)}, u32[]{:S(2)}, u32[]{:S(2)}) collective-permute-start(bf16[4,384,128]{2,1,0:T(8,128)(2,1)S(1)} %get-tuple-element.69), channel_id=1, source_target_pairs={{0,1},{1,0},{2,3},{3,2},{4,5},{5,4},{6,7},{7,6},{8,9},{9,8},{10,11... | collective-permute-start | bytes 1179656 | tf_op jit(solution)/shard_map/ppermute | solution.py:122
  19.0 20.4 %collective-permute-start.11 = (bf16[4,384,128]{2,1,0:T(8,128)(2,1)S(1)}, bf16[4,384,128]{2,1,0:T(8,128)(2,1)S(1)}, u32[]{:S(2)}, u32[]{:S(2)}) collective-permute-start(bf16[4,384,128]{2,1,0:T(8,128)(2,1)S(1)} %get-tuple-element.70), channel_id=1, source_target_pairs={{1,2},{3,4},{5,6},{7,8},{9,10},{11,12},{13,14},{15,16},{17,18},{19... | collective-permute-start | bytes 1179656 | tf_op jit(solution)/shard_map/ppermute | solution.py:1053
  19.7 3.0 %collective-permute-start.6 = (bf16[352,128]{1,0:T(8,128)(2,1)S(1)}, bf16[352,128]{1,0:T(8,128)(2,1)S(1)}, u32[]{:S(2)}, u32[]{:S(2)}) collective-permute-start(bf16[352,128]{1,0:T(8,128)(2,1)S(1)} %constant_dynamic-update-slice_fusion.refs_0_), channel_id=1, source_target_pairs={{0,1},{1,0},{2,3},{3,2},{4,5},{5,4},{6,7},{7,6},{8,9},{9,8},{10,11... | collective-permute-start | bytes 270344 | tf_op jit(solution)/shard_map/ppermute | solution.py:122
  21.7 1.3 %collective-permute-start.7 = (bf16[352,128]{1,0:T(8,128)(2,1)S(1)}, bf16[352,128]{1,0:T(8,128)(2,1)S(1)}, u32[]{:S(2)}, u32[]{:S(2)}) collective-permute-start(bf16[352,128]{1,0:T(8,128)(2,1)S(1)} %collective-permute-done.3.refs_1_), channel_id=1, source_target_pairs={{0,1},{1,0},{2,3},{3,2},{4,5},{5,4},{6,7},{7,6},{8,9},{9,8},{10,11... | collective-permute-start | bytes 270344 | tf_op jit(solution)/shard_map/ppermute | solution.py:122
  21.8 17.6 %collective-permute-start.12 = (bf16[4,16,1024]{2,1,0:T(8,128)(2,1)S(1)}, bf16[4,16,1024]{2,1,0:T(8,128)(2,1)S(1)}, u32[]{:S(2)}, u32[]{:S(2)}) collective-permute-start(bf16[4,16,1024]{2,1,0:T(8,128)(2,1)S(1)} %bitcast.11), channel_id=1, source_target_pairs={{0,1},{1,0},{2,3},{3,2},{4,5},{5,4},{6,7},{7,6},{8,9},{9,8},{10,11... | collective-permute-start | bytes 393224 | tf_op jit(solution)/shard_map/ppermute | solution.py:122
  22.7 1.3 %collective-permute-start.8 = (bf16[352,128]{1,0:T(8,128)(2,1)S(1)}, bf16[352,128]{1,0:T(8,128)(2,1)S(1)}, u32[]{:S(2)}, u32[]{:S(2)}) collective-permute-start(bf16[352,128]{1,0:T(8,128)(2,1)S(1)} %collective-permute-done.4.refs_2_), channel_id=1, source_target_pairs={{0,1},{1,0},{2,3},{3,2},{4,5},{5,4},{6,7},{7,6},{8,9},{9,8},{10,11... | collective-permute-start | bytes 270344 | tf_op jit(solution)/shard_map/ppermute | solution.py:122
  23.0 1.3 %collective-permute-start.9 = (bf16[352,128]{1,0:T(8,128)(2,1)S(1)}, bf16[352,128]{1,0:T(8,128)(2,1)S(1)}, u32[]{:S(2)}, u32[]{:S(2)}) collective-permute-start(bf16[352,128]{1,0:T(8,128)(2,1)S(1)} %collective-permute-done.5.refs_3_), channel_id=1, source_target_pairs={{0,1},{1,0},{2,3},{3,2},{4,5},{5,4},{6,7},{7,6},{8,9},{9,8},{10,11... | collective-permute-start | bytes 270344 | tf_op jit(solution)/shard_map/ppermute | solution.py:122
  67.1 12.4 %collective-permute-start.14 = (bf16[4,128,128]{2,1,0:T(8,128)(2,1)S(1)}, bf16[4,128,128]{2,1,0:T(8,128)(2,1)S(1)}, u32[]{:S(2)}, u32[]{:S(2)}) collective-permute-start(bf16[4,128,128]{2,1,0:T(8,128)(2,1)S(1)} %get-tuple-element.122), channel_id=1, source_target_pairs={{1,2},{3,4},{5,6},{7,8},{9,10},{11,12},{13,14},{15,16},{17,18},{19... | collective-permute-start | bytes 393224 | tf_op jit(solution)/shard_map/ppermute | solution.py:1066
  67.8 11.7 %collective-permute-start.13 = (bf16[4,128,128]{2,1,0:T(8,128)(2,1)S(1)}, bf16[4,128,128]{2,1,0:T(8,128)(2,1)S(1)}, u32[]{:S(2)}, u32[]{:S(2)}) collective-permute-start(bf16[4,128,128]{2,1,0:T(8,128)(2,1)S(1)} %get-tuple-element.123), channel_id=1, source_target_pairs={{0,1},{1,0},{2,3},{3,2},{4,5},{5,4},{6,7},{7,6},{8,9},{9,8},{10,11... | collective-permute-start | bytes 393224 | tf_op jit(solution)/shard_map/ppermute | solution.py:122
  91.1 17.0 %copy-start.4 = (f32[11,1024]{1,0:T(8,128)S(1)}, f32[11,1024]{1,0:T(8,128)}, u32[]{:S(2)}) copy-start(f32[11,1024]{1,0:T(8,128)} %refs_4_.1) | copy-start | bytes 135172
  91.1 17.0 %copy-start.6 = (f32[11,1024]{1,0:T(8,128)S(1)}, f32[11,1024]{1,0:T(8,128)}, u32[]{:S(2)}) copy-start(f32[11,1024]{1,0:T(8,128)} %refs_5_.1) | copy-start | bytes 135172
  91.1 17.0 %copy-start.7 = (f32[11,1024]{1,0:T(8,128)S(1)}, f32[11,1024]{1,0:T(8,128)}, u32[]{:S(2)}) copy-start(f32[11,1024]{1,0:T(8,128)} %refs_6_.1) | copy-start | bytes 135172
  92.4 1.7 %collective-permute-start.16 = (bf16[1408,128]{1,0:T(8,128)(2,1)S(1)}, bf16[1408,128]{1,0:T(8,128)(2,1)S(1)}, u32[]{:S(2)}, u32[]{:S(2)}) collective-permute-start(bf16[1408,128]{1,0:T(8,128)(2,1)S(1)} %get-tuple-element.98), channel_id=1, source_target_pairs={{0,1},{1,0},{2,3},{3,2},{4,5},{5,4},{6,7},{7,6},{8,9},{9,8},{10,11... | collective-permute-start | bytes 1081352 | tf_op jit(solution)/shard_map/ppermute | solution.py:122
  92.4 5.3 %collective-permute-start.15 = (bf16[4,16,512]{2,1,0:T(8,128)(2,1)S(1)}, bf16[4,16,512]{2,1,0:T(8,128)(2,1)S(1)}, u32[]{:S(2)}, u32[]{:S(2)}) collective-permute-start(bf16[4,16,512]{2,1,0:T(8,128)(2,1)S(1)} %get-tuple-element.89), channel_id=1, source_target_pairs={{0,1},{1,0},{2,3},{3,2},{4,5},{5,4},{6,7},{7,6},{8,9},{9,8},{10,11... | collective-permute-start | bytes 196616 | tf_op jit(solution)/shard_map/ppermute | solution.py:122
  94.2 5.3 %collective-permute-start.17 = (bf16[352,128]{1,0:T(8,128)(2,1)S(1)}, bf16[352,128]{1,0:T(8,128)(2,1)S(1)}, u32[]{:S(2)}, u32[]{:S(2)}) collective-permute-start(bf16[352,128]{1,0:T(8,128)(2,1)S(1)} %get-tuple-element.100), channel_id=1, source_target_pairs={{0,2},{1,3},{2,0},{3,1},{4,6},{5,7},{6,4},{7,5},{8,10},{9,11},{10,... | collective-permute-start | bytes 270344 | tf_op jit(solution)/shard_map/ppermute | solution.py:122
  94.8 6.5 %collective-permute-start.18 = (bf16[352,128]{1,0:T(8,128)(2,1)S(1)}, bf16[352,128]{1,0:T(8,128)(2,1)S(1)}, u32[]{:S(2)}, u32[]{:S(2)}) collective-permute-start(bf16[352,128]{1,0:T(8,128)(2,1)S(1)} %get-tuple-element.101), channel_id=1, source_target_pairs={{0,4},{1,5},{2,6},{3,7},{4,0},{5,1},{6,2},{7,3},{8,12},{9,13},{10,... | collective-permute-start | bytes 270344 | tf_op jit(solution)/shard_map/ppermute | solution.py:122
  95.4 5.8 %collective-permute-start.19 = (bf16[352,128]{1,0:T(8,128)(2,1)S(1)}, bf16[352,128]{1,0:T(8,128)(2,1)S(1)}, u32[]{:S(2)}, u32[]{:S(2)}) collective-permute-start(bf16[352,128]{1,0:T(8,128)(2,1)S(1)} %get-tuple-element.102), channel_id=1, source_target_pairs={{0,6},{1,7},{2,4},{3,5},{4,2},{5,3},{6,0},{7,1},{8,14},{9,15},{10,... | collective-permute-start | bytes 270344 | tf_op jit(solution)/shard_map/ppermute | solution.py:122
  101.3 5.1 %collective-permute-start.20 = (bf16[88,128]{1,0:T(8,128)(2,1)S(1)}, bf16[88,128]{1,0:T(8,128)(2,1)S(1)}, u32[]{:S(2)}, u32[]{:S(2)}) collective-permute-start(bf16[88,128]{1,0:T(8,128)(2,1)S(1)} %get-tuple-element.104), channel_id=1, source_target_pairs={{0,8},{1,9},{2,10},{3,11},{4,12},{5,13},{6,14},{7,15},{8,0},{9,1},... | collective-permute-start | bytes 67592 | tf_op jit(solution)/shard_map/ppermute | solution.py:122
  101.9 4.7 %collective-permute-start.21 = (bf16[88,128]{1,0:T(8,128)(2,1)S(1)}, bf16[88,128]{1,0:T(8,128)(2,1)S(1)}, u32[]{:S(2)}, u32[]{:S(2)}) collective-permute-start(bf16[88,128]{1,0:T(8,128)(2,1)S(1)} %get-tuple-element.105), channel_id=1, source_target_pairs={{0,16},{1,17},{2,18},{3,19},{4,20},{5,21},{6,22},{7,23},{8,24},{9,... | collective-permute-start | bytes 67592 | tf_op jit(solution)/shard_map/ppermute | solution.py:122
  102.5 5.6 %collective-permute-start.22 = (bf16[88,128]{1,0:T(8,128)(2,1)S(1)}, bf16[88,128]{1,0:T(8,128)(2,1)S(1)}, u32[]{:S(2)}, u32[]{:S(2)}) collective-permute-start(bf16[88,128]{1,0:T(8,128)(2,1)S(1)} %get-tuple-element.106), channel_id=1, source_target_pairs={{0,24},{1,25},{2,26},{3,27},{4,28},{5,29},{6,30},{7,31},{8,16},{9,... | collective-permute-start | bytes 67592 | tf_op jit(solution)/shard_map/ppermute | solution.py:122

commit v4 on v3

--- a/solution.py
+++ b/solution.py
@@ -122,14 +122,14 @@
     return lax.ppermute(value, AXES, [(i, i ^ mask) for i in range(n_dev)])
 
 
-def gather_tiles(tiles, n_dev, early, late):
+def gather_tiles(tiles, n_dev, early, rows, sides):
     parts = [tiles]
     for k, bits in enumerate(stages(n_dev)[:-1]):
         if k == 1:
-            parts, early = lax.optimization_barrier((parts, early))
+            parts, early, rows = lax.optimization_barrier((parts, early, rows))
         z = parts[0] if len(parts) == 1 else jnp.concatenate(parts, axis=0)
         parts = [z] + [swap(z, spread(bits, q), n_dev) for q in range(1, 1 << len(bits))]
-    parts, late = lax.optimization_barrier((parts, late))
+    parts, late = lax.optimization_barrier((parts, sides(*rows)))
     return parts + [swap(z, 1, n_dev) for z in parts], early, late
 
 
@@ -460,6 +460,8 @@
     dn2_s,
     dw_s,
     wave_s,
+    block_s,
+    sems,
 ):
     micro, frames, _ = d_ref.shape
     nb = frames // BLK
@@ -487,6 +489,9 @@
             )
             for k, v in enumerate(rows):
                 par[m, k, h : h + 1, :] = v
+
+    def leave(m):
+        return pltpu.make_async_copy(block_s.at[m], block_ref.at[m], sems.at[m])
 
     def norm_steps(m, slot):
         def step(h, cols):
@@ -566,9 +571,10 @@
         def skip():
             rows = slice(0, frames)
             ys = mm(n2_s[slot, rows, :], w_rs[...])
-            block_ref[m, rows, :] = (x_ref[m, rows, :].astype(f32) + ys[:, 0:B]).astype(bf16)
+            block_s[m, rows, :] = (x_ref[m, rows, :].astype(f32) + ys[:, 0:B]).astype(bf16)
             half = 0.5 * ys[:, B : B + SC]
             z, slope = slope_parts(half, jnp.tanh(half))
+            leave(m).start()
             z_s[rows, :] = z.astype(bf16)
             slope_s[rows, :] = slope
 
@@ -653,6 +659,8 @@
     for step in end_steps(last, last % 2):
         step()
     row = end_row(last, last * nb * KINDS, last % 2, row, True)
+    for m in range(micro):
+        leave(m).wait()
     out_stats[...] = jnp.broadcast_to(row[None], out_stats.shape)
 
 
@@ -672,7 +680,7 @@
     return pl.pallas_call(
         head_kernel,
         in_specs=[smem(), smem()] + [vmem()] * 11,
-        out_specs=(vmem(),) * len(outs),
+        out_specs=(pl.BlockSpec(memory_space=pl.ANY),) + (vmem(),) * (len(outs) - 1),
         scratch_shapes=[
             pltpu.VMEM((2, SEGS, 128), f32),
             pltpu.VMEM((micro, 5, 8, HW), f32),
@@ -692,6 +700,8 @@
             pltpu.VMEM((frames, HW), f32),
             pltpu.VMEM((2, C, L, frames), bf16),
             pltpu.VMEM((C, L, frames), bf16),
+            pltpu.VMEM(feats.shape, bf16),
+            pltpu.SemaphoreType.DMA((micro,)),
         ],
         out_shape=tuple(jax.ShapeDtypeStruct(s, t) for s, t in outs),
         compiler_params=pltpu.CompilerParams(vmem_limit_bytes=HEAD_MIB * MIB),
@@ -735,6 +745,8 @@
     dd_s,
     a_s,
     da_s,
+    feats_s,
+    sems,
 ):
     micro, frames, _ = d_ref.shape
     nb = frames // BLK
@@ -868,17 +880,23 @@
         def feats(r):
             rows = slice(r, r + BLK)
             grad = dy_ref[m, rows, :].astype(f32) + 2.0 * mm_t(da_s[rows, :], w_in[...])
-            feats_ref[m, rows, :] = grad.astype(bf16)
+            feats_s[m, rows, :] = grad.astype(bf16)
 
         return [part(weight, c) for c in range(0, HW, HALF_W)] + [
             part(feats, r) for r in range(0, frames, BLK)
         ]
 
+    def leave(m):
+        return pltpu.make_async_copy(feats_s.at[m], feats_ref.at[m], sems.at[m])
+
     def body(m, slot, carry):
         run(project(m, 0) + depth_steps(m) + hidden_steps(m, 0) + last_steps(m))
+        leave(m).start()
         return carry
 
     lax.fori_loop(0, micro, lambda m, c: body(m, 0, c), 0)
+    for m in range(micro):
+        leave(m).wait()
 
 
 def input_grad(me, lengths, stats, d, edge, feats, dy, near, far, ds, ds_near, ds_far, w_in, w_rs, vec):
@@ -891,7 +909,7 @@
             jax.ShapeDtypeStruct((8, HW), f32),
         ),
         in_specs=[smem(), smem()] + [vmem()] * 15,
-        out_specs=(vmem(),) * 3,
+        out_specs=(pl.BlockSpec(memory_space=pl.ANY), vmem(), vmem()),
         scratch_shapes=[
             pltpu.VMEM((8, SEGS, 128), f32),
             pltpu.VMEM((micro, 3, 8, HW), f32),
@@ -901,6 +919,8 @@
             pltpu.VMEM((frames + 2 * DIL, HW), f32),
             pltpu.VMEM((2, frames, HW), f32),
             pltpu.VMEM((frames, HW), bf16),
+            pltpu.VMEM(feats.shape, bf16),
+            pltpu.SemaphoreType.DMA((micro,)),
         ],
         compiler_params=pltpu.CompilerParams(vmem_limit_bytes=INPUT_MIB * MIB),
         name="input_grad",
@@ -1044,10 +1064,13 @@
     here = me.astype(jnp.int32).reshape(1)
 
     cot = jnp.transpose(wave_cot[:, 0], (0, 2, 1))
-    halo = (feats, BLK), (out_cot, DIL)
-    sides = ends(core == 0, *halo), ends(core == 1, *halo)
+
+    def sides(x, dy, other):
+        halo = (x, BLK), (dy, DIL)
+        return ends(core == 0, *halo), ends(core == 1, *halo), other
+
     parts, (pos, here, count), (near, far, cot_other) = gather_tiles(
-        to_tiles(master), n_dev, (pos, here, count), (*sides, cot)
+        to_tiles(master), n_dev, (pos, here, count), (feats, out_cot, cot), sides
     )
     near = swap(near, 1, n_dev)
     far = lax.ppermute(far, AXES, across)

time: 110 us -> 108 us (0.982)
  blocking collectives: 31.3 us -> 30 us
    all_to_all x3, blocking collectives: 31.3 us -> 30 us  [share_sums(): return lax.all_to_all(rows, AXES, 0, 0, tiled=True)]
where the time goes in v4:
time: 108 us; the launch traced here: 107 us
  Pallas kernels  34.9 us (32%)
  blocking collectives  30 us (28%)
  starting transfers between devices  24.1 us (22%)
  waiting for transfers between devices  12.1 us (11%)
  local copies, waits for them, and re-layouts  3.06 us (3%)
  other arithmetic  2.35 us (2%)
    all_to_all x3, blocking collectives, share_sums(): return lax.all_to_all(rows, AXES, 0, 0, tiled=True)  30 us
    ppermute x21, starting transfers between devices, swap(): return lax.ppermute(value, AXES, [(i, i ^ mask) for i in range(n_dev)])  22.8 us
    pallas_call x1, Pallas kernels, head(): pl.pallas_call(head_kernel, in_specs=[smem(), smem()] + [vmem()] * 11, ou...  12.3 us
    ppermute x21, waiting for transfers between devices, swap(): return lax.ppermute(value, AXES, [(i, i ^ mask) for i in range(n_dev)])  12.1 us
    pallas_call x1, Pallas kernels, input_grad(): pl.pallas_call(input_kernel, out_shape=(jax.ShapeDtypeStruct(feats.shape,...  11.5 us
    pallas_call x1, Pallas kernels, depth(): pl.pallas_call(depth_kernel, out_shape=(jax.ShapeDtypeStruct((micro, fram...  5.92 us
    pallas_call x1, Pallas kernels, unpack(): pl.pallas_call(functools.partial(unpack_kernel, len(parts)), out_shape=ou...  2.4 us
  transfers between devices with their start and end apart: 23, of which 12 were waited for; matrix products, arithmetic and copies ran while one was open for 4% of the time, Pallas kernels for 2%

profile of v4, /device:TPU:0, one launch (start us, length us, event | category | flops | bytes accessed | tf_op | source)
XLA Modules:
  0.0 107.5 jit_solution(8730395899515535818)
XLA Ops:
  0.7 0.9 copy-done.3
  1.6 5.1 %collective-permute-start.2 = (bf16[88,128]{1,0:T(8,128)(2,1)S(1)}, bf16[88,128]{1,0:T(8,128)(2,1)S(1)}, u32[]{:S(2)}, u32[]{:S(2)}) collective-permute-start(bf16[88,128]{1,0:T(8,128)(2,1)S(1)} %to_tiles.1), channel_id=1, source_target_pairs={{0,24},{1,25},{2,26},{3,27},{4,28},{5,29},{6,30},{7,31},{8,16},{9,... | collective-permute-start | bytes 67592 | tf_op jit(solution)/shard_map/ppermute | solution.py:122
  7.3 0.7 reduce
  8.2 0.7 convert_reduce_fusion.1
  9.0 2.4 %collective-permute-done.1 = bf16[88,128]{1,0:T(8,128)(2,1)S(1)} collective-permute-done((bf16[88,128]{1,0:T(8,128)(2,1)S(1)}, bf16[88,128]{1,0:T(8,128)(2,1)S(1)}, u32[]{:S(2)}, u32[]{:S(2)}) %collective-permute-start.1) | collective-permute-done | bytes 22560 | tf_op jit(solution)/shard_map/ppermute | solution.py:122
  11.4 2.5 %collective-permute-start.5 = (bf16[352,128]{1,0:T(8,128)(2,1)S(1)}, bf16[352,128]{1,0:T(8,128)(2,1)S(1)}, u32[]{:S(2)}, u32[]{:S(2)}) collective-permute-start(bf16[352,128]{1,0:T(8,128)(2,1)S(1)} %constant_dynamic-update-slice_fusion.refs_0_), channel_id=1, source_target_pairs={{0,6},{1,7},{2,4},{3,5},{4,2},{5,3},{6,0},{7,1},{8,14},{9,15},{10,... | collective-permute-start | bytes 270344 | tf_op jit(solution)/shard_map/ppermute | solution.py:122
  15.0 1.0 constant_dynamic-slice_fusion.2
  16.0 1.1 %constant_dynamic-slice_fusion.3 = (bf16[4,256,128]{2,1,0:T(8,128)(2,1)S(1)}, bf16[4,256,128]{2,1,0:T(8,128)(2,1)S(1)}) fusion(bf16[4,512,128]{2,1,0:T(8,128)(2,1)} %x_ref.7, s32[]{:T(128)S(6)} %select_n.35, s32[]{:T(128)S(6)} %select_n.33), kind=kLoop, calls=%fused_computation.17 | loop fusion | bytes 1048584 | tf_op jit(solution)/shard_map/dynamic_slice | solution.py:1055
  17.2 0.7 collective-permute-done.5.refs_3_
  17.9 0.8 collective-permute-done.4.refs_2_
  19.0 0.7 collective-permute-start.11
  19.7 1.9 %collective-permute-start.6 = (bf16[352,128]{1,0:T(8,128)(2,1)S(1)}, bf16[352,128]{1,0:T(8,128)(2,1)S(1)}, u32[]{:S(2)}, u32[]{:S(2)}) collective-permute-start(bf16[352,128]{1,0:T(8,128)(2,1)S(1)} %constant_dynamic-update-slice_fusion.refs_0_), channel_id=1, source_target_pairs={{0,1},{1,0},{2,3},{3,2},{4,5},{5,4},{6,7},{7,6},{8,9},{9,8},{10,11... | collective-permute-start | bytes 270344 | tf_op jit(solution)/shard_map/ppermute | solution.py:122
  23.1 0.8 collective-permute-done.8.refs_6_
  24.2 2.4 %unpack.1 = (bf16[128,512]{1,0:T(8,128)(2,1)S(1)}, bf16[512,256]{1,0:T(8,128)(2,1)S(1)}, bf16[128,1024]{1,0:T(8,128)(2,1)S(1)}, bf16[16,1024]{1,0:T(8,128)(2,1)S...) custom-call(s32[340]{0:T(512)S(1)} %get-tuple-element.62.pos_ref, bf16[4,512,128]{2,1,0:T(8,128)(2,1)S(1)} %copy-done, ...), custom_call_target="tpu_custom_call" | custom-call | tf_op jit(solution)/shard_map/unpack/pallas_call | solution.py:229
  26.6 11.4 %all_to_all.15.stats_ref.stats1_ref = f32[32,1,128]{2,1,0:T(1,128)S(1)} all-to-all(f32[32,1,128]{2,1,0:T(1,128)S(1)} %get-tuple-element.74), channel_id=1, replica_groups=mesh['tm'=16,'src'=2] {'tm','src'}, dimensions={0} | all-to-all | bytes 32768 | tf_op jit(solution)/shard_map/all_to_all | solution.py:148
  38.0 5.9 %depth.1 = (f32[4,512,512]{2,1,0:T(8,128)S(1)}, f32[4,256,512]{2,1,0:T(8,128)S(1)}, f32[32,1,128]{2,1,0:T(1,128)S(1)}) custom-call(s32[1]{0:T(128)} %bitcast.me_ref, s32[4,8]{1,0:T(4,128)S(1)} %copy-done.8, f32[32,1,128]{2,1,0:T(1,128)S(1)} %all_to_all.15.stats_ref.stats1_ref, bf16[4,512,128]{2,1,0:T(8,128)(2,1)S(1)} %copy-done, ...), custom_call_target="tpu_custom_call" | custom-call | tf_op jit(solution)/shard_map/depth/pallas_call | solution.py:402
  43.9 8.8 %all_to_all.16.stats_ref.stats2_ref = f32[32,1,128]{2,1,0:T(1,128)S(1)} all-to-all(f32[32,1,128]{2,1,0:T(1,128)S(1)} %get-tuple-element.83), channel_id=1, replica_groups=mesh['tm'=16,'src'=2] {'tm','src'}, dimensions={0} | all-to-all | bytes 32768 | tf_op jit(solution)/shard_map/all_to_all | solution.py:148
  52.8 12.3 %head.1 = (bf16[4,512,128]{2,1,0:T(8,128)(2,1)}, bf16[4,16,512]{2,1,0:T(8,128)(2,1)S(1)}, bf16[4,16,512]{2,1,0:T(8,128)(2,1)S(1)}, bf16[4,512,128]{2,1,0:T(8,128...) custom-call(s32[1]{0:T(128)} %bitcast.me_ref, ...), custom_call_target="tpu_custom_call" | custom-call | tf_op jit(solution)/shard_map/head/pallas_call | solution.py:680
  65.1 0.7 collective-permute-start.14
  65.8 2.0 %collective-permute-start.13 = (bf16[4,128,128]{2,1,0:T(8,128)(2,1)S(1)}, bf16[4,128,128]{2,1,0:T(8,128)(2,1)S(1)}, u32[]{:S(2)}, u32[]{:S(2)}) collective-permute-start(bf16[4,128,128]{2,1,0:T(8,128)(2,1)S(1)} %get-tuple-element.129), channel_id=1, source_target_pairs={{0,1},{1,0},{2,3},{3,2},{4,5},{5,4},{6,7},{7,6},{8,9},{9,8},{10,11... | collective-permute-start | bytes 393224 | tf_op jit(solution)/shard_map/ppermute | solution.py:122
  67.8 9.7 %all_to_all.17.stats3_ref = f32[32,1,128]{2,1,0:T(1,128)S(1)} all-to-all(f32[32,1,128]{2,1,0:T(1,128)S(1)} %get-tuple-element.90), channel_id=1, replica_groups=mesh['tm'=16,'src'=2] {'tm','src'}, dimensions={0} | all-to-all | bytes 32768 | tf_op jit(solution)/shard_map/all_to_all | solution.py:148
  77.5 11.5 %input_grad.1 = (bf16[4,512,128]{2,1,0:T(8,128)(2,1)}, f32[128,512]{1,0:T(8,128)S(1)}, f32[8,512]{1,0:T(8,128)S(1)}) custom-call(s32[1]{0:T(128)} %bitcast.me_ref, s32[4,8]{1,0:T(4,128)S(1)} %copy-done.8, f32[32,1,128]{2,1,0:T(1,128)S(1)} %all_to_all.15.stats_ref.stats1_ref, f32[32,1,128]{2,1,0:T(1,128)S(1)} %all_to_all.16.stats_ref.stats2_ref, ...), custom_call_target="tpu_custom_call" | custom-call | tf_op jit(solution)/shard_map/input_grad/pallas_call | solution.py:904
  89.0 1.3 %pack.1 = (f32[1408,128]{1,0:T(8,128)S(1)}, bf16[1408,128]{1,0:T(8,128)(2,1)S(1)}) custom-call(s32[340]{0:T(512)S(1)} %get-tuple-element.62.pos_ref, f32[128,512]{1,0:T(8,128)S(1)} %get-tuple-element.97.g_in, f32[256,512]{1,0:T(8,128)S(1)} %get-tuple-element.98.g_rs, f32[128,1024]{1,0:T(8,128)S(1)} %get-tuple-element.99.g_mask, ...), custom_call_target="tpu_custom_call" | custom-call | tf_op jit(solution)/shard_map/pack/pallas_call | solution.py:959
  90.9 1.2 %collective-permute-done.16.refs_1_ = bf16[1408,128]{1,0:T(8,128)(2,1)S(1)} collective-permute-done((bf16[1408,128]{1,0:T(8,128)(2,1)S(1)}, bf16[1408,128]{1,0:T(8,128)(2,1)S(1)}, u32[]{:S(2)}, u32[]{:S(2)}) %collective-permute-start.16) | collective-permute-done | bytes 360480 | tf_op jit(solution)/shard_map/ppermute | solution.py:122
  92.7 0.6 collective-permute-start.18
  93.4 2.3 %collective-permute-start.19 = (bf16[352,128]{1,0:T(8,128)(2,1)S(1)}, bf16[352,128]{1,0:T(8,128)(2,1)S(1)}, u32[]{:S(2)}, u32[]{:S(2)}) collective-permute-start(bf16[352,128]{1,0:T(8,128)(2,1)S(1)} %get-tuple-element.108), channel_id=1, source_target_pairs={{0,6},{1,7},{2,4},{3,5},{4,2},{5,3},{6,0},{7,1},{8,14},{9,15},{10,... | collective-permute-start | bytes 270344 | tf_op jit(solution)/shard_map/ppermute | solution.py:122
  95.7 1.7 %collective-permute-done.17.refs_1_ = bf16[352,128]{1,0:T(8,128)(2,1)S(1)} collective-permute-done((bf16[352,128]{1,0:T(8,128)(2,1)S(1)}, bf16[352,128]{1,0:T(8,128)(2,1)S(1)}, u32[]{:S(2)}, u32[]{:S(2)}) %collective-permute-start.17) | collective-permute-done | bytes 90144 | tf_op jit(solution)/shard_map/ppermute | solution.py:122
  97.4 1.8 %collective-permute-done.18.refs_2_ = bf16[352,128]{1,0:T(8,128)(2,1)S(1)} collective-permute-done((bf16[352,128]{1,0:T(8,128)(2,1)S(1)}, bf16[352,128]{1,0:T(8,128)(2,1)S(1)}, u32[]{:S(2)}, u32[]{:S(2)}) %collective-permute-start.18) | collective-permute-done | bytes 90144 | tf_op jit(solution)/shard_map/ppermute | solution.py:122
  100.4 3.3 %collective-permute-start.22 = (bf16[88,128]{1,0:T(8,128)(2,1)S(1)}, bf16[88,128]{1,0:T(8,128)(2,1)S(1)}, u32[]{:S(2)}, u32[]{:S(2)}) collective-permute-start(bf16[88,128]{1,0:T(8,128)(2,1)S(1)} %get-tuple-element.112), channel_id=1, source_target_pairs={{0,24},{1,25},{2,26},{3,27},{4,28},{5,29},{6,30},{7,31},{8,16},{9,... | collective-permute-start | bytes 67592 | tf_op jit(solution)/shard_map/ppermute | solution.py:122
  103.7 0.7 maximum_bitcast_fusion
  104.6 1.4 %collective-permute-done.22.refs_3_ = bf16[88,128]{1,0:T(8,128)(2,1)S(1)} collective-permute-done((bf16[88,128]{1,0:T(8,128)(2,1)S(1)}, bf16[88,128]{1,0:T(8,128)(2,1)S(1)}, u32[]{:S(2)}, u32[]{:S(2)}) %collective-permute-start.22) | collective-permute-done | bytes 22560 | tf_op jit(solution)/shard_map/ppermute | solution.py:122
  106.1 1.4 %adam.1 = (f32[11,1024]{1,0:T(8,128)}, f32[11,1024]{1,0:T(8,128)}, f32[11,1024]{1,0:T(8,128)}) custom-call(s32[1]{0:T(128)} %bitcast.1.count_ref, f32[88,128]{1,0:T(8,128)S(1)} %get-tuple-element.109.refs_0_, bf16[88,128]{1,0:T(8,128)(2,1)S(1)} %collective-permute-done.20.refs_1_, bf16[88,128]{1,0:T(8,128)(2,1)S(1)} %collective-permute-done.21.refs_2_, ...), custom_call_target="tpu_custom_call" | custom-call | tf_op jit(solution)/shard_map/adam/pallas_call | solution.py:1030
  (57 shorter events, 6.9 us)
Async XLA Ops:
  0.6 23.6 %copy-start = (bf16[4,512,128]{2,1,0:T(8,128)(2,1)S(1)}, bf16[4,512,128]{2,1,0:T(8,128)(2,1)}, u32[]{:S(2)}) copy-start(bf16[4,512,128]{2,1,0:T(8,128)(2,1)} %x_ref.7) | copy-start | bytes 1572868
  0.6 0.9 copy-start.3
  1.5 20.1 %copy-start.5 = (bf16[4,1,1024,16]{2,3,1,0:T(8,128)(2,1)S(1)}, bf16[4,1,1024,16]{2,3,1,0:T(8,128)(2,1)}, u32[]{:S(2)}) copy-start(bf16[4,1,1024,16]{2,3,1,0:T(8,128)(2,1)} %param.17) | copy-start | bytes 393220
  1.6 7.4 %collective-permute-start.2 = (bf16[88,128]{1,0:T(8,128)(2,1)S(1)}, bf16[88,128]{1,0:T(8,128)(2,1)S(1)}, u32[]{:S(2)}, u32[]{:S(2)}) collective-permute-start(bf16[88,128]{1,0:T(8,128)(2,1)S(1)} %to_tiles.1), channel_id=1, source_target_pairs={{0,24},{1,25},{2,26},{3,27},{4,28},{5,29},{6,30},{7,31},{8,16},{9,... | collective-permute-start | bytes 67592 | tf_op jit(solution)/shard_map/ppermute | solution.py:122
  6.7 4.7 %collective-permute-start.1 = (bf16[88,128]{1,0:T(8,128)(2,1)S(1)}, bf16[88,128]{1,0:T(8,128)(2,1)S(1)}, u32[]{:S(2)}, u32[]{:S(2)}) collective-permute-start(bf16[88,128]{1,0:T(8,128)(2,1)S(1)} %to_tiles.1), channel_id=1, source_target_pairs={{0,16},{1,17},{2,18},{3,19},{4,20},{5,21},{6,22},{7,23},{8,24},{9,... | collective-permute-start | bytes 67592 | tf_op jit(solution)/shard_map/ppermute | solution.py:122
  6.7 4.7 %collective-permute-start = (bf16[88,128]{1,0:T(8,128)(2,1)S(1)}, bf16[88,128]{1,0:T(8,128)(2,1)S(1)}, u32[]{:S(2)}, u32[]{:S(2)}) collective-permute-start(bf16[88,128]{1,0:T(8,128)(2,1)S(1)} %to_tiles.1), channel_id=1, source_target_pairs={{0,8},{1,9},{2,10},{3,11},{4,12},{5,13},{6,14},{7,15},{8,0},{9,1},... | collective-permute-start | bytes 67592 | tf_op jit(solution)/shard_map/ppermute | solution.py:122
  11.4 26.6 %copy-start.8 = (s32[4,8]{1,0:T(4,128)S(1)}, s32[4,8]{1,0:T(4,128)}, u32[]{:S(2)}) copy-start(s32[4,8]{1,0:T(4,128)} %seg_ref.5) | copy-start | bytes 388
  11.4 6.5 %collective-permute-start.5 = (bf16[352,128]{1,0:T(8,128)(2,1)S(1)}, bf16[352,128]{1,0:T(8,128)(2,1)S(1)}, u32[]{:S(2)}, u32[]{:S(2)}) collective-permute-start(bf16[352,128]{1,0:T(8,128)(2,1)S(1)} %constant_dynamic-update-slice_fusion.refs_0_), channel_id=1, source_target_pairs={{0,6},{1,7},{2,4},{3,5},{4,2},{5,3},{6,0},{7,1},{8,14},{9,15},{10,... | collective-permute-start | bytes 270344 | tf_op jit(solution)/shard_map/ppermute | solution.py:122
  13.9 4.7 %collective-permute-start.4 = (bf16[352,128]{1,0:T(8,128)(2,1)S(1)}, bf16[352,128]{1,0:T(8,128)(2,1)S(1)}, u32[]{:S(2)}, u32[]{:S(2)}) collective-permute-start(bf16[352,128]{1,0:T(8,128)(2,1)S(1)} %constant_dynamic-update-slice_fusion.refs_0_), channel_id=1, source_target_pairs={{0,4},{1,5},{2,6},{3,7},{4,0},{5,1},{6,2},{7,3},{8,12},{9,13},{10,... | collective-permute-start | bytes 270344 | tf_op jit(solution)/shard_map/ppermute | solution.py:122
  14.5 4.5 %collective-permute-start.3 = (bf16[352,128]{1,0:T(8,128)(2,1)S(1)}, bf16[352,128]{1,0:T(8,128)(2,1)S(1)}, u32[]{:S(2)}, u32[]{:S(2)}) collective-permute-start(bf16[352,128]{1,0:T(8,128)(2,1)S(1)} %constant_dynamic-update-slice_fusion.refs_0_), channel_id=1, source_target_pairs={{0,2},{1,3},{2,0},{3,1},{4,6},{5,7},{6,4},{7,5},{8,10},{9,11},{10,... | collective-permute-start | bytes 270344 | tf_op jit(solution)/shard_map/ppermute | solution.py:122
  17.1 35.7 %copy-start.1 = (bf16[4,512,128]{2,1,0:T(8,128)(2,1)S(1)}, bf16[4,512,128]{2,1,0:T(8,128)(2,1)}, u32[]{:S(2)}) copy-start(bf16[4,512,128]{2,1,0:T(8,128)(2,1)} %dy_ref.3) | copy-start | bytes 1572868
  17.1 35.7 %copy-start.2 = (bf16[4,512,512]{2,1,0:T(8,128)(2,1)S(1)}, bf16[4,512,512]{2,1,0:T(8,128)(2,1)}, u32[]{:S(2)}) copy-start(bf16[4,512,512]{2,1,0:T(8,128)(2,1)} %enc_ref.1) | copy-start | bytes 6291460
  19.0 19.0 %collective-permute-start.10 = (bf16[4,384,128]{2,1,0:T(8,128)(2,1)S(1)}, bf16[4,384,128]{2,1,0:T(8,128)(2,1)S(1)}, u32[]{:S(2)}, u32[]{:S(2)}) collective-permute-start(bf16[4,384,128]{2,1,0:T(8,128)(2,1)S(1)} %get-tuple-element.75), channel_id=1, source_target_pairs={{0,1},{1,0},{2,3},{3,2},{4,5},{5,4},{6,7},{7,6},{8,9},{9,8},{10,11... | collective-permute-start | bytes 1179656 | tf_op jit(solution)/shard_map/ppermute | solution.py:122
  19.0 19.0 %collective-permute-start.11 = (bf16[4,384,128]{2,1,0:T(8,128)(2,1)S(1)}, bf16[4,384,128]{2,1,0:T(8,128)(2,1)S(1)}, u32[]{:S(2)}, u32[]{:S(2)}) collective-permute-start(bf16[4,384,128]{2,1,0:T(8,128)(2,1)S(1)} %get-tuple-element.76), channel_id=1, source_target_pairs={{1,2},{3,4},{5,6},{7,8},{9,10},{11,12},{13,14},{15,16},{17,18},{19... | collective-permute-start | bytes 1179656 | tf_op jit(solution)/shard_map/ppermute | solution.py:1076
  19.7 2.9 %collective-permute-start.6 = (bf16[352,128]{1,0:T(8,128)(2,1)S(1)}, bf16[352,128]{1,0:T(8,128)(2,1)S(1)}, u32[]{:S(2)}, u32[]{:S(2)}) collective-permute-start(bf16[352,128]{1,0:T(8,128)(2,1)S(1)} %constant_dynamic-update-slice_fusion.refs_0_), channel_id=1, source_target_pairs={{0,1},{1,0},{2,3},{3,2},{4,5},{5,4},{6,7},{7,6},{8,9},{9,8},{10,11... | collective-permute-start | bytes 270344 | tf_op jit(solution)/shard_map/ppermute | solution.py:122
  21.6 1.3 %collective-permute-start.7 = (bf16[352,128]{1,0:T(8,128)(2,1)S(1)}, bf16[352,128]{1,0:T(8,128)(2,1)S(1)}, u32[]{:S(2)}, u32[]{:S(2)}) collective-permute-start(bf16[352,128]{1,0:T(8,128)(2,1)S(1)} %collective-permute-done.3.refs_1_), channel_id=1, source_target_pairs={{0,1},{1,0},{2,3},{3,2},{4,5},{5,4},{6,7},{7,6},{8,9},{9,8},{10,11... | collective-permute-start | bytes 270344 | tf_op jit(solution)/shard_map/ppermute | solution.py:122
  21.7 16.3 %collective-permute-start.12 = (bf16[4,16,1024]{2,1,0:T(8,128)(2,1)S(1)}, bf16[4,16,1024]{2,1,0:T(8,128)(2,1)S(1)}, u32[]{:S(2)}, u32[]{:S(2)}) collective-permute-start(bf16[4,16,1024]{2,1,0:T(8,128)(2,1)S(1)} %bitcast.11), channel_id=1, source_target_pairs={{0,1},{1,0},{2,3},{3,2},{4,5},{5,4},{6,7},{7,6},{8,9},{9,8},{10,11... | collective-permute-start | bytes 393224 | tf_op jit(solution)/shard_map/ppermute | solution.py:122
  22.5 1.3 %collective-permute-start.8 = (bf16[352,128]{1,0:T(8,128)(2,1)S(1)}, bf16[352,128]{1,0:T(8,128)(2,1)S(1)}, u32[]{:S(2)}, u32[]{:S(2)}) collective-permute-start(bf16[352,128]{1,0:T(8,128)(2,1)S(1)} %collective-permute-done.4.refs_2_), channel_id=1, source_target_pairs={{0,1},{1,0},{2,3},{3,2},{4,5},{5,4},{6,7},{7,6},{8,9},{9,8},{10,11... | collective-permute-start | bytes 270344 | tf_op jit(solution)/shard_map/ppermute | solution.py:122
  22.9 1.3 %collective-permute-start.9 = (bf16[352,128]{1,0:T(8,128)(2,1)S(1)}, bf16[352,128]{1,0:T(8,128)(2,1)S(1)}, u32[]{:S(2)}, u32[]{:S(2)}) collective-permute-start(bf16[352,128]{1,0:T(8,128)(2,1)S(1)} %collective-permute-done.5.refs_3_), channel_id=1, source_target_pairs={{0,1},{1,0},{2,3},{3,2},{4,5},{5,4},{6,7},{7,6},{8,9},{9,8},{10,11... | collective-permute-start | bytes 270344 | tf_op jit(solution)/shard_map/ppermute | solution.py:122
  65.1 12.4 %collective-permute-start.14 = (bf16[4,128,128]{2,1,0:T(8,128)(2,1)S(1)}, bf16[4,128,128]{2,1,0:T(8,128)(2,1)S(1)}, u32[]{:S(2)}, u32[]{:S(2)}) collective-permute-start(bf16[4,128,128]{2,1,0:T(8,128)(2,1)S(1)} %get-tuple-element.128), channel_id=1, source_target_pairs={{1,2},{3,4},{5,6},{7,8},{9,10},{11,12},{13,14},{15,16},{17,18},{19... | collective-permute-start | bytes 393224 | tf_op jit(solution)/shard_map/ppermute | solution.py:1089
  65.8 11.7 %collective-permute-start.13 = (bf16[4,128,128]{2,1,0:T(8,128)(2,1)S(1)}, bf16[4,128,128]{2,1,0:T(8,128)(2,1)S(1)}, u32[]{:S(2)}, u32[]{:S(2)}) collective-permute-start(bf16[4,128,128]{2,1,0:T(8,128)(2,1)S(1)} %get-tuple-element.129), channel_id=1, source_target_pairs={{0,1},{1,0},{2,3},{3,2},{4,5},{5,4},{6,7},{7,6},{8,9},{9,8},{10,11... | collective-permute-start | bytes 393224 | tf_op jit(solution)/shard_map/ppermute | solution.py:122
  89.0 17.1 %copy-start.4 = (f32[11,1024]{1,0:T(8,128)S(1)}, f32[11,1024]{1,0:T(8,128)}, u32[]{:S(2)}) copy-start(f32[11,1024]{1,0:T(8,128)} %refs_4_.1) | copy-start | bytes 135172
  89.0 17.1 %copy-start.6 = (f32[11,1024]{1,0:T(8,128)S(1)}, f32[11,1024]{1,0:T(8,128)}, u32[]{:S(2)}) copy-start(f32[11,1024]{1,0:T(8,128)} %refs_5_.1) | copy-start | bytes 135172
  89.0 17.0 %copy-start.7 = (f32[11,1024]{1,0:T(8,128)S(1)}, f32[11,1024]{1,0:T(8,128)}, u32[]{:S(2)}) copy-start(f32[11,1024]{1,0:T(8,128)} %refs_6_.1) | copy-start | bytes 135172
  90.3 1.7 %collective-permute-start.16 = (bf16[1408,128]{1,0:T(8,128)(2,1)S(1)}, bf16[1408,128]{1,0:T(8,128)(2,1)S(1)}, u32[]{:S(2)}, u32[]{:S(2)}) collective-permute-start(bf16[1408,128]{1,0:T(8,128)(2,1)S(1)} %get-tuple-element.104), channel_id=1, source_target_pairs={{0,1},{1,0},{2,3},{3,2},{4,5},{5,4},{6,7},{7,6},{8,9},{9,8},{10,11... | collective-permute-start | bytes 1081352 | tf_op jit(solution)/shard_map/ppermute | solution.py:122
  90.4 5.3 %collective-permute-start.15 = (bf16[4,16,512]{2,1,0:T(8,128)(2,1)S(1)}, bf16[4,16,512]{2,1,0:T(8,128)(2,1)S(1)}, u32[]{:S(2)}, u32[]{:S(2)}) collective-permute-start(bf16[4,16,512]{2,1,0:T(8,128)(2,1)S(1)} %get-tuple-element.95), channel_id=1, source_target_pairs={{0,1},{1,0},{2,3},{3,2},{4,5},{5,4},{6,7},{7,6},{8,9},{9,8},{10,11... | collective-permute-start | bytes 196616 | tf_op jit(solution)/shard_map/ppermute | solution.py:122
  92.1 5.3 %collective-permute-start.17 = (bf16[352,128]{1,0:T(8,128)(2,1)S(1)}, bf16[352,128]{1,0:T(8,128)(2,1)S(1)}, u32[]{:S(2)}, u32[]{:S(2)}) collective-permute-start(bf16[352,128]{1,0:T(8,128)(2,1)S(1)} %get-tuple-element.106), channel_id=1, source_target_pairs={{0,2},{1,3},{2,0},{3,1},{4,6},{5,7},{6,4},{7,5},{8,10},{9,11},{10,... | collective-permute-start | bytes 270344 | tf_op jit(solution)/shard_map/ppermute | solution.py:122
  92.7 6.5 %collective-permute-start.18 = (bf16[352,128]{1,0:T(8,128)(2,1)S(1)}, bf16[352,128]{1,0:T(8,128)(2,1)S(1)}, u32[]{:S(2)}, u32[]{:S(2)}) collective-permute-start(bf16[352,128]{1,0:T(8,128)(2,1)S(1)} %get-tuple-element.107), channel_id=1, source_target_pairs={{0,4},{1,5},{2,6},{3,7},{4,0},{5,1},{6,2},{7,3},{8,12},{9,13},{10,... | collective-permute-start | bytes 270344 | tf_op jit(solution)/shard_map/ppermute | solution.py:122
  93.4 5.8 %collective-permute-start.19 = (bf16[352,128]{1,0:T(8,128)(2,1)S(1)}, bf16[352,128]{1,0:T(8,128)(2,1)S(1)}, u32[]{:S(2)}, u32[]{:S(2)}) collective-permute-start(bf16[352,128]{1,0:T(8,128)(2,1)S(1)} %get-tuple-element.108), channel_id=1, source_target_pairs={{0,6},{1,7},{2,4},{3,5},{4,2},{5,3},{6,0},{7,1},{8,14},{9,15},{10,... | collective-permute-start | bytes 270344 | tf_op jit(solution)/shard_map/ppermute | solution.py:122
  99.3 5.1 %collective-permute-start.20 = (bf16[88,128]{1,0:T(8,128)(2,1)S(1)}, bf16[88,128]{1,0:T(8,128)(2,1)S(1)}, u32[]{:S(2)}, u32[]{:S(2)}) collective-permute-start(bf16[88,128]{1,0:T(8,128)(2,1)S(1)} %get-tuple-element.110), channel_id=1, source_target_pairs={{0,8},{1,9},{2,10},{3,11},{4,12},{5,13},{6,14},{7,15},{8,0},{9,1},... | collective-permute-start | bytes 67592 | tf_op jit(solution)/shard_map/ppermute | solution.py:122
  99.9 4.7 %collective-permute-start.21 = (bf16[88,128]{1,0:T(8,128)(2,1)S(1)}, bf16[88,128]{1,0:T(8,128)(2,1)S(1)}, u32[]{:S(2)}, u32[]{:S(2)}) collective-permute-start(bf16[88,128]{1,0:T(8,128)(2,1)S(1)} %get-tuple-element.111), channel_id=1, source_target_pairs={{0,16},{1,17},{2,18},{3,19},{4,20},{5,21},{6,22},{7,23},{8,24},{9,... | collective-permute-start | bytes 67592 | tf_op jit(solution)/shard_map/ppermute | solution.py:122
  100.4 5.6 %collective-permute-start.22 = (bf16[88,128]{1,0:T(8,128)(2,1)S(1)}, bf16[88,128]{1,0:T(8,128)(2,1)S(1)}, u32[]{:S(2)}, u32[]{:S(2)}) collective-permute-start(bf16[88,128]{1,0:T(8,128)(2,1)S(1)} %get-tuple-element.112), channel_id=1, source_target_pairs={{0,24},{1,25},{2,26},{3,27},{4,28},{5,29},{6,30},{7,31},{8,16},{9,... | collective-permute-start | bytes 67592 | tf_op jit(solution)/shard_map/ppermute | solution.py:122

commit v5 on v4

--- a/solution.py
+++ b/solution.py
@@ -129,8 +129,8 @@
             parts, early, rows = lax.optimization_barrier((parts, early, rows))
         z = parts[0] if len(parts) == 1 else jnp.concatenate(parts, axis=0)
         parts = [z] + [swap(z, spread(bits, q), n_dev) for q in range(1, 1 << len(bits))]
-    parts, late = lax.optimization_barrier((parts, sides(*rows)))
-    return parts + [swap(z, 1, n_dev) for z in parts], early, late
+    got, late = lax.optimization_barrier(([swap(z, 1, n_dev) for z in parts], sides(*rows)))
+    return parts + got, early, late
 
 
 def relative_block(owner, me, n_dev):

time: 108 us -> 107 us (level)
  blocking collectives: 30 us -> 28.9 us
    all_to_all x3, blocking collectives: 30 us -> 28.9 us  [share_sums(): return lax.all_to_all(rows, AXES, 0, 0, tiled=True)]
  transfers between devices with their start and end apart: 23 -> 23, of which waited for: 12 -> 11; matrix products, arithmetic and copies ran while one was open for 4% -> 4% of each run, Pallas kernels for 2% -> 2%
where the time goes in v5:
time: 107 us
  Pallas kernels  34.9 us (33%)
  blocking collectives  28.9 us (27%)
  starting transfers between devices  25 us (23%)
  waiting for transfers between devices  11.9 us (11%)
  local copies, waits for them, and re-layouts  3.06 us (3%)
  other arithmetic  2.35 us (2%)
    all_to_all x3, blocking collectives, share_sums(): return lax.all_to_all(rows, AXES, 0, 0, tiled=True)  28.9 us
    ppermute x21, starting transfers between devices, swap(): return lax.ppermute(value, AXES, [(i, i ^ mask) for i in range(n_dev)])  23.6 us
    pallas_call x1, Pallas kernels, head(): pl.pallas_call(head_kernel, in_specs=[smem(), smem()] + [vmem()] * 11, ou...  12.3 us
    ppermute x21, waiting for transfers between devices, swap(): return lax.ppermute(value, AXES, [(i, i ^ mask) for i in range(n_dev)])  11.9 us
    pallas_call x1, Pallas kernels, input_grad(): pl.pallas_call(input_kernel, out_shape=(jax.ShapeDtypeStruct(feats.shape,...  11.5 us
    pallas_call x1, Pallas kernels, depth(): pl.pallas_call(depth_kernel, out_shape=(jax.ShapeDtypeStruct((micro, fram...  5.91 us
    pallas_call x1, Pallas kernels, unpack(): pl.pallas_call(functools.partial(unpack_kernel, len(parts)), out_shape=ou...  2.39 us
  transfers between devices with their start and end apart: 23, of which 11 were waited for; matrix products, arithmetic and copies ran while one was open for 4% of the time, Pallas kernels for 2%

profile of v5, /device:TPU:0, one launch (start us, length us, event | category | flops | bytes accessed | tf_op | source)
XLA Modules:
  0.0 106.9 jit_solution(3555804360165885676)
XLA Ops:
  0.7 0.9 copy-done.3
  1.6 5.1 %collective-permute-start.2 = (bf16[88,128]{1,0:T(8,128)(2,1)S(1)}, bf16[88,128]{1,0:T(8,128)(2,1)S(1)}, u32[]{:S(2)}, u32[]{:S(2)}) collective-permute-start(bf16[88,128]{1,0:T(8,128)(2,1)S(1)} %to_tiles.1), channel_id=1, source_target_pairs={{0,24},{1,25},{2,26},{3,27},{4,28},{5,29},{6,30},{7,31},{8,16},{9,... | collective-permute-start | bytes 67592 | tf_op jit(solution)/shard_map/ppermute | solution.py:122
  7.3 0.7 reduce
  8.2 0.7 convert_reduce_fusion.1
  9.0 2.4 %collective-permute-done.1 = bf16[88,128]{1,0:T(8,128)(2,1)S(1)} collective-permute-done((bf16[88,128]{1,0:T(8,128)(2,1)S(1)}, bf16[88,128]{1,0:T(8,128)(2,1)S(1)}, u32[]{:S(2)}, u32[]{:S(2)}) %collective-permute-start.1) | collective-permute-done | bytes 22560 | tf_op jit(solution)/shard_map/ppermute | solution.py:122
  11.5 2.5 %collective-permute-start.5 = (bf16[352,128]{1,0:T(8,128)(2,1)S(1)}, bf16[352,128]{1,0:T(8,128)(2,1)S(1)}, u32[]{:S(2)}, u32[]{:S(2)}) collective-permute-start(bf16[352,128]{1,0:T(8,128)(2,1)S(1)} %constant_dynamic-update-slice_fusion.refs_0_), channel_id=1, source_target_pairs={{0,6},{1,7},{2,4},{3,5},{4,2},{5,3},{6,0},{7,1},{8,14},{9,15},{10,... | collective-permute-start | bytes 270344 | tf_op jit(solution)/shard_map/ppermute | solution.py:122
  15.1 1.1 constant_dynamic-slice_fusion.3
  16.1 1.0 constant_dynamic-slice_fusion.2
  17.5 1.9 %collective-permute-done.4.refs_2_ = bf16[352,128]{1,0:T(8,128)(2,1)S(1)} collective-permute-done((bf16[352,128]{1,0:T(8,128)(2,1)S(1)}, bf16[352,128]{1,0:T(8,128)(2,1)S(1)}, u32[]{:S(2)}, u32[]{:S(2)}) %collective-permute-start.4) | collective-permute-done | bytes 90144 | tf_op jit(solution)/shard_map/ppermute | solution.py:122
  20.0 0.7 collective-permute-done.8.refs_6_
  21.2 0.7 collective-permute-start.11
  21.9 2.9 %collective-permute-start.12 = (bf16[4,16,1024]{2,1,0:T(8,128)(2,1)S(1)}, bf16[4,16,1024]{2,1,0:T(8,128)(2,1)S(1)}, u32[]{:S(2)}, u32[]{:S(2)}) collective-permute-start(bf16[4,16,1024]{2,1,0:T(8,128)(2,1)S(1)} %bitcast.11), channel_id=1, source_target_pairs={{0,1},{1,0},{2,3},{3,2},{4,5},{5,4},{6,7},{7,6},{8,9},{9,8},{10,11... | collective-permute-start | bytes 393224 | tf_op jit(solution)/shard_map/ppermute | solution.py:122
  24.8 2.4 %unpack.1 = (bf16[128,512]{1,0:T(8,128)(2,1)S(1)}, bf16[512,256]{1,0:T(8,128)(2,1)S(1)}, bf16[128,1024]{1,0:T(8,128)(2,1)S(1)}, bf16[16,1024]{1,0:T(8,128)(2,1)S...) custom-call(s32[340]{0:T(512)S(1)} %get-tuple-element.62.pos_ref, bf16[4,512,128]{2,1,0:T(8,128)(2,1)S(1)} %copy-done, ...), custom_call_target="tpu_custom_call" | custom-call | tf_op jit(solution)/shard_map/unpack/pallas_call | solution.py:229
  27.2 10.3 %all_to_all.15.stats_ref.stats1_ref = f32[32,1,128]{2,1,0:T(1,128)S(1)} all-to-all(f32[32,1,128]{2,1,0:T(1,128)S(1)} %get-tuple-element.74), channel_id=1, replica_groups=mesh['tm'=16,'src'=2] {'tm','src'}, dimensions={0} | all-to-all | bytes 32768 | tf_op jit(solution)/shard_map/all_to_all | solution.py:148
  37.5 5.9 %depth.1 = (f32[4,512,512]{2,1,0:T(8,128)S(1)}, f32[4,256,512]{2,1,0:T(8,128)S(1)}, f32[32,1,128]{2,1,0:T(1,128)S(1)}) custom-call(s32[1]{0:T(128)} %bitcast.me_ref, s32[4,8]{1,0:T(4,128)S(1)} %copy-done.8, f32[32,1,128]{2,1,0:T(1,128)S(1)} %all_to_all.15.stats_ref.stats1_ref, bf16[4,512,128]{2,1,0:T(8,128)(2,1)S(1)} %copy-done, ...), custom_call_target="tpu_custom_call" | custom-call | tf_op jit(solution)/shard_map/depth/pallas_call | solution.py:402
  43.4 8.8 %all_to_all.16.stats_ref.stats2_ref = f32[32,1,128]{2,1,0:T(1,128)S(1)} all-to-all(f32[32,1,128]{2,1,0:T(1,128)S(1)} %get-tuple-element.83), channel_id=1, replica_groups=mesh['tm'=16,'src'=2] {'tm','src'}, dimensions={0} | all-to-all | bytes 32768 | tf_op jit(solution)/shard_map/all_to_all | solution.py:148
  52.2 12.3 %head.1 = (bf16[4,512,128]{2,1,0:T(8,128)(2,1)}, bf16[4,16,512]{2,1,0:T(8,128)(2,1)S(1)}, bf16[4,16,512]{2,1,0:T(8,128)(2,1)S(1)}, bf16[4,512,128]{2,1,0:T(8,128...) custom-call(s32[1]{0:T(128)} %bitcast.me_ref, ...), custom_call_target="tpu_custom_call" | custom-call | tf_op jit(solution)/shard_map/head/pallas_call | solution.py:680
  64.6 0.7 collective-permute-start.14
  65.3 2.0 %collective-permute-start.13 = (bf16[4,128,128]{2,1,0:T(8,128)(2,1)S(1)}, bf16[4,128,128]{2,1,0:T(8,128)(2,1)S(1)}, u32[]{:S(2)}, u32[]{:S(2)}) collective-permute-start(bf16[4,128,128]{2,1,0:T(8,128)(2,1)S(1)} %get-tuple-element.129), channel_id=1, source_target_pairs={{0,1},{1,0},{2,3},{3,2},{4,5},{5,4},{6,7},{7,6},{8,9},{9,8},{10,11... | collective-permute-start | bytes 393224 | tf_op jit(solution)/shard_map/ppermute | solution.py:122
  67.2 9.7 %all_to_all.17.stats3_ref = f32[32,1,128]{2,1,0:T(1,128)S(1)} all-to-all(f32[32,1,128]{2,1,0:T(1,128)S(1)} %get-tuple-element.90), channel_id=1, replica_groups=mesh['tm'=16,'src'=2] {'tm','src'}, dimensions={0} | all-to-all | bytes 32768 | tf_op jit(solution)/shard_map/all_to_all | solution.py:148
  77.0 11.5 %input_grad.1 = (bf16[4,512,128]{2,1,0:T(8,128)(2,1)}, f32[128,512]{1,0:T(8,128)S(1)}, f32[8,512]{1,0:T(8,128)S(1)}) custom-call(s32[1]{0:T(128)} %bitcast.me_ref, s32[4,8]{1,0:T(4,128)S(1)} %copy-done.8, f32[32,1,128]{2,1,0:T(1,128)S(1)} %all_to_all.15.stats_ref.stats1_ref, f32[32,1,128]{2,1,0:T(1,128)S(1)} %all_to_all.16.stats_ref.stats2_ref, ...), custom_call_target="tpu_custom_call" | custom-call | tf_op jit(solution)/shard_map/input_grad/pallas_call | solution.py:904
  88.5 1.3 %pack.1 = (f32[1408,128]{1,0:T(8,128)S(1)}, bf16[1408,128]{1,0:T(8,128)(2,1)S(1)}) custom-call(s32[340]{0:T(512)S(1)} %get-tuple-element.62.pos_ref, f32[128,512]{1,0:T(8,128)S(1)} %get-tuple-element.97.g_in, f32[256,512]{1,0:T(8,128)S(1)} %get-tuple-element.98.g_rs, f32[128,1024]{1,0:T(8,128)S(1)} %get-tuple-element.99.g_mask, ...), custom_call_target="tpu_custom_call" | custom-call | tf_op jit(solution)/shard_map/pack/pallas_call | solution.py:959
  90.4 1.2 %collective-permute-done.16.refs_1_ = bf16[1408,128]{1,0:T(8,128)(2,1)S(1)} collective-permute-done((bf16[1408,128]{1,0:T(8,128)(2,1)S(1)}, bf16[1408,128]{1,0:T(8,128)(2,1)S(1)}, u32[]{:S(2)}, u32[]{:S(2)}) %collective-permute-start.16) | collective-permute-done | bytes 360480 | tf_op jit(solution)/shard_map/ppermute | solution.py:122
  92.2 0.6 collective-permute-start.18
  92.8 2.3 %collective-permute-start.19 = (bf16[352,128]{1,0:T(8,128)(2,1)S(1)}, bf16[352,128]{1,0:T(8,128)(2,1)S(1)}, u32[]{:S(2)}, u32[]{:S(2)}) collective-permute-start(bf16[352,128]{1,0:T(8,128)(2,1)S(1)} %get-tuple-element.108), channel_id=1, source_target_pairs={{0,6},{1,7},{2,4},{3,5},{4,2},{5,3},{6,0},{7,1},{8,14},{9,15},{10,... | collective-permute-start | bytes 270344 | tf_op jit(solution)/shard_map/ppermute | solution.py:122
  95.2 1.7 %collective-permute-done.17.refs_1_ = bf16[352,128]{1,0:T(8,128)(2,1)S(1)} collective-permute-done((bf16[352,128]{1,0:T(8,128)(2,1)S(1)}, bf16[352,128]{1,0:T(8,128)(2,1)S(1)}, u32[]{:S(2)}, u32[]{:S(2)}) %collective-permute-start.17) | collective-permute-done | bytes 90144 | tf_op jit(solution)/shard_map/ppermute | solution.py:122
  96.9 1.8 %collective-permute-done.18.refs_2_ = bf16[352,128]{1,0:T(8,128)(2,1)S(1)} collective-permute-done((bf16[352,128]{1,0:T(8,128)(2,1)S(1)}, bf16[352,128]{1,0:T(8,128)(2,1)S(1)}, u32[]{:S(2)}, u32[]{:S(2)}) %collective-permute-start.18) | collective-permute-done | bytes 90144 | tf_op jit(solution)/shard_map/ppermute | solution.py:122
  98.7 0.6 collective-permute-start.20
  99.9 3.3 %collective-permute-start.22 = (bf16[88,128]{1,0:T(8,128)(2,1)S(1)}, bf16[88,128]{1,0:T(8,128)(2,1)S(1)}, u32[]{:S(2)}, u32[]{:S(2)}) collective-permute-start(bf16[88,128]{1,0:T(8,128)(2,1)S(1)} %get-tuple-element.112), channel_id=1, source_target_pairs={{0,24},{1,25},{2,26},{3,27},{4,28},{5,29},{6,30},{7,31},{8,16},{9,... | collective-permute-start | bytes 67592 | tf_op jit(solution)/shard_map/ppermute | solution.py:122
  103.2 0.7 maximum_bitcast_fusion
  104.1 1.4 %collective-permute-done.22.refs_3_ = bf16[88,128]{1,0:T(8,128)(2,1)S(1)} collective-permute-done((bf16[88,128]{1,0:T(8,128)(2,1)S(1)}, bf16[88,128]{1,0:T(8,128)(2,1)S(1)}, u32[]{:S(2)}, u32[]{:S(2)}) %collective-permute-start.22) | collective-permute-done | bytes 22560 | tf_op jit(solution)/shard_map/ppermute | solution.py:122
  105.5 1.4 %adam.1 = (f32[11,1024]{1,0:T(8,128)}, f32[11,1024]{1,0:T(8,128)}, f32[11,1024]{1,0:T(8,128)}) custom-call(s32[1]{0:T(128)} %bitcast.1.count_ref, f32[88,128]{1,0:T(8,128)S(1)} %get-tuple-element.109.refs_0_, bf16[88,128]{1,0:T(8,128)(2,1)S(1)} %collective-permute-done.20.refs_1_, bf16[88,128]{1,0:T(8,128)(2,1)S(1)} %collective-permute-done.21.refs_2_, ...), custom_call_target="tpu_custom_call" | custom-call | tf_op jit(solution)/shard_map/adam/pallas_call | solution.py:1030
  (57 shorter events, 5.7 us)
Async XLA Ops:
  0.6 24.1 %copy-start = (bf16[4,512,128]{2,1,0:T(8,128)(2,1)S(1)}, bf16[4,512,128]{2,1,0:T(8,128)(2,1)}, u32[]{:S(2)}) copy-start(bf16[4,512,128]{2,1,0:T(8,128)(2,1)} %x_ref.7) | copy-start | bytes 1572868
  0.6 0.9 copy-start.3
  1.5 20.3 %copy-start.5 = (bf16[4,1,1024,16]{2,3,1,0:T(8,128)(2,1)S(1)}, bf16[4,1,1024,16]{2,3,1,0:T(8,128)(2,1)}, u32[]{:S(2)}) copy-start(bf16[4,1,1024,16]{2,3,1,0:T(8,128)(2,1)} %param.17) | copy-start | bytes 393220
  1.6 7.4 %collective-permute-start.2 = (bf16[88,128]{1,0:T(8,128)(2,1)S(1)}, bf16[88,128]{1,0:T(8,128)(2,1)S(1)}, u32[]{:S(2)}, u32[]{:S(2)}) collective-permute-start(bf16[88,128]{1,0:T(8,128)(2,1)S(1)} %to_tiles.1), channel_id=1, source_target_pairs={{0,24},{1,25},{2,26},{3,27},{4,28},{5,29},{6,30},{7,31},{8,16},{9,... | collective-permute-start | bytes 67592 | tf_op jit(solution)/shard_map/ppermute | solution.py:122
  6.7 4.7 %collective-permute-start.1 = (bf16[88,128]{1,0:T(8,128)(2,1)S(1)}, bf16[88,128]{1,0:T(8,128)(2,1)S(1)}, u32[]{:S(2)}, u32[]{:S(2)}) collective-permute-start(bf16[88,128]{1,0:T(8,128)(2,1)S(1)} %to_tiles.1), channel_id=1, source_target_pairs={{0,16},{1,17},{2,18},{3,19},{4,20},{5,21},{6,22},{7,23},{8,24},{9,... | collective-permute-start | bytes 67592 | tf_op jit(solution)/shard_map/ppermute | solution.py:122
  6.7 4.7 %collective-permute-start = (bf16[88,128]{1,0:T(8,128)(2,1)S(1)}, bf16[88,128]{1,0:T(8,128)(2,1)S(1)}, u32[]{:S(2)}, u32[]{:S(2)}) collective-permute-start(bf16[88,128]{1,0:T(8,128)(2,1)S(1)} %to_tiles.1), channel_id=1, source_target_pairs={{0,8},{1,9},{2,10},{3,11},{4,12},{5,13},{6,14},{7,15},{8,0},{9,1},... | collective-permute-start | bytes 67592 | tf_op jit(solution)/shard_map/ppermute | solution.py:122
  11.4 26.0 %copy-start.8 = (s32[4,8]{1,0:T(4,128)S(1)}, s32[4,8]{1,0:T(4,128)}, u32[]{:S(2)}) copy-start(s32[4,8]{1,0:T(4,128)} %seg_ref.5) | copy-start | bytes 388
  11.4 8.5 %collective-permute-start.6 = (bf16[352,128]{1,0:T(8,128)(2,1)S(1)}, bf16[352,128]{1,0:T(8,128)(2,1)S(1)}, u32[]{:S(2)}, u32[]{:S(2)}) collective-permute-start(bf16[352,128]{1,0:T(8,128)(2,1)S(1)} %constant_dynamic-update-slice_fusion.refs_0_), channel_id=1, source_target_pairs={{0,1},{1,0},{2,3},{3,2},{4,5},{5,4},{6,7},{7,6},{8,9},{9,8},{10,11... | collective-permute-start | bytes 270344 | tf_op jit(solution)/shard_map/ppermute | solution.py:122
  11.5 6.0 %collective-permute-start.5 = (bf16[352,128]{1,0:T(8,128)(2,1)S(1)}, bf16[352,128]{1,0:T(8,128)(2,1)S(1)}, u32[]{:S(2)}, u32[]{:S(2)}) collective-permute-start(bf16[352,128]{1,0:T(8,128)(2,1)S(1)} %constant_dynamic-update-slice_fusion.refs_0_), channel_id=1, source_target_pairs={{0,6},{1,7},{2,4},{3,5},{4,2},{5,3},{6,0},{7,1},{8,14},{9,15},{10,... | collective-permute-start | bytes 270344 | tf_op jit(solution)/shard_map/ppermute | solution.py:122
  14.0 5.4 %collective-permute-start.4 = (bf16[352,128]{1,0:T(8,128)(2,1)S(1)}, bf16[352,128]{1,0:T(8,128)(2,1)S(1)}, u32[]{:S(2)}, u32[]{:S(2)}) collective-permute-start(bf16[352,128]{1,0:T(8,128)(2,1)S(1)} %constant_dynamic-update-slice_fusion.refs_0_), channel_id=1, source_target_pairs={{0,4},{1,5},{2,6},{3,7},{4,0},{5,1},{6,2},{7,3},{8,12},{9,13},{10,... | collective-permute-start | bytes 270344 | tf_op jit(solution)/shard_map/ppermute | solution.py:122
  14.5 4.9 %collective-permute-start.3 = (bf16[352,128]{1,0:T(8,128)(2,1)S(1)}, bf16[352,128]{1,0:T(8,128)(2,1)S(1)}, u32[]{:S(2)}, u32[]{:S(2)}) collective-permute-start(bf16[352,128]{1,0:T(8,128)(2,1)S(1)} %constant_dynamic-update-slice_fusion.refs_0_), channel_id=1, source_target_pairs={{0,2},{1,3},{2,0},{3,1},{4,6},{5,7},{6,4},{7,5},{8,10},{9,11},{10,... | collective-permute-start | bytes 270344 | tf_op jit(solution)/shard_map/ppermute | solution.py:122
  17.5 2.4 %collective-permute-start.9 = (bf16[352,128]{1,0:T(8,128)(2,1)S(1)}, bf16[352,128]{1,0:T(8,128)(2,1)S(1)}, u32[]{:S(2)}, u32[]{:S(2)}) collective-permute-start(bf16[352,128]{1,0:T(8,128)(2,1)S(1)} %collective-permute-done.5.refs_3_), channel_id=1, source_target_pairs={{0,1},{1,0},{2,3},{3,2},{4,5},{5,4},{6,7},{7,6},{8,9},{9,8},{10,11... | collective-permute-start | bytes 270344 | tf_op jit(solution)/shard_map/ppermute | solution.py:122
  19.4 1.3 %collective-permute-start.8 = (bf16[352,128]{1,0:T(8,128)(2,1)S(1)}, bf16[352,128]{1,0:T(8,128)(2,1)S(1)}, u32[]{:S(2)}, u32[]{:S(2)}) collective-permute-start(bf16[352,128]{1,0:T(8,128)(2,1)S(1)} %collective-permute-done.4.refs_2_), channel_id=1, source_target_pairs={{0,1},{1,0},{2,3},{3,2},{4,5},{5,4},{6,7},{7,6},{8,9},{9,8},{10,11... | collective-permute-start | bytes 270344 | tf_op jit(solution)/shard_map/ppermute | solution.py:122
  19.4 1.4 %collective-permute-start.7 = (bf16[352,128]{1,0:T(8,128)(2,1)S(1)}, bf16[352,128]{1,0:T(8,128)(2,1)S(1)}, u32[]{:S(2)}, u32[]{:S(2)}) collective-permute-start(bf16[352,128]{1,0:T(8,128)(2,1)S(1)} %collective-permute-done.3.refs_1_), channel_id=1, source_target_pairs={{0,1},{1,0},{2,3},{3,2},{4,5},{5,4},{6,7},{7,6},{8,9},{9,8},{10,11... | collective-permute-start | bytes 270344 | tf_op jit(solution)/shard_map/ppermute | solution.py:122
  19.9 32.3 %copy-start.1 = (bf16[4,512,128]{2,1,0:T(8,128)(2,1)S(1)}, bf16[4,512,128]{2,1,0:T(8,128)(2,1)}, u32[]{:S(2)}) copy-start(bf16[4,512,128]{2,1,0:T(8,128)(2,1)} %dy_ref.3) | copy-start | bytes 1572868
  19.9 32.3 %copy-start.2 = (bf16[4,512,512]{2,1,0:T(8,128)(2,1)S(1)}, bf16[4,512,512]{2,1,0:T(8,128)(2,1)}, u32[]{:S(2)}) copy-start(bf16[4,512,512]{2,1,0:T(8,128)(2,1)} %enc_ref.1) | copy-start | bytes 6291460
  20.8 16.6 %collective-permute-start.10 = (bf16[4,384,128]{2,1,0:T(8,128)(2,1)S(1)}, bf16[4,384,128]{2,1,0:T(8,128)(2,1)S(1)}, u32[]{:S(2)}, u32[]{:S(2)}) collective-permute-start(bf16[4,384,128]{2,1,0:T(8,128)(2,1)S(1)} %get-tuple-element.75), channel_id=1, source_target_pairs={{0,1},{1,0},{2,3},{3,2},{4,5},{5,4},{6,7},{7,6},{8,9},{9,8},{10,11... | collective-permute-start | bytes 1179656 | tf_op jit(solution)/shard_map/ppermute | solution.py:122
  21.2 16.3 %collective-permute-start.11 = (bf16[4,384,128]{2,1,0:T(8,128)(2,1)S(1)}, bf16[4,384,128]{2,1,0:T(8,128)(2,1)S(1)}, u32[]{:S(2)}, u32[]{:S(2)}) collective-permute-start(bf16[4,384,128]{2,1,0:T(8,128)(2,1)S(1)} %get-tuple-element.76), channel_id=1, source_target_pairs={{1,2},{3,4},{5,6},{7,8},{9,10},{11,12},{13,14},{15,16},{17,18},{19... | collective-permute-start | bytes 1179656 | tf_op jit(solution)/shard_map/ppermute | solution.py:1076
  21.9 15.6 %collective-permute-start.12 = (bf16[4,16,1024]{2,1,0:T(8,128)(2,1)S(1)}, bf16[4,16,1024]{2,1,0:T(8,128)(2,1)S(1)}, u32[]{:S(2)}, u32[]{:S(2)}) collective-permute-start(bf16[4,16,1024]{2,1,0:T(8,128)(2,1)S(1)} %bitcast.11), channel_id=1, source_target_pairs={{0,1},{1,0},{2,3},{3,2},{4,5},{5,4},{6,7},{7,6},{8,9},{9,8},{10,11... | collective-permute-start | bytes 393224 | tf_op jit(solution)/shard_map/ppermute | solution.py:122
  64.6 12.4 %collective-permute-start.14 = (bf16[4,128,128]{2,1,0:T(8,128)(2,1)S(1)}, bf16[4,128,128]{2,1,0:T(8,128)(2,1)S(1)}, u32[]{:S(2)}, u32[]{:S(2)}) collective-permute-start(bf16[4,128,128]{2,1,0:T(8,128)(2,1)S(1)} %get-tuple-element.128), channel_id=1, source_target_pairs={{1,2},{3,4},{5,6},{7,8},{9,10},{11,12},{13,14},{15,16},{17,18},{19... | collective-permute-start | bytes 393224 | tf_op jit(solution)/shard_map/ppermute | solution.py:1089
  65.3 11.7 %collective-permute-start.13 = (bf16[4,128,128]{2,1,0:T(8,128)(2,1)S(1)}, bf16[4,128,128]{2,1,0:T(8,128)(2,1)S(1)}, u32[]{:S(2)}, u32[]{:S(2)}) collective-permute-start(bf16[4,128,128]{2,1,0:T(8,128)(2,1)S(1)} %get-tuple-element.129), channel_id=1, source_target_pairs={{0,1},{1,0},{2,3},{3,2},{4,5},{5,4},{6,7},{7,6},{8,9},{9,8},{10,11... | collective-permute-start | bytes 393224 | tf_op jit(solution)/shard_map/ppermute | solution.py:122
  88.4 17.1 %copy-start.4 = (f32[11,1024]{1,0:T(8,128)S(1)}, f32[11,1024]{1,0:T(8,128)}, u32[]{:S(2)}) copy-start(f32[11,1024]{1,0:T(8,128)} %refs_4_.1) | copy-start | bytes 135172
  88.4 17.1 %copy-start.6 = (f32[11,1024]{1,0:T(8,128)S(1)}, f32[11,1024]{1,0:T(8,128)}, u32[]{:S(2)}) copy-start(f32[11,1024]{1,0:T(8,128)} %refs_5_.1) | copy-start | bytes 135172
  88.5 17.0 %copy-start.7 = (f32[11,1024]{1,0:T(8,128)S(1)}, f32[11,1024]{1,0:T(8,128)}, u32[]{:S(2)}) copy-start(f32[11,1024]{1,0:T(8,128)} %refs_6_.1) | copy-start | bytes 135172
  89.8 1.7 %collective-permute-start.16 = (bf16[1408,128]{1,0:T(8,128)(2,1)S(1)}, bf16[1408,128]{1,0:T(8,128)(2,1)S(1)}, u32[]{:S(2)}, u32[]{:S(2)}) collective-permute-start(bf16[1408,128]{1,0:T(8,128)(2,1)S(1)} %get-tuple-element.104), channel_id=1, source_target_pairs={{0,1},{1,0},{2,3},{3,2},{4,5},{5,4},{6,7},{7,6},{8,9},{9,8},{10,11... | collective-permute-start | bytes 1081352 | tf_op jit(solution)/shard_map/ppermute | solution.py:122
  89.9 5.3 %collective-permute-start.15 = (bf16[4,16,512]{2,1,0:T(8,128)(2,1)S(1)}, bf16[4,16,512]{2,1,0:T(8,128)(2,1)S(1)}, u32[]{:S(2)}, u32[]{:S(2)}) collective-permute-start(bf16[4,16,512]{2,1,0:T(8,128)(2,1)S(1)} %get-tuple-element.95), channel_id=1, source_target_pairs={{0,1},{1,0},{2,3},{3,2},{4,5},{5,4},{6,7},{7,6},{8,9},{9,8},{10,11... | collective-permute-start | bytes 196616 | tf_op jit(solution)/shard_map/ppermute | solution.py:122
  91.6 5.3 %collective-permute-start.17 = (bf16[352,128]{1,0:T(8,128)(2,1)S(1)}, bf16[352,128]{1,0:T(8,128)(2,1)S(1)}, u32[]{:S(2)}, u32[]{:S(2)}) collective-permute-start(bf16[352,128]{1,0:T(8,128)(2,1)S(1)} %get-tuple-element.106), channel_id=1, source_target_pairs={{0,2},{1,3},{2,0},{3,1},{4,6},{5,7},{6,4},{7,5},{8,10},{9,11},{10,... | collective-permute-start | bytes 270344 | tf_op jit(solution)/shard_map/ppermute | solution.py:122
  92.2 6.5 %collective-permute-start.18 = (bf16[352,128]{1,0:T(8,128)(2,1)S(1)}, bf16[352,128]{1,0:T(8,128)(2,1)S(1)}, u32[]{:S(2)}, u32[]{:S(2)}) collective-permute-start(bf16[352,128]{1,0:T(8,128)(2,1)S(1)} %get-tuple-element.107), channel_id=1, source_target_pairs={{0,4},{1,5},{2,6},{3,7},{4,0},{5,1},{6,2},{7,3},{8,12},{9,13},{10,... | collective-permute-start | bytes 270344 | tf_op jit(solution)/shard_map/ppermute | solution.py:122
  92.8 5.8 %collective-permute-start.19 = (bf16[352,128]{1,0:T(8,128)(2,1)S(1)}, bf16[352,128]{1,0:T(8,128)(2,1)S(1)}, u32[]{:S(2)}, u32[]{:S(2)}) collective-permute-start(bf16[352,128]{1,0:T(8,128)(2,1)S(1)} %get-tuple-element.108), channel_id=1, source_target_pairs={{0,6},{1,7},{2,4},{3,5},{4,2},{5,3},{6,0},{7,1},{8,14},{9,15},{10,... | collective-permute-start | bytes 270344 | tf_op jit(solution)/shard_map/ppermute | solution.py:122
  98.7 5.1 %collective-permute-start.20 = (bf16[88,128]{1,0:T(8,128)(2,1)S(1)}, bf16[88,128]{1,0:T(8,128)(2,1)S(1)}, u32[]{:S(2)}, u32[]{:S(2)}) collective-permute-start(bf16[88,128]{1,0:T(8,128)(2,1)S(1)} %get-tuple-element.110), channel_id=1, source_target_pairs={{0,8},{1,9},{2,10},{3,11},{4,12},{5,13},{6,14},{7,15},{8,0},{9,1},... | collective-permute-start | bytes 67592 | tf_op jit(solution)/shard_map/ppermute | solution.py:122
  99.4 4.7 %collective-permute-start.21 = (bf16[88,128]{1,0:T(8,128)(2,1)S(1)}, bf16[88,128]{1,0:T(8,128)(2,1)S(1)}, u32[]{:S(2)}, u32[]{:S(2)}) collective-permute-start(bf16[88,128]{1,0:T(8,128)(2,1)S(1)} %get-tuple-element.111), channel_id=1, source_target_pairs={{0,16},{1,17},{2,18},{3,19},{4,20},{5,21},{6,22},{7,23},{8,24},{9,... | collective-permute-start | bytes 67592 | tf_op jit(solution)/shard_map/ppermute | solution.py:122
  99.9 5.6 %collective-permute-start.22 = (bf16[88,128]{1,0:T(8,128)(2,1)S(1)}, bf16[88,128]{1,0:T(8,128)(2,1)S(1)}, u32[]{:S(2)}, u32[]{:S(2)}) collective-permute-start(bf16[88,128]{1,0:T(8,128)(2,1)S(1)} %get-tuple-element.112), channel_id=1, source_target_pairs={{0,24},{1,25},{2,26},{3,27},{4,28},{5,29},{6,30},{7,31},{8,16},{9,... | collective-permute-start | bytes 67592 | tf_op jit(solution)/shard_map/ppermute | solution.py:122
